TPU v7x, 32 devices: a whole 2x2x4 slice. The times are simulated.
32 devices in a mesh: sec: 2 (over core), tile: 16 (over z, y, x).
Axes of the slice: x: 2, y: 2, z: 4, core: 2. Of those that a mesh axis runs over, the one named last changes fastest.
Arguments:
- object_field: bfloat16 [2, 2, 4096, 512], P(None, 'sec', 'tile'), may hold values from -1 to 1
- probe: bfloat16 [2, 256, 256], replicated, may hold values from -6 to 6
- phases: float32 [256], replicated, may hold values from -3.140625 to 3.140625
- intensities: bfloat16 [32, 256, 256], P('tile'), may hold values from 0.099609375 to 2
- pos_row: int32 [32], P('tile'), may hold values from 0 to 255
- pos_col: int32 [32], P('tile'), may hold values from 0 to 256
- counts: int32 [16], P('tile'), may hold values from 1 to 2, as said below
Outputs:
- object_gradient: float32 [2, 2, 4096, 512], P(None, 'sec', 'tile')
Inputs may be any that keep to these rules, and one draw needn't show every extreme that they name: `counts`: every strip has at least one live position, and some strip has exactly 2 in every draw.
All inputs are finite; a program needn't handle non-finite values.
Results may differ from a plain program's by a relative error of at most 0.025.
Values may be sent and summed in bfloat16 or wider, within the bound.
No kernel may reach another device: no remote copies, remote signals or barrier semaphores. Data moves between devices by JAX's collectives and lax.ppermute only.
A program may use at most 64 MiB of HBM per device.

v0:
```python
import math

import jax
import jax.numpy as jnp
from jax import lax
from jax.sharding import PartitionSpec as P


def shifted(value, axis, steps):
    count = lax.axis_size(axis)
    first, last = (max(0, -steps), min(count, count - steps))
    return lax.ppermute(value, axis, [(source, source + steps) for source in range(first, last)])


def build_tables(phases, wave_side):
    frequency = jnp.arange(wave_side, dtype=jnp.int32)
    product = frequency[:, None] * frequency[None, :] % wave_side
    angles = product.astype(jnp.float32) * (2.0 * math.pi / wave_side)
    cosine = jnp.cos(angles)
    sine_table = jnp.sin(angles)
    turned = phases[:, None] + angles
    turned_re = jnp.cos(turned)
    turned_im = jnp.sin(turned)
    highest = lax.Precision.HIGHEST
    kernel_re = (
        jnp.dot(turned_re.T, cosine, precision=highest, preferred_element_type=jnp.float32)
        + jnp.dot(turned_im.T, sine_table, precision=highest, preferred_element_type=jnp.float32)
    ) / wave_side
    kernel_im = (
        jnp.dot(turned_im.T, cosine, precision=highest, preferred_element_type=jnp.float32)
        - jnp.dot(turned_re.T, sine_table, precision=highest, preferred_element_type=jnp.float32)
    ) / wave_side
    norm_scale = 1.0 / math.sqrt(wave_side)
    far_re = cosine * norm_scale
    far_im = -sine_table * norm_scale
    return (
        kernel_re.astype(jnp.bfloat16),
        kernel_im.astype(jnp.bfloat16),
        far_re.astype(jnp.bfloat16),
        far_im.astype(jnp.bfloat16),
    )


def left_product(matrix, field):
    return jnp.einsum("mj,bjn->bmn", matrix, field, preferred_element_type=jnp.float32)


def right_product(field, matrix):
    return jnp.einsum("bmj,nj->bmn", field, matrix, preferred_element_type=jnp.float32)


def propagate(matrix_re, matrix_im, field_re, field_im):
    inner_re = (left_product(matrix_re, field_re) - left_product(matrix_im, field_im)).astype(
        jnp.bfloat16
    )
    inner_im = (left_product(matrix_re, field_im) + left_product(matrix_im, field_re)).astype(
        jnp.bfloat16
    )
    outer_re = (right_product(inner_re, matrix_re) - right_product(inner_im, matrix_im)).astype(
        jnp.bfloat16
    )
    outer_im = (right_product(inner_re, matrix_im) + right_product(inner_im, matrix_re)).astype(
        jnp.bfloat16
    )
    return (outer_re, outer_im)


def transmit(trans_re, trans_im, wave_re, wave_im):
    t_re = trans_re.astype(jnp.float32)
    t_im = trans_im.astype(jnp.float32)
    w_re = wave_re.astype(jnp.float32)
    w_im = wave_im.astype(jnp.float32)
    return (
        (t_re * w_re - t_im * w_im).astype(jnp.bfloat16),
        (t_re * w_im + t_im * w_re).astype(jnp.bfloat16),
    )


def conj_times(first_re, first_im, second_re, second_im):
    a_re = first_re.astype(jnp.float32)
    a_im = first_im.astype(jnp.float32)
    b_re = second_re.astype(jnp.float32)
    b_im = second_im.astype(jnp.float32)
    return (a_re * b_re + a_im * b_im, a_re * b_im - a_im * b_re)


def on_device(object_field, probe, phases, intensities, pos_row, pos_col, counts):
    slot_count = pos_row.shape[0]
    layer_count = object_field.shape[1]
    strip_rows = object_field.shape[2]
    wave_side = probe.shape[1]
    section = lax.axis_index("sec")
    sections = lax.axis_size("sec")
    first_section = section == 0
    last_section = section == sections - 1
    next_strip = shifted(object_field, "tile", -1)
    extended = jnp.concatenate([object_field, next_strip], axis=2)
    kernel_re, kernel_im, far_re, far_im = build_tables(phases, wave_side)
    live_slots = counts[0]
    anchor = jnp.zeros((), jnp.int32)
    forward_mats = []
    layer_index = 0
    forward_mats.append(
        (jnp.where(last_section, far_re, kernel_re), jnp.where(last_section, far_im, kernel_im))
    )
    adjoint_mats = [(matrix_pair[0].T, -matrix_pair[1].T) for matrix_pair in forward_mats]
    per_step = 1
    groups = slot_count // per_step

    def windows_of(group_index):
        top_rows = lax.dynamic_slice_in_dim(pos_row, group_index * per_step, per_step)
        left_cols = lax.dynamic_slice_in_dim(pos_col, group_index * per_step, per_step)

        def cut_window(top_row, left_col):
            return lax.dynamic_slice(
                extended,
                (anchor, anchor, top_row, left_col),
                (2, layer_count, wave_side, wave_side),
            )

        return (jax.vmap(cut_window)(top_rows, left_cols), top_rows, left_cols)

    def forward(group_index, wave_re, wave_im, stored):
        windows, top_rows, left_cols = windows_of(group_index)
        entries = [jnp.stack([wave_re, wave_im], axis=1)]
        mixed_re, mixed_im = transmit(windows[:, 0, 0], windows[:, 1, 0], wave_re, wave_im)
        wave_re, wave_im = propagate(forward_mats[0][0], forward_mats[0][1], mixed_re, mixed_im)
        stored = lax.dynamic_update_slice_in_dim(
            stored, jnp.stack(entries, axis=1)[None], group_index, 0
        )
        return (stored, jnp.stack([wave_re, wave_im], axis=1))

    def backward(group_index, back_re, back_im, stored, gradient):
        windows, top_rows, left_cols = windows_of(group_index)
        entries = lax.dynamic_index_in_dim(stored, group_index, 0, keepdims=False)
        patch_re = [None] * layer_count
        patch_im = [None] * layer_count
        for layer_index in reversed(range(layer_count)):
            matrix_re, matrix_im = adjoint_mats[layer_index]
            spread_re, spread_im = propagate(matrix_re, matrix_im, back_re, back_im)
            patch_re[layer_index], patch_im[layer_index] = conj_times(
                entries[:, layer_index, 0], entries[:, layer_index, 1], spread_re, spread_im
            )
            next_re, next_im = conj_times(
                windows[:, 0, layer_index], windows[:, 1, layer_index], spread_re, spread_im
            )
            back_re = next_re.astype(jnp.bfloat16)
            back_im = next_im.astype(jnp.bfloat16)
        patches = jnp.stack([jnp.stack(patch_re, axis=1), jnp.stack(patch_im, axis=1)], axis=1)
        corner = (anchor, anchor, top_rows[0], left_cols[0])
        current = lax.dynamic_slice(gradient, corner, (2, layer_count, wave_side, wave_side))
        gradient = lax.dynamic_update_slice(gradient, current + patches[0], corner)
        return (gradient, jnp.stack([back_re, back_im], axis=1))

    probe_wave = probe[None]

    def advance(step_index, carried, send_down, send_up):
        stored, gradient, from_above, from_below = carried
        front_group = step_index - section
        rear_group = step_index - 2 * (sections - 1) + section
        front_ok = (front_group >= 0) & (front_group < groups)
        rear_ok = (rear_group >= 0) & (rear_group < groups)
        front_at = jnp.clip(front_group, 0, groups - 1)
        rear_at = jnp.clip(rear_group, 0, groups - 1)
        start_wave = jnp.where(first_section, probe_wave, from_above)
        stored, leaving = lax.cond(
            front_ok,
            lambda saved_in: forward(front_at, start_wave[:, 0], start_wave[:, 1], saved_in),
            lambda saved_in: (saved_in, jnp.zeros_like(start_wave)),
            stored,
        )
        measured = lax.dynamic_slice_in_dim(intensities, front_at * per_step, per_step, 0).astype(
            jnp.float32
        )
        slot_ids = front_at * per_step + jnp.arange(per_step, dtype=jnp.int32)
        weights = (slot_ids < live_slots).astype(jnp.float32)
        leave_re = leaving[:, 0].astype(jnp.float32)
        leave_im = leaving[:, 1].astype(jnp.float32)
        factor = (
            2.0 * (leave_re * leave_re + leave_im * leave_im - measured) * weights[:, None, None]
        )
        residual = jnp.stack([factor * leave_re, factor * leave_im], axis=1).astype(jnp.bfloat16)
        arriving = jnp.where(last_section, residual, from_below)
        gradient, returning = lax.cond(
            rear_ok,
            lambda grad_in: backward(rear_at, arriving[:, 0], arriving[:, 1], stored, grad_in),
            lambda grad_in: (grad_in, jnp.zeros_like(arriving)),
            gradient,
        )
        if send_down:
            from_above = shifted(leaving, "sec", 1)
        if send_up:
            from_below = shifted(returning, "sec", -1)
        return (stored, gradient, from_above, from_below)

    carried = (
        jnp.zeros((groups, per_step, layer_count, 2, wave_side, wave_side), jnp.bfloat16),
        jnp.zeros((2, layer_count, 2 * strip_rows, object_field.shape[3]), jnp.float32),
        jnp.zeros((per_step, 2, wave_side, wave_side), jnp.bfloat16),
        jnp.zeros((per_step, 2, wave_side, wave_side), jnp.bfloat16),
    )
    carried = advance(0, carried, True, False)
    carried = lax.fori_loop(
        1,
        groups + 1,
        lambda step_index, inner_state: advance(step_index, inner_state, True, True),
        carried,
    )
    carried = advance(groups + 1, carried, False, False)
    gradient = carried[1]
    arrived = shifted(gradient[:, :, strip_rows:].astype(jnp.bfloat16), "tile", 1).astype(
        jnp.float32
    )
    return gradient[:, :, :strip_rows] + arrived


def solution(mesh):
    placed = (
        P(None, "sec", "tile", None),
        P(),
        P(),
        P("tile", None, None),
        P("tile"),
        P("tile"),
        P("tile"),
    )
    return jax.shard_map(
        on_device,
        mesh=mesh,
        in_specs=placed,
        out_specs=P(None, "sec", "tile", None),
        check_vma=False,
    )
```

profile of v0, /device:TPU:24, one launch (start us, length us, event | category | flops | bytes accessed | tf_op | source)
XLA Modules:
  0.0 139.5 jit_solution(12729323497896378083)
XLA Ops:
  0.0 4.4 %collective-permute-start.2 = (bf16[2,1,256,512]{3,2,0,1:T(8,128)(2,1)}, bf16[2,1,256,512]{3,2,0,1:T(8,128)(2,1)S(1)}, u32[]{:S(2)}, u32[]{:S(2)}) collective-permute-start(bf16[2,1,256,512]{3,2,0,1:T(8,128)(2,1)} %bitcast.458), channel_id=1, source_target_pairs={{1,0},{2,1},{3,2},{4,3},{5,4},{6,5},{7,6},{8,7},{9,8},{10,9},{11,1... | collective-permute-start | bytes 1572872 | tf_op jit(solution)/shard_map/ppermute | solution.py:12
  4.4 1.0 broadcast_multiply_fusion
  5.4 3.1 %fusion.114 = f32[256,256]{1,0:T(8,128)S(1)} fusion(f32[256]{0:T(256)} %param.23), kind=kOutput, calls=%fused_computation.239 | convolution fusion | flops 203227136 | bytes 263168 | tf_op jit(solution)/shard_map/dot_general | solution.py:26
  8.4 2.4 %fusion.115 = f32[256,256]{1,0:T(8,128)S(1)} fusion(f32[256]{0:T(256)S(1)} %copy-done.4), kind=kOutput, calls=%fused_computation.240 | convolution fusion | flops 203227136 | bytes 263168 | tf_op jit(solution)/shard_map/dot_general | solution.py:30
  10.8 2.4 %fusion.96 = bf16[256,256]{1,0:T(8,128)(2,1)S(1)} fusion(f32[256,256]{1,0:T(8,128)S(1)} %fusion.114, f32[256]{0:T(256)S(1)} %copy-done.4), kind=kOutput, calls=%fused_computation.202 | convolution fusion | flops 203423744 | bytes 394240 | tf_op jit(solution)/shard_map/dot_general | solution.py:27
  13.2 2.4 %broadcast_select_fusion.4 = (bf16[256,256]{1,0:T(8,128)(2,1)S(1)}, bf16[256,256]{1,0:T(8,128)(2,1)S(1)}) fusion(pred[]{:T(512)} %eq.9, f32[256,256]{1,0:T(8,128)S(1)} %fusion.115, f32[256]{0:T(256)S(1)} %copy-done.4), kind=kOutput, calls=%fused_computation.255 | convolution fusion | flops 204603392 | bytes 525313 | tf_op jit(solution)/shard_map/dot_general | solution.py:31
  15.7 1.0 multiply_convert_fusion
  18.7 1.0 copy.17
  20.0 13.2 %conditional.6 = (bf16[2,1,1,2,256,256]{5,4,3,2,1,0:T(8,128)(2,1)}, bf16[1,2,256,256]{3,2,1,0:T(8,128)(2,1)}) conditional(s32[]{:T(128)} %convert_element_type.747, () %tuple.99, (pred[]{:T(512)}, bf16[2,256,256]{2,1,0:T(8,128)(2,1)S(1)}, s32[]{:T(128)}, s32[2]{0:T(128)S(1)}, s32[2]{0:T(128)S(1)}, /*index=5*/bf16[2,1,512,512]{3,2,0,1:T(8,128)(2,1)S(1)}, ...), branch_computations={%region_0.1_spmd, %region_1.2_spmd} | conditional | flops 270139392 | bytes 8127133 | solution.py:166
  25.4 1.1 fusion.155
  26.7 1.1 fusion.156
  27.9 1.1 fusion.157
  29.7 1.1 fusion.33
  30.8 0.7 pad_maximum_fusion
  31.6 0.8 broadcast_in_dim.27
  32.4 0.7 bitcast_dynamic-update-slice_fusion
  33.1 1.3 collective-permute-start.3
  34.4 1.1 fusion.117
  36.3 1.6 %conditional.7 = (f32[2,1,512,512]{3,2,0,1:T(8,128)}) conditional(s32[]{:T(128)} %convert_element_type.753, () %tuple.101, (s32[]{:T(128)}, bf16[2,1,1,2,256,256]{5,4,3,2,1,0:T(8,128)(2,1)}, pred[1,2,256,256]{3,2,1,0:T(8,128)(4,1)}, bf16[1,2,256,256]{3,2,1,0:T(8,128)(2,1)S(1)}, bf16[1,2,256,256]{3,2,1,0:T(8,128)(2,1)S(1)}, ...), branch_computations={%region_2.3_spmd, %region_3.4_spmd} | conditional | bytes 12189832 | solution.py:184
  36.3 1.6 %broadcast_in_dim.38 = f32[2,1,512,512]{3,2,0,1:T(8,128)} broadcast(f32[]{:T(128)} %constant.147.clone), dimensions={} | broadcast | bytes 2097156 | tf_op jit(solution)/shard_map/broadcast_in_dim | solution.py:198
  38.0 66.7 %while.39 = (s32[]{:T(128)}, bf16[2,1,1,2,256,256]{5,4,3,2,1,0:T(8,128)(2,1)}, f32[2,1,512,512]{3,2,0,1:T(8,128)}, bf16[1,2,256,256]{3,2,1,0:T(8,128)(2,1)S(1)},...) while((s32[]{:T(128)}, ...), condition=%wide.region_9.10_spmd, body=%wide.region_4.9_spmd.sunk | while | flops 541720576 | bytes 22152668 | solution.py:203
  38.0 8.0 %conditional.12 = (bf16[2,1,1,2,256,256]{5,4,3,2,1,0:T(8,128)(2,1)}, bf16[1,2,256,256]{3,2,1,0:T(8,128)(2,1)S(1)}) conditional(s32[]{:T(128)} %convert_element_type.968, bf16[2,1,1,2,256,256]{5,4,3,2,1,0:T(8,128)(2,1)} %get-tuple-element.1119, (pred[]{:T(512)}, bf16[1,2,256,256]{3,2,1,0:T(8,128)(2,1)S(1)}, bf16[1,2,256,256]{3,2,1,0:T(8,128)(2,1)S(1)}, ...), branch_computations={%region_5.5_spmd, %region_6.6_spmd} | conditional | flops 270008320 | bytes 7602842 | solution.py:166
  43.2 0.8 bitcast_dynamic-update-slice_fusion.1
  46.6 1.0 fusion.254
  47.7 0.7 conditional.13
  47.7 0.7 broadcast.84
  48.4 1.3 collective-permute-start.1
  49.7 19.3 %collective-permute-start = (bf16[1,2,256,256]{3,2,1,0:T(8,128)(2,1)S(1)}, bf16[1,2,256,256]{3,2,1,0:T(8,128)(2,1)S(1)}, u32[]{:S(2)}, u32[]{:S(2)}) collective-permute-start(bf16[1,2,256,256]{3,2,1,0:T(8,128)(2,1)S(1)} %get-tuple-element.1077), channel_id=1, source_target_pairs={{0,16},{1,17},{2,18},{3,19},{4,20},{5,21},{6,22},{7,23},{8,24},{9,... | collective-permute-start | bytes 786440 | tf_op jit(solution)/shard_map/while/body/eval_jaxpr/ppermute | solution.py:12
  69.1 1.1 collective-permute-done
  70.9 1.0 fusion.254
  71.9 20.0 %conditional.13 = (f32[2,1,512,512]{3,2,0,1:T(8,128)}, bf16[1,2,256,256]{3,2,1,0:T(8,128)(2,1)}) conditional(s32[]{:T(128)} %convert_element_type.969, f32[2,1,512,512]{3,2,0,1:T(8,128)} %get-tuple-element.1120, (s32[]{:T(128)}, s32[2]{0:T(128)S(1)}, s32[2]{0:T(128)S(1)}, f32[2,1,512,512]{3,2,0,1:T(8,128)}, ...), branch_computations={%region_7.7_spmd, %region_8.8_spmd} | conditional | flops 270794752 | bytes 11272417 | solution.py:184
  78.3 1.0 dynamic-slice_bitcast_fusion.5
  79.6 0.7 pad_maximum_fusion.2
  83.8 1.4 fusion.62
  85.2 6.7 %dynamic_update_slice.15 = f32[2,1,512,512]{3,2,0,1:T(8,128)} dynamic-update-slice(f32[2,1,512,512]{3,2,0,1:T(8,128)} %get-tuple-element.726, f32[2,1,256,256]{3,2,0,1:T(8,128)S(1)} %fusion.62, s32[]{:T(128)} %constant.162.clone, s32[]{:T(128)} %constant.162.clone, s32[]{:T(128)S(6)} %select_n.165, s32[]{:T(128)S(6)} %select_n.166) | dynamic-update-slice | bytes 1048580 | tf_op jit(solution)/shard_map/while/body/eval_jaxpr/cond/branch_1_fun/dynamic_update_slice | solution.py:152
  91.9 1.3 collective-permute-start.1
  93.2 10.4 %collective-permute-start = (bf16[1,2,256,256]{3,2,1,0:T(8,128)(2,1)S(1)}, bf16[1,2,256,256]{3,2,1,0:T(8,128)(2,1)S(1)}, u32[]{:S(2)}, u32[]{:S(2)}) collective-permute-start(bf16[1,2,256,256]{3,2,1,0:T(8,128)(2,1)S(1)} %get-tuple-element.1077), channel_id=1, source_target_pairs={{0,16},{1,17},{2,18},{3,19},{4,20},{5,21},{6,22},{7,23},{8,24},{9,... | collective-permute-start | bytes 786440 | tf_op jit(solution)/shard_map/while/body/eval_jaxpr/ppermute | solution.py:12
  103.5 1.1 collective-permute-done
  104.7 1.0 fusion.116
  105.8 17.1 %conditional.9 = (f32[2,1,512,512]{3,2,0,1:T(8,128)}) conditional(s32[]{:T(128)} %convert_element_type.746, f32[2,1,512,512]{3,2,0,1:T(8,128)} %get-tuple-element.790, (s32[]{:T(128)}, s32[2]{0:T(128)S(1)}, s32[2]{0:T(128)S(1)}, f32[2,1,512,512]{3,2,0,1:T(8,128)}, bf16[2,1,1,2,256,256]{5,4,3,2,1,0:T(8,128)(2,1)}, ...), branch_computations={%region_12.13_spmd, %region_13.14_spmd} | conditional | flops 270008320 | bytes 9830540 | solution.py:184
  105.8 1.0 select_n.179
  108.4 1.0 dynamic-slice_bitcast_fusion.1
  114.7 1.4 fusion.22
  116.1 6.8 %dynamic_update_slice.17 = f32[2,1,512,512]{3,2,0,1:T(8,128)} dynamic-update-slice(f32[2,1,512,512]{3,2,0,1:T(8,128)} %get-tuple-element.770, f32[2,1,256,256]{3,2,0,1:T(8,128)S(1)} %fusion.22, s32[]{:T(128)} %constant.181.clone, s32[]{:T(128)} %constant.181.clone, s32[]{:T(128)S(6)} %select_n.177, s32[]{:T(128)S(6)} %select_n.178) | dynamic-update-slice | bytes 1048580 | tf_op jit(solution)/shard_map/cond/branch_1_fun/dynamic_update_slice | solution.py:152
  122.9 1.3 slice.376
  124.2 1.9 %collective-permute-start.4 = (bf16[2,1,256,512]{3,2,1,0:T(8,128)(2,1)S(1)}, bf16[2,1,256,512]{3,2,1,0:T(8,128)(2,1)S(1)}, u32[]{:S(2)}, u32[]{:S(2)}) collective-permute-start(bf16[2,1,256,512]{3,2,1,0:T(8,128)(2,1)S(1)} %slice.376), channel_id=1, source_target_pairs={{0,1},{1,2},{2,3},{3,4},{4,5},{5,6},{6,7},{7,8},{8,9},{9,10},{10,1... | collective-permute-start | bytes 1572872 | tf_op jit(solution)/shard_map/ppermute | solution.py:12
  126.1 10.9 %collective-permute-done.4 = bf16[2,1,256,512]{3,2,1,0:T(8,128)(2,1)S(1)} collective-permute-done((bf16[2,1,256,512]{3,2,1,0:T(8,128)(2,1)S(1)}, bf16[2,1,256,512]{3,2,1,0:T(8,128)(2,1)S(1)}, u32[]{:S(2)}, u32[]{:S(2)}) %collective-permute-start.4) | collective-permute-done | bytes 524320 | tf_op jit(solution)/shard_map/ppermute | solution.py:12
  137.1 2.4 %slice_add_fusion = f32[2,1,256,512]{3,2,1,0:T(8,128)} fusion(f32[2,1,512,512]{3,2,1,0:T(8,128)} %bitcast.174, bf16[2,1,256,512]{3,2,1,0:T(8,128)(2,1)S(1)} %collective-permute-done.4), kind=kLoop, calls=%fused_computation.205 | loop fusion | flops 524288 | bytes 2621440 | tf_op jit(solution)/shard_map/add | solution.py:214
  (80 shorter events, 14.6 us)
Async XLA Ops:
  0.0 8.4 %copy-start.4 = (f32[256]{0:T(256)S(1)}, f32[256]{0:T(256)}, u32[]{:S(2)}) copy-start(f32[256]{0:T(256)} %param.23) | copy-start | bytes 3076
  0.0 19.8 %collective-permute-start.2 = (bf16[2,1,256,512]{3,2,0,1:T(8,128)(2,1)}, bf16[2,1,256,512]{3,2,0,1:T(8,128)(2,1)S(1)}, u32[]{:S(2)}, u32[]{:S(2)}) collective-permute-start(bf16[2,1,256,512]{3,2,0,1:T(8,128)(2,1)} %bitcast.458), channel_id=1, source_target_pairs={{1,0},{2,1},{3,2},{4,3},{5,4},{6,5},{7,6},{8,7},{9,8},{10,9},{11,1... | collective-permute-start | bytes 1572872 | tf_op jit(solution)/shard_map/ppermute | solution.py:12
  15.6 4.2 %copy-start.3 = (bf16[2,1,256,512]{3,2,1,0:T(8,128)(2,1)S(1)}, bf16[2,1,256,512]{3,2,1,0:T(8,128)(2,1)}, u32[]{:S(2)}) copy-start(bf16[2,1,256,512]{3,2,1,0:T(8,128)(2,1)} %param.21) | copy-start | bytes 1572868
  17.5 2.4 %copy-start = (bf16[2,256,256]{2,1,0:T(8,128)(2,1)S(1)}, bf16[2,256,256]{2,1,0:T(8,128)(2,1)}, u32[]{:S(2)}) copy-start(bf16[2,256,256]{2,1,0:T(8,128)(2,1)} %param.22) | copy-start | bytes 786436
  17.5 2.4 %copy-start.5 = (s32[2]{0:T(128)S(1)}, s32[2]{0:T(128)}, u32[]{:S(2)}) copy-start(s32[2]{0:T(128)} %param.25) | copy-start | bytes 28
  17.6 2.4 %copy-start.6 = (s32[2]{0:T(128)S(1)}, s32[2]{0:T(128)}, u32[]{:S(2)}) copy-start(s32[2]{0:T(128)} %param.26) | copy-start | bytes 28
  18.7 17.7 %copy-start.1 = (bf16[256,256]{0,1:T(8,128)(2,1)}, bf16[256,256]{0,1:T(8,128)(2,1)S(1)}, u32[]{:S(2)}) copy-start(bf16[256,256]{0,1:T(8,128)(2,1)S(1)} %get-tuple-element.957) | copy-start | bytes 393220
  33.1 4.8 %collective-permute-start.3 = (bf16[1,2,256,256]{3,2,1,0:T(8,128)(2,1)}, bf16[1,2,256,256]{3,2,1,0:T(8,128)(2,1)S(1)}, u32[]{:S(2)}, u32[]{:S(2)}) collective-permute-start(bf16[1,2,256,256]{3,2,1,0:T(8,128)(2,1)} %get-tuple-element.789), channel_id=1, source_target_pairs={{0,16},{1,17},{2,18},{3,19},{4,20},{5,21},{6,22},{7,23},{8,24},{9,... | collective-permute-start | bytes 786440 | tf_op jit(solution)/shard_map/ppermute | solution.py:12
  48.4 20.6 %collective-permute-start.1 = (bf16[1,2,256,256]{3,2,1,0:T(8,128)(2,1)}, bf16[1,2,256,256]{3,2,1,0:T(8,128)(2,1)S(1)}, u32[]{:S(2)}, u32[]{:S(2)}) collective-permute-start(bf16[1,2,256,256]{3,2,1,0:T(8,128)(2,1)} %get-tuple-element.1081), channel_id=1, source_target_pairs={{16,0},{17,1},{18,2},{19,3},{20,4},{21,5},{22,6},{23,7},{24,8},{25... | collective-permute-start | bytes 786440 | tf_op jit(solution)/shard_map/while/body/eval_jaxpr/ppermute | solution.py:12
  49.7 20.5 %collective-permute-start = (bf16[1,2,256,256]{3,2,1,0:T(8,128)(2,1)S(1)}, bf16[1,2,256,256]{3,2,1,0:T(8,128)(2,1)S(1)}, u32[]{:S(2)}, u32[]{:S(2)}) collective-permute-start(bf16[1,2,256,256]{3,2,1,0:T(8,128)(2,1)S(1)} %get-tuple-element.1077), channel_id=1, source_target_pairs={{0,16},{1,17},{2,18},{3,19},{4,20},{5,21},{6,22},{7,23},{8,24},{9,... | collective-permute-start | bytes 786440 | tf_op jit(solution)/shard_map/while/body/eval_jaxpr/ppermute | solution.py:12
  91.9 11.7 %collective-permute-start.1 = (bf16[1,2,256,256]{3,2,1,0:T(8,128)(2,1)}, bf16[1,2,256,256]{3,2,1,0:T(8,128)(2,1)S(1)}, u32[]{:S(2)}, u32[]{:S(2)}) collective-permute-start(bf16[1,2,256,256]{3,2,1,0:T(8,128)(2,1)} %get-tuple-element.1081), channel_id=1, source_target_pairs={{16,0},{17,1},{18,2},{19,3},{20,4},{21,5},{22,6},{23,7},{24,8},{25... | collective-permute-start | bytes 786440 | tf_op jit(solution)/shard_map/while/body/eval_jaxpr/ppermute | solution.py:12
  93.2 11.5 %collective-permute-start = (bf16[1,2,256,256]{3,2,1,0:T(8,128)(2,1)S(1)}, bf16[1,2,256,256]{3,2,1,0:T(8,128)(2,1)S(1)}, u32[]{:S(2)}, u32[]{:S(2)}) collective-permute-start(bf16[1,2,256,256]{3,2,1,0:T(8,128)(2,1)S(1)} %get-tuple-element.1077), channel_id=1, source_target_pairs={{0,16},{1,17},{2,18},{3,19},{4,20},{5,21},{6,22},{7,23},{8,24},{9,... | collective-permute-start | bytes 786440 | tf_op jit(solution)/shard_map/while/body/eval_jaxpr/ppermute | solution.py:12
  104.7 1.1 copy-start.2
  124.2 12.9 %collective-permute-start.4 = (bf16[2,1,256,512]{3,2,1,0:T(8,128)(2,1)S(1)}, bf16[2,1,256,512]{3,2,1,0:T(8,128)(2,1)S(1)}, u32[]{:S(2)}, u32[]{:S(2)}) collective-permute-start(bf16[2,1,256,512]{3,2,1,0:T(8,128)(2,1)S(1)} %slice.376), channel_id=1, source_target_pairs={{0,1},{1,2},{2,3},{3,4},{4,5},{5,6},{6,7},{7,8},{8,9},{9,10},{10,1... | collective-permute-start | bytes 1572872 | tf_op jit(solution)/shard_map/ppermute | solution.py:12
where the time goes:
time: 140 us; the launch traced here: 139 us
  starting transfers between devices  39.8 us (28%)
  local copies, waits for them, and re-layouts  27.9 us (20%)
  matrix products  21.2 us (15%)
  loops' own time  20 us (14%)
  other arithmetic  16.4 us (12%)
  waiting for transfers between devices  13.2 us (9%)
    ppermute x7, starting transfers between devices, shifted(): lax.ppermute(value, axis, [(source, source + steps) for source in range(f...  39.8 us
    dynamic_update_slice x2, local copies, waits for them, and re-layouts, backward(): gradient = lax.dynamic_update_slice(gradient, current + patches[0], corner)  13.5 us
    ppermute x7, waiting for transfers between devices, shifted(): lax.ppermute(value, axis, [(source, source + steps) for source in range(f...  13.2 us
    another operation x4, loops' own time, advance(): lax.cond(rear_ok, lambda grad_in: backward(rear_at, arriving[:, 0], arriv...  10.8 us
    another operation x4, loops' own time, advance(): lax.cond(front_ok, lambda saved_in: forward(front_at, start_wave[:, 0], s...  7.8 us
    dot_general x16, matrix products, right_product(): jnp.einsum('bmj,nj->bmn', field, matrix, preferred_element_type=jnp.float32)  5.52 us
    dot_general x16, matrix products, left_product(): jnp.einsum('mj,bjn->bmn', matrix, field, preferred_element_type=jnp.float32)  5.42 us
    another operation x8, other arithmetic, advance(): jnp.stack([factor * leave_re, factor * leave_im], axis=1)  4.3 us
  transfers between devices with their start and end apart: 7, of which 3 were waited for; matrix products, arithmetic and copies ran while one was open for 13% of the time, Pallas kernels for 0%

commit v1 on v0

v1 whole, which is shorter than its diff:
```python
import functools
import math

import jax
import jax.numpy as jnp
import numpy as np
from jax import lax
from jax.experimental import pallas as pl
from jax.experimental.pallas import tpu as pltpu
from jax.sharding import PartitionSpec as P

BF = jnp.bfloat16
F32 = jnp.float32


def mm(a, b):
    return jnp.dot(a, b, preferred_element_type=F32)


def base_tables(n):
    product = np.outer(np.arange(n), np.arange(n)) % n
    angles = product * (2.0 * math.pi / n)
    return np.cos(angles), np.sin(angles)


def tables_kernel(phase_ref, cos_ref, sin_ref, near_left, near_right):
    n = cos_ref.shape[0]
    phase = jnp.broadcast_to(phase_ref[...], (8, n))
    turn = jnp.where(
        lax.broadcasted_iota(jnp.int32, (8, n), 0) == 0, jnp.cos(phase), jnp.sin(phase)
    )

    def exact(a, b):
        return jnp.dot(a, b, precision=lax.Precision.HIGHEST, preferred_element_type=F32)

    by_cos = exact(turn, cos_ref[...])
    by_sin = exact(turn, sin_ref[...])
    scale = 1.0 / n
    ahead_re = (by_cos[0:1] + by_sin[1:2]) * scale
    ahead_im = (by_cos[1:2] - by_sin[0:1]) * scale
    behind_re = (by_cos[0:1] - by_sin[1:2]) * scale
    behind_im = (by_cos[1:2] + by_sin[0:1]) * scale

    def circulant(row):
        return pltpu.roll(
            jnp.broadcast_to(row, (n, n)), 0, 1, stride=1, stride_axis=0
        ).astype(BF)

    m_re, m_im = circulant(ahead_re), circulant(ahead_im)
    t_re, t_im = circulant(behind_re), circulant(behind_im)
    near_left[:n, :n] = m_re
    near_left[:n, n:] = -m_im
    near_left[n:, :n] = m_im
    near_left[n:, n:] = m_re
    near_right[:n, :n] = t_re
    near_right[:n, n:] = t_im
    near_right[n:, :n] = -t_im
    near_right[n:, n:] = t_re


def propagate(left, right, waves_re, waves_im):
    n = waves_re[0].shape[0]
    count = len(waves_re)
    field = jnp.concatenate(
        [jnp.concatenate(waves_re, axis=1), jnp.concatenate(waves_im, axis=1)], axis=0
    )
    inner = mm(left, field).astype(BF)
    rows = [
        jnp.concatenate([inner[:n, w * n : (w + 1) * n], inner[n:, w * n : (w + 1) * n]], axis=1)
        for w in range(count)
    ]
    outer = mm(jnp.concatenate(rows, axis=0), right)
    return (
        [outer[w * n : (w + 1) * n, :n] for w in range(count)],
        [outer[w * n : (w + 1) * n, n:] for w in range(count)],
    )


def wave_kernel(
    own_set,
    meta_ref,
    here_ref,
    there_ref,
    probe_ref,
    own_int_ref,
    int_here_ref,
    int_there_ref,
    near_left,
    near_right,
    far_left,
    far_right,
    own_here_ref,
    own_there_ref,
    base_ref,
    out_ref,
    patch_re,
    patch_im,
):
    n = probe_ref.shape[1]
    slots = own_int_ref.shape[0]
    sec = meta_ref[2, 0]
    parity = meta_ref[2, 1]
    is_own = (parity == 0) if own_set else (parity != 0)
    which = jnp.where(is_own, 0, 1)
    rows = lax.broadcasted_iota(jnp.int32, (n, n), 0)
    cols = lax.broadcasted_iota(jnp.int32, (n, n), 1)
    top = sec == 0

    masks = []
    for w in range(slots):
        r = meta_ref[which, w]
        c = meta_ref[which, slots + w]
        at_or_past = (rows >= r).astype(jnp.int32)
        mine = at_or_past == jnp.where(is_own, 1, 0)
        masks.append((mine, cols >= c, r, c))
    live = meta_ref[which, 2 * slots]

    def planes(layer, part):
        def pick(a_ref, b_ref):
            a, b = a_ref[part, 0], b_ref[part, 0]
            return jnp.where(top if layer == 0 else jnp.logical_not(top), a, b).astype(F32)

        own = pick(own_here_ref, own_there_ref)
        other = pick(here_ref, there_ref)
        return [
            jnp.where(
                mine,
                jnp.where(left, own[:, :n], own[:, n:]),
                jnp.where(left, other[:, :n], other[:, n:]),
            )
            for mine, left, _, _ in masks
        ]

    def rolled(part):
        plane = probe_ref[part].astype(F32)
        return [pltpu.roll(pltpu.roll(plane, r, 0), c, 1) for _, _, r, c in masks]

    def to_bf(parts):
        return [p.astype(BF) for p in parts]

    def times(a_re, a_im, b_re, b_im):
        return (
            [ar * br - ai * bi for ar, ai, br, bi in zip(a_re, a_im, b_re, b_im)],
            [ar * bi + ai * br for ar, ai, br, bi in zip(a_re, a_im, b_re, b_im)],
        )

    def conj_times(a_re, a_im, b_re, b_im):
        return (
            [ar * br + ai * bi for ar, ai, br, bi in zip(a_re, a_im, b_re, b_im)],
            [ar * bi - ai * br for ar, ai, br, bi in zip(a_re, a_im, b_re, b_im)],
        )

    def rounded(parts):
        return [p.astype(BF).astype(F32) for p in parts]

    near_l, near_r = near_left[...], near_right[...]
    far_l, far_r = far_left[...], far_right[...]
    probe_re, probe_im = rolled(0), rolled(1)
    t_re, t_im = planes(0, 0), planes(0, 1)
    z_re, z_im = times(t_re, t_im, probe_re, probe_im)
    psi_re, psi_im = propagate(near_l, near_r, to_bf(z_re), to_bf(z_im))
    psi_re, psi_im = rounded(psi_re), rounded(psi_im)
    t_re, t_im = planes(1, 0), planes(1, 1)
    z_re, z_im = times(t_re, t_im, psi_re, psi_im)
    end_re, end_im = propagate(far_l, far_r, to_bf(z_re), to_bf(z_im))
    chi_re, chi_im = [], []
    for w in range(slots):
        received = jnp.where(
            top,
            jnp.concatenate([int_here_ref[w], int_there_ref[w]], axis=0),
            jnp.concatenate([int_there_ref[w], int_here_ref[w]], axis=0),
        )
        measured = jnp.where(is_own, own_int_ref[w], received).astype(F32)
        weight = jnp.where(w < live, 2.0, 0.0)
        factor = weight * (end_re[w] * end_re[w] + end_im[w] * end_im[w] - measured)
        chi_re.append(factor * end_re[w])
        chi_im.append(factor * end_im[w])
    y_re, y_im = propagate(far_r, far_l, to_bf(chi_re), to_bf(chi_im))
    y_re, y_im = rounded(y_re), rounded(y_im)

    def keep(a_re, a_im, b_re, b_im):
        parts_re, parts_im = conj_times(a_re, a_im, b_re, b_im)
        for w in range(slots):
            patch_re[w] = parts_re[w]
            patch_im[w] = parts_im[w]

    @pl.when(top)
    def _():
        g_re, g_im = conj_times(t_re, t_im, y_re, y_im)
        w_re, w_im = propagate(near_r, near_l, to_bf(g_re), to_bf(g_im))
        keep(probe_re, probe_im, rounded(w_re), rounded(w_im))

    @pl.when(jnp.logical_not(top))
    def _():
        keep(psi_re, psi_im, y_re, y_im)

    for part, patch in ((0, patch_re), (1, patch_im)):
        left_sum = base_ref[part, 0, :, :n] if base_ref is not None else jnp.zeros((n, n), F32)
        right_sum = base_ref[part, 0, :, n:] if base_ref is not None else jnp.zeros((n, n), F32)
        for w, (mine, left, _, _) in enumerate(masks):
            value = jnp.where(mine, patch[w], 0.0)
            left_sum = left_sum + jnp.where(left, value, 0.0)
            right_sum = right_sum + jnp.where(left, 0.0, value)
        out_ref[part, 0, :, :n] = left_sum
        out_ref[part, 0, :, n:] = right_sum


def first_kernel(meta, h, t, p, oi, ih, it, nl, nr, fl, fr, oh, ot, out, pr, pi):
    wave_kernel(True, meta, h, t, p, oi, ih, it, nl, nr, fl, fr, oh, ot, None, out, pr, pi)


def second_kernel(meta, h, t, p, oi, ih, it, nl, nr, fl, fr, oh, ot, base, out, pr, pi):
    wave_kernel(False, meta, h, t, p, oi, ih, it, nl, nr, fl, fr, oh, ot, base, out, pr, pi)


VM = pl.BlockSpec(memory_space=pltpu.VMEM)
SM = pl.BlockSpec(memory_space=pltpu.SMEM)


def on_device(obj, probe, phases, intensities, pos_row, pos_col, counts):
    n = probe.shape[1]
    slots = pos_row.shape[0]
    tiles = lax.axis_size("tile")
    sec = lax.axis_index("sec")
    tile = lax.axis_index("tile")
    parity = tile % 2

    def swap(value):
        return lax.ppermute(value, "sec", [(0, 1), (1, 0)])

    def send(value, pairs):
        return lax.ppermute(value, "tile", [(a, b) for a, b in pairs if 0 <= b < tiles])

    onward = [(i, i + 1) for i in range(tiles)]
    paired = [(i, i ^ 1) for i in range(tiles)]
    across = [(i, i + 1 if i % 2 else i - 1) for i in range(tiles)]

    facing = send(obj, paired)
    own_meta = jnp.concatenate([pos_row, pos_col, counts])
    past_meta = send(own_meta, onward)
    half = intensities.shape[1] // 2
    int_here = send(
        lax.dynamic_slice_in_dim(intensities, sec * half, half, 1), onward
    )
    own_there = swap(obj)
    cos_table, sin_table = base_tables(n)
    f_re, f_im = cos_table / math.sqrt(n), -sin_table / math.sqrt(n)
    far_left = jnp.asarray(np.block([[f_re, -f_im], [f_im, f_re]]), BF)
    far_right = jnp.asarray(np.block([[f_re, f_im], [-f_im, f_re]]), BF)
    double = jax.ShapeDtypeStruct((2 * n, 2 * n), BF)
    near_left, near_right = pl.pallas_call(
        tables_kernel,
        out_shape=(double, double),
        in_specs=[VM] * 3,
        out_specs=(VM, VM),
        name="tables",
    )(phases[None], jnp.asarray(cos_table, F32), jnp.asarray(sin_table, F32))
    later, near_left = lax.optimization_barrier((obj, near_left))
    opposite = send(later, across)
    facing_there = swap(facing)
    int_there = swap(int_here)
    opposite_there = swap(opposite)
    place = jnp.stack([sec, parity] + [jnp.zeros((), jnp.int32)] * (2 * slots - 1))
    meta = jnp.stack([own_meta, past_meta, place]).astype(jnp.int32)
    out_shape = jax.ShapeDtypeStruct(obj.shape, F32)
    scratch = [pltpu.VMEM((slots, n, n), F32)] * 2
    params = pltpu.CompilerParams(vmem_limit_bytes=40 * 1024 * 1024)
    shared = (probe, intensities, int_here, int_there, near_left, near_right, far_left, far_right, obj, own_there)
    partial = pl.pallas_call(
        first_kernel,
        out_shape=out_shape,
        in_specs=[SM] + [VM] * 12,
        out_specs=VM,
        scratch_shapes=scratch,
        compiler_params=params,
        name="facing_waves",
    )(meta, facing, facing_there, *shared)
    return pl.pallas_call(
        second_kernel,
        out_shape=out_shape,
        in_specs=[SM] + [VM] * 13,
        out_specs=VM,
        scratch_shapes=scratch,
        compiler_params=params,
        name="opposite_waves",
    )(meta, opposite, opposite_there, *shared, partial)


def solution(mesh):
    placed = (
        P(None, "sec", "tile", None),
        P(),
        P(),
        P("tile", None, None),
        P("tile"),
        P("tile"),
        P("tile"),
    )
    return jax.shard_map(
        on_device,
        mesh=mesh,
        in_specs=placed,
        out_specs=P(None, "sec", "tile", None),
        check_vma=False,
    )
```

time: 140 us -> 55.7 us (0.40)
  starting transfers between devices: 39.8 us -> 16.2 us
  local copies, waits for them, and re-layouts: 27.9 us -> 6.69 us
  matrix products: 21.2 us -> 0 us
  loops' own time: 20 us -> 0 us
  other arithmetic: 16.4 us -> 0.24 us
  Pallas kernels: 0 us -> 13.4 us
  waiting for transfers between devices: 13.2 us -> 17.9 us
    ppermute x7 -> x8, starting transfers between devices: 39.8 us -> 16.2 us  [the longest x4 16.1 us: send(): lax.ppermute(value, 'tile', [(a, b) for a, b in pairs if 0 <= b < tiles])]
    dot_general x36 -> x0, matrix products: 21.2 us -> none  [the longest x16 5.52 us: right_product(): jnp.einsum('bmj,nj->bmn', field, matrix, preferred_element_type=jnp.float32)]
    another operation x9 -> x0, loops' own time: 20 us -> none  [the longest x4 10.8 us: advance(): lax.cond(rear_ok, lambda grad_in: backward(rear_at, arriving[:, 0], arriv...]
    dynamic_update_slice x2 -> x0, local copies, waits for them, and re-layouts: 13.5 us -> none  [backward(): gradient = lax.dynamic_update_slice(gradient, current + patches[0], corner)]
    pallas_call x0 -> x3, Pallas kernels: none -> 13.4 us  [the longest x1 5.97 us: on_device(): pl.pallas_call(second_kernel, out_shape=out_shape, in_specs=[SM] + [VM] *...]
    another operation x11 -> x3, other arithmetic: 5.79 us -> 0.17 us  [on_device(): meta = jnp.stack([own_meta, past_meta, place]).astype(jnp.int32)]
    add x3 -> x0, other arithmetic: 5.11 us -> none  [the longest x2 2.74 us: backward(): gradient = lax.dynamic_update_slice(gradient, current + patches[0], corner)]
    unnamed x14 -> x20, local copies, waits for them, and re-layouts: 0.04 us -> 5.13 us
  transfers between devices with their start and end apart: 7 -> 8, of which waited for: 3 -> 3; matrix products, arithmetic and copies ran while one was open for 13% -> 3% of each run, Pallas kernels for 0% -> 13%
where the time goes in v1:
time: 55.7 us; the launch traced here: 55.2 us
  waiting for transfers between devices  17.9 us (32%)
  starting transfers between devices  16.2 us (29%)
  Pallas kernels  13.4 us (24%)
  local copies, waits for them, and re-layouts  6.69 us (12%)
  between operations  0.81 us (1%)
    ppermute x4, waiting for transfers between devices, send(): lax.ppermute(value, 'tile', [(a, b) for a, b in pairs if 0 <= b < tiles])  17.9 us
    ppermute x4, starting transfers between devices, send(): lax.ppermute(value, 'tile', [(a, b) for a, b in pairs if 0 <= b < tiles])  16.1 us
    pallas_call x1, Pallas kernels, on_device(): pl.pallas_call(second_kernel, out_shape=out_shape, in_specs=[SM] + [VM] *...  5.97 us
    unnamed x20, local copies, waits for them, and re-layouts  5.13 us
    pallas_call x1, Pallas kernels, on_device(): pl.pallas_call(first_kernel, out_shape=out_shape, in_specs=[SM] + [VM] *...  4.91 us
    pallas_call x1, Pallas kernels, on_device(): pl.pallas_call(tables_kernel, out_shape=(double, double), in_specs=[VM] *...  2.53 us
    dynamic_slice x1, local copies, waits for them, and re-layouts, on_device(): lax.dynamic_slice_in_dim(intensities, sec * half, half, 1)  1.56 us
  transfers between devices with their start and end apart: 8, of which 3 were waited for; matrix products, arithmetic and copies ran while one was open for 3% of the time, Pallas kernels for 13%

profile of v1, /device:TPU:24, one launch (start us, length us, event | category | flops | bytes accessed | tf_op | source)
XLA Modules:
  0.0 55.2 jit_solution(13841424148676230452)
XLA Ops:
  0.0 0.0 copy-start
  0.0 1.5 %collective-permute-start.6 = (bf16[2,1,256,512]{3,2,1,0:T(8,128)(2,1)}, bf16[2,1,256,512]{3,2,1,0:T(8,128)(2,1)S(1)}, u32[]{:S(2)}, u32[]{:S(2)}) collective-permute-start(bf16[2,1,256,512]{3,2,1,0:T(8,128)(2,1)} %oh.3), channel_id=1, source_target_pairs={{0,1},{1,0},{2,3},{3,2},{4,5},{5,4},{6,7},{7,6},{8,9},{9,8},{10,11... | collective-permute-start | bytes 1572872 | tf_op jit(solution)/shard_map/ppermute | solution.py:232
  1.5 2.5 %tables.1 = (bf16[512,512]{1,0:T(8,128)(2,1)}, bf16[512,512]{1,0:T(8,128)(2,1)}) custom-call(f32[1,256]{1,0:T(1,128)} %bitcast.8, f32[256,256]{1,0:T(8,128)} %constant.40.clone.cos_ref, f32[256,256]{1,0:T(8,128)} %constant.41.clone.sin_ref), custom_call_target="tpu_custom_call" | custom-call | tf_op jit(solution)/shard_map/tables/pallas_call | solution.py:251
  4.0 0.0 copy-start.6
  4.0 0.0 copy-done
  4.0 3.4 %collective-permute-start.1 = (bf16[2,1,256,512]{3,2,1,0:T(8,128)(2,1)S(1)}, bf16[2,1,256,512]{3,2,1,0:T(8,128)(2,1)S(1)}, u32[]{:S(2)}, u32[]{:S(2)}) collective-permute-start(bf16[2,1,256,512]{3,2,1,0:T(8,128)(2,1)S(1)} %copy-done), channel_id=1, source_target_pairs={{1,2},{2,1},{3,4},{4,3},{5,6},{6,5},{7,8},{8,7},{9,10},{10,9},{11,... | collective-permute-start | bytes 1572872 | tf_op jit(solution)/shard_map/ppermute | solution.py:232
  7.4 0.1 collective-permute-start.5
  7.5 7.5 %collective-permute-done.6.h = bf16[2,1,256,512]{3,2,1,0:T(8,128)(2,1)S(1)} collective-permute-done((bf16[2,1,256,512]{3,2,1,0:T(8,128)(2,1)}, bf16[2,1,256,512]{3,2,1,0:T(8,128)(2,1)S(1)}, u32[]{:S(2)}, u32[]{:S(2)}) %collective-permute-start.6) | collective-permute-done | bytes 524320 | tf_op jit(solution)/shard_map/ppermute | solution.py:232
  15.0 0.0 collective-permute-start.7
  15.0 6.3 %collective-permute-done.1.h = bf16[2,1,256,512]{3,2,1,0:T(8,128)(2,1)S(1)} collective-permute-done((bf16[2,1,256,512]{3,2,1,0:T(8,128)(2,1)S(1)}, bf16[2,1,256,512]{3,2,1,0:T(8,128)(2,1)S(1)}, u32[]{:S(2)}, u32[]{:S(2)}) %collective-permute-start.1) | collective-permute-done | bytes 524320 | tf_op jit(solution)/shard_map/ppermute | solution.py:232
  21.3 0.0 collective-permute-start.2
  21.3 1.6 %constant_dynamic-slice_fusion = bf16[2,128,256]{2,1,0:T(8,128)(2,1)} fusion(bf16[2,256,256]{2,1,0:T(8,128)(2,1)} %oi.3, s32[]{:T(128)S(6)} %select_n.11), kind=kLoop, calls=%fused_computation.3 | loop fusion | bytes 262148 | tf_op jit(solution)/shard_map/dynamic_slice | solution.py:243
  22.9 0.0 copy-start.8
  22.9 0.0 copy-start.9
  22.9 8.3 %collective-permute-start.3 = (bf16[2,128,256]{2,1,0:T(8,128)(2,1)}, bf16[2,128,256]{2,1,0:T(8,128)(2,1)S(1)}, u32[]{:S(2)}, u32[]{:S(2)}) collective-permute-start(bf16[2,128,256]{2,1,0:T(8,128)(2,1)} %constant_dynamic-slice_fusion), channel_id=1, source_target_pairs={{0,1},{1,2},{2,3},{3,4},{4,5},{5,6},{6,7},{7,8},{8,9},{9,10},{10,1... | collective-permute-start | bytes 393224 | tf_op jit(solution)/shard_map/ppermute | solution.py:232
  31.8 0.0 copy-done.8
  31.8 0.0 copy-done.9
  31.8 0.1 pad_add_fusion.1
  31.9 2.9 %collective-permute-start = (s32[5]{0:T(128)S(1)}, s32[5]{0:T(128)S(1)}, u32[]{:S(2)}, u32[]{:S(2)}) collective-permute-start(s32[5]{0:T(128)S(1)} %pad_add_fusion.1), channel_id=1, source_target_pairs={{0,1},{1,2},{2,3},{3,4},{4,5},{5,6},{6,7},{7,8},{8,9},{9,10},{10,1... | collective-permute-start | bytes 68 | tf_op jit(solution)/shard_map/ppermute | solution.py:232
  34.9 0.1 fusion
  34.9 0.0 collective-permute-done.3.ih
  35.0 0.0 collective-permute-start.4
  35.0 0.1 add_bitcast_fusion
  35.1 4.1 %collective-permute-done = s32[5]{0:T(128)S(1)} collective-permute-done((s32[5]{0:T(128)S(1)}, s32[5]{0:T(128)S(1)}, u32[]{:S(2)}, u32[]{:S(2)}) %collective-permute-start) | collective-permute-done | bytes 52 | tf_op jit(solution)/shard_map/ppermute | solution.py:232
  39.1 0.0 collective-permute-done.4.it
  39.2 0.0 collective-permute-done.5.ot
  39.2 0.0 collective-permute-done.7.t
  39.2 0.0 copy-done.6
  39.2 0.0 copy-start.1
  39.2 1.0 %copy-done.1 = bf16[512,512]{1,0:T(8,128)(2,1)S(1)} copy-done((bf16[512,512]{1,0:T(8,128)(2,1)S(1)}, bf16[512,512]{1,0:T(8,128)(2,1)}, u32[]{:S(2)}) %copy-start.1) | copy-done | bytes 524312
  40.2 0.0 copy-start.3
  40.2 1.0 %copy-done.3 = bf16[512,512]{1,0:T(8,128)(2,1)S(1)} copy-done((bf16[512,512]{1,0:T(8,128)(2,1)S(1)}, bf16[512,512]{1,0:T(8,128)(2,1)}, u32[]{:S(2)}) %copy-start.3) | copy-done | bytes 524312
  41.3 0.0 copy-start.4
  41.3 1.0 %copy-done.4 = bf16[512,512]{1,0:T(8,128)(2,1)S(1)} copy-done((bf16[512,512]{1,0:T(8,128)(2,1)S(1)}, bf16[512,512]{1,0:T(8,128)(2,1)}, u32[]{:S(2)}) %copy-start.4) | copy-done | bytes 524312
  42.3 0.0 copy-start.5
  42.3 1.0 %copy-done.5 = bf16[512,512]{1,0:T(8,128)(2,1)S(1)} copy-done((bf16[512,512]{1,0:T(8,128)(2,1)S(1)}, bf16[512,512]{1,0:T(8,128)(2,1)}, u32[]{:S(2)}) %copy-start.5) | copy-done | bytes 524312
  43.4 0.0 copy-start.7
  43.4 0.9 %copy-done.7 = bf16[2,256,256]{2,1,0:T(8,128)(2,1)S(1)} copy-done((bf16[2,256,256]{2,1,0:T(8,128)(2,1)S(1)}, bf16[2,256,256]{2,1,0:T(8,128)(2,1)}, u32[]{:S(2)}) %copy-start.7) | copy-done | bytes 262168
  44.3 0.0 copy-start.2
  44.3 4.9 %facing_waves.1.base = f32[2,1,256,512]{3,2,1,0:T(8,128)S(1)} custom-call(s32[3,5]{1,0:T(4,128)S(1)} %pad_add_fusion.meta, bf16[2,1,256,512]{3,2,1,0:T(8,128)(2,1)S(1)} %collective-permute-done.6.h, bf16[2,1,256,512]{3,2,1,0:T(8,128)(2,1)S(1)} %collective-permute-done.7.t, bf16[2,256,256]{2,1,0:T(8,128)(2,1)S(1)} %copy-done.7, ...), custom_call_target="tpu_custom_call" | custom-call | tf_op jit(solution)/shard_map/facing_waves/pallas_call | solution.py:269
  49.2 0.0 collective-permute-done.2.t
  49.2 0.0 copy-done.2
  49.2 6.0 %opposite_waves.1 = f32[2,1,256,512]{3,2,1,0:T(8,128)} custom-call(s32[3,5]{1,0:T(4,128)S(1)} %pad_add_fusion.meta, bf16[2,1,256,512]{3,2,1,0:T(8,128)(2,1)S(1)} %collective-permute-done.1.h, bf16[2,1,256,512]{3,2,1,0:T(8,128)(2,1)S(1)} %collective-permute-done.2.t, bf16[2,256,256]{2,1,0:T(8,128)(2,1)S(1)} %copy-done.7, bf16[2,256,256]{2,1,0:T(8,128)(2,1)S(1)} %copy-done.6, ...), custom_call_target="tpu_custom_call" | custom-call | tf_op jit(solution)/shard_map/opposite_waves/pallas_call | solution.py:278
  (2 shorter events, 0.0 us)
Async XLA Ops:
  0.0 4.0 %copy-start = (bf16[2,1,256,512]{3,2,1,0:T(8,128)(2,1)S(1)}, bf16[2,1,256,512]{3,2,1,0:T(8,128)(2,1)}, u32[]{:S(2)}) copy-start(bf16[2,1,256,512]{3,2,1,0:T(8,128)(2,1)} %oh.3) | copy-start | bytes 1572868
  0.0 15.0 %collective-permute-start.6 = (bf16[2,1,256,512]{3,2,1,0:T(8,128)(2,1)}, bf16[2,1,256,512]{3,2,1,0:T(8,128)(2,1)S(1)}, u32[]{:S(2)}, u32[]{:S(2)}) collective-permute-start(bf16[2,1,256,512]{3,2,1,0:T(8,128)(2,1)} %oh.3), channel_id=1, source_target_pairs={{0,1},{1,0},{2,3},{3,2},{4,5},{5,4},{6,7},{7,6},{8,9},{9,8},{10,11... | collective-permute-start | bytes 1572872 | tf_op jit(solution)/shard_map/ppermute | solution.py:232
  4.0 35.1 %copy-start.6 = (bf16[2,256,256]{2,1,0:T(8,128)(2,1)S(1)}, bf16[2,256,256]{2,1,0:T(8,128)(2,1)}, u32[]{:S(2)}) copy-start(bf16[2,256,256]{2,1,0:T(8,128)(2,1)} %oi.3) | copy-start | bytes 786436
  4.0 17.3 %collective-permute-start.1 = (bf16[2,1,256,512]{3,2,1,0:T(8,128)(2,1)S(1)}, bf16[2,1,256,512]{3,2,1,0:T(8,128)(2,1)S(1)}, u32[]{:S(2)}, u32[]{:S(2)}) collective-permute-start(bf16[2,1,256,512]{3,2,1,0:T(8,128)(2,1)S(1)} %copy-done), channel_id=1, source_target_pairs={{1,2},{2,1},{3,4},{4,3},{5,6},{6,5},{7,8},{8,7},{9,10},{10,9},{11,... | collective-permute-start | bytes 1572872 | tf_op jit(solution)/shard_map/ppermute | solution.py:232
  7.4 31.7 %collective-permute-start.5 = (bf16[2,1,256,512]{3,2,1,0:T(8,128)(2,1)S(1)}, bf16[2,1,256,512]{3,2,1,0:T(8,128)(2,1)S(1)}, u32[]{:S(2)}, u32[]{:S(2)}) collective-permute-start(bf16[2,1,256,512]{3,2,1,0:T(8,128)(2,1)S(1)} %copy-done), channel_id=1, source_target_pairs={{0,16},{16,0},{1,17},{17,1},{2,18},{18,2},{3,19},{19,3},{4,20},{20... | collective-permute-start | bytes 1572872 | tf_op jit(solution)/shard_map/ppermute | solution.py:229
  15.0 24.1 %collective-permute-start.7 = (bf16[2,1,256,512]{3,2,1,0:T(8,128)(2,1)S(1)}, bf16[2,1,256,512]{3,2,1,0:T(8,128)(2,1)S(1)}, u32[]{:S(2)}, u32[]{:S(2)}) collective-permute-start(bf16[2,1,256,512]{3,2,1,0:T(8,128)(2,1)S(1)} %collective-permute-done.6.h), channel_id=1, source_target_pairs={{0,16},{16,0},{1,17},{17,1},{2,18},{18,2},{3,19},{19,3},{4,20},{20... | collective-permute-start | bytes 1572872 | tf_op jit(solution)/shard_map/ppermute | solution.py:229
  21.3 27.9 %collective-permute-start.2 = (bf16[2,1,256,512]{3,2,1,0:T(8,128)(2,1)S(1)}, bf16[2,1,256,512]{3,2,1,0:T(8,128)(2,1)S(1)}, u32[]{:S(2)}, u32[]{:S(2)}) collective-permute-start(bf16[2,1,256,512]{3,2,1,0:T(8,128)(2,1)S(1)} %collective-permute-done.1.h), channel_id=1, source_target_pairs={{0,16},{16,0},{1,17},{17,1},{2,18},{18,2},{3,19},{19,3},{4,20},{20... | collective-permute-start | bytes 1572872 | tf_op jit(solution)/shard_map/ppermute | solution.py:229
  22.9 8.9 %copy-start.8 = (s32[2]{0:T(128)S(1)}, s32[2]{0:T(128)}, u32[]{:S(2)}) copy-start(s32[2]{0:T(128)} %param.16) | copy-start | bytes 28
  22.9 8.9 %copy-start.9 = (s32[2]{0:T(128)S(1)}, s32[2]{0:T(128)}, u32[]{:S(2)}) copy-start(s32[2]{0:T(128)} %param.15) | copy-start | bytes 28
  22.9 12.1 %collective-permute-start.3 = (bf16[2,128,256]{2,1,0:T(8,128)(2,1)}, bf16[2,128,256]{2,1,0:T(8,128)(2,1)S(1)}, u32[]{:S(2)}, u32[]{:S(2)}) collective-permute-start(bf16[2,128,256]{2,1,0:T(8,128)(2,1)} %constant_dynamic-slice_fusion), channel_id=1, source_target_pairs={{0,1},{1,2},{2,3},{3,4},{4,5},{5,6},{6,7},{7,8},{8,9},{9,10},{10,1... | collective-permute-start | bytes 393224 | tf_op jit(solution)/shard_map/ppermute | solution.py:232
  31.9 7.2 %collective-permute-start = (s32[5]{0:T(128)S(1)}, s32[5]{0:T(128)S(1)}, u32[]{:S(2)}, u32[]{:S(2)}) collective-permute-start(s32[5]{0:T(128)S(1)} %pad_add_fusion.1), channel_id=1, source_target_pairs={{0,1},{1,2},{2,3},{3,4},{4,5},{5,6},{6,7},{7,8},{8,9},{9,10},{10,1... | collective-permute-start | bytes 68 | tf_op jit(solution)/shard_map/ppermute | solution.py:232
  35.0 4.2 %collective-permute-start.4 = (bf16[2,128,256]{2,1,0:T(8,128)(2,1)S(1)}, bf16[2,128,256]{2,1,0:T(8,128)(2,1)S(1)}, u32[]{:S(2)}, u32[]{:S(2)}) collective-permute-start(bf16[2,128,256]{2,1,0:T(8,128)(2,1)S(1)} %collective-permute-done.3.ih), channel_id=1, source_target_pairs={{0,16},{16,0},{1,17},{17,1},{2,18},{18,2},{3,19},{19,3},{4,20},{20... | collective-permute-start | bytes 393224 | tf_op jit(solution)/shard_map/ppermute | solution.py:229
  39.2 1.0 %copy-start.1 = (bf16[512,512]{1,0:T(8,128)(2,1)S(1)}, bf16[512,512]{1,0:T(8,128)(2,1)}, u32[]{:S(2)}) copy-start(bf16[512,512]{1,0:T(8,128)(2,1)} %constant.39.clone.fr) | copy-start | bytes 1572868
  40.2 1.0 %copy-start.3 = (bf16[512,512]{1,0:T(8,128)(2,1)S(1)}, bf16[512,512]{1,0:T(8,128)(2,1)}, u32[]{:S(2)}) copy-start(bf16[512,512]{1,0:T(8,128)(2,1)} %constant.38.clone.fl) | copy-start | bytes 1572868
  41.3 1.0 %copy-start.4 = (bf16[512,512]{1,0:T(8,128)(2,1)S(1)}, bf16[512,512]{1,0:T(8,128)(2,1)}, u32[]{:S(2)}) copy-start(bf16[512,512]{1,0:T(8,128)(2,1)} %get-tuple-element.11.nl) | copy-start | bytes 1572868
  42.3 1.0 %copy-start.5 = (bf16[512,512]{1,0:T(8,128)(2,1)S(1)}, bf16[512,512]{1,0:T(8,128)(2,1)}, u32[]{:S(2)}) copy-start(bf16[512,512]{1,0:T(8,128)(2,1)} %get-tuple-element.12.nr) | copy-start | bytes 1572868
  43.4 0.9 %copy-start.7 = (bf16[2,256,256]{2,1,0:T(8,128)(2,1)S(1)}, bf16[2,256,256]{2,1,0:T(8,128)(2,1)}, u32[]{:S(2)}) copy-start(bf16[2,256,256]{2,1,0:T(8,128)(2,1)} %p.3) | copy-start | bytes 786436
  44.3 4.9 %copy-start.2 = (bf16[512,512]{1,0:T(8,128)(2,1)S(1)}, bf16[512,512]{1,0:T(8,128)(2,1)}, u32[]{:S(2)}) copy-start(bf16[512,512]{1,0:T(8,128)(2,1)} %constant.39.clone.fr) | copy-start | bytes 1572868

commit v2 on v1

v2 whole, which is shorter than its diff:
```python
import math

import jax
import jax.numpy as jnp
import numpy as np
from jax import lax
from jax.experimental import pallas as pl
from jax.experimental.pallas import tpu as pltpu
from jax.sharding import PartitionSpec as P

BF = jnp.bfloat16
F32 = jnp.float32
VM = pl.BlockSpec(memory_space=pltpu.VMEM)
SM = pl.BlockSpec(memory_space=pltpu.SMEM)
MIB = 1024 * 1024
CODE_ROWS = 16
TINY = pl.CostEstimate(flops=1000, bytes_accessed=1000, transcendentals=0)


def mm(a, b):
    return jnp.dot(a, b, preferred_element_type=F32)


def in_top():
    return lax.axis_index("sec") == 0


def owned(which_set):
    return lax.axis_index("tile") % 2 == which_set


def message_kernel(row_ref, col_ref, count_ref, ints_ref, strip_ref, out, second):
    second[...] = strip_ref[1:2]
    slots, size, n = out.shape
    half = size - CODE_ROWS
    start = pl.multiple_of(lax.axis_index("sec") * half, half)
    out[:, :half, :] = ints_ref[:, pl.ds(start, half), :]
    at_row = lax.broadcasted_iota(jnp.int32, (CODE_ROWS, n), 0)
    values = [row_ref[w] for w in range(slots)] + [col_ref[w] for w in range(slots)]
    codes = jnp.zeros((CODE_ROWS, n), F32)
    for k, value in enumerate(values + [count_ref[0]]):
        codes = jnp.where(at_row == k, value.astype(F32), codes)
    for w in range(slots):
        out[w, half:, :] = codes.astype(BF)


def place_waves(corners, live, own, probe_ref, own_here, own_there, marks, rolled, seen):
    n = probe_ref.shape[1]
    rows = lax.broadcasted_iota(jnp.int32, (n, n), 0)
    cols = lax.broadcasted_iota(jnp.int32, (n, n), 1)
    at_row = lax.broadcasted_iota(jnp.int32, (8, n), 0)
    top = in_top()
    for w, (r, c) in enumerate(corners):
        weight = jnp.where(w < live, 2, 0)
        signed = r if own else -r
        marks[w] = jnp.where(at_row == 0, signed, jnp.where(at_row == 1, c, weight))
        mine, left = (rows >= r) if own else (rows < r), cols >= c
        for part in range(2):
            plane = pltpu.roll(probe_ref[part].astype(F32), r, 0)
            rolled[w, part] = pltpu.roll(plane, c, 1).astype(BF)

            def choose(ref):
                plane = ref[part, 0].astype(F32)
                both = jnp.where(left, plane[:, :n], plane[:, n:])
                return jnp.where(mine, both, 0.0).astype(BF)

            here, there = choose(own_here), choose(own_there)

            @pl.when(top)
            def _():
                seen[w, 0, part] = here
                seen[w, 1, part] = there

            @pl.when(jnp.logical_not(top))
            def _():
                seen[w, 0, part] = there
                seen[w, 1, part] = here


def own_kernel(
    row_ref, col_ref, count_ref, phase_ref, probe_ref, own_here, own_there,
    near_left, near_right, far_left, far_right, marks, rolled, seen,
):
    n = probe_ref.shape[1]
    slots = rolled.shape[0]
    phase = jnp.broadcast_to(phase_ref[...], (8, n))
    turn = jnp.where(
        lax.broadcasted_iota(jnp.int32, (8, n), 0) == 0, jnp.cos(phase), jnp.sin(phase)
    )

    def exact(a, b):
        return jnp.dot(a, b, precision=lax.Precision.HIGHEST, preferred_element_type=F32)

    product = lax.broadcasted_iota(jnp.int32, (n, n), 0) * lax.broadcasted_iota(
        jnp.int32, (n, n), 1
    )
    angles = lax.rem(product, n).astype(F32) * (2.0 * math.pi / n)
    cosine, sine = jnp.cos(angles), jnp.sin(angles)
    by_cos = exact(turn, cosine)
    by_sin = exact(turn, sine)
    scale = 1.0 / n

    def circulant(row):
        return pltpu.roll(
            jnp.broadcast_to(row * scale, (n, n)), 0, 1, stride=1, stride_axis=0
        ).astype(BF)

    m_re, m_im = circulant(by_cos[0:1] + by_sin[1:2]), circulant(by_cos[1:2] - by_sin[0:1])
    t_re, t_im = circulant(by_cos[0:1] - by_sin[1:2]), circulant(by_cos[1:2] + by_sin[0:1])
    f_re, f_im = (cosine / math.sqrt(n)).astype(BF), (-sine / math.sqrt(n)).astype(BF)

    def fill(table, re, im, low):
        table[:n, :n] = re
        table[n:, n:] = re
        table[:n, n:] = -im if low else im
        table[n:, :n] = im if low else -im

    fill(near_left, m_re, m_im, True)
    fill(near_right, t_re, t_im, False)
    fill(far_left, f_re, f_im, True)
    fill(far_right, f_re, f_im, False)
    corners = [(row_ref[w], col_ref[w]) for w in range(slots)]
    place_waves(
        corners, count_ref[0], True, probe_ref, own_here, own_there, marks, rolled, seen
    )


def past_kernel(received, probe_ref, own_here, own_there, marks, rolled, seen):
    slots, n = rolled.shape[0], rolled.shape[2]
    height = received.shape[1] - CODE_ROWS
    codes = received[0, height:].astype(F32)
    at_row = lax.broadcasted_iota(jnp.int32, codes.shape, 0)

    def decode(k):
        return jnp.max(jnp.where(at_row == k, codes, 0.0)).astype(jnp.int32)

    corners = [(decode(w), decode(slots + w)) for w in range(slots)]
    place_waves(
        corners, decode(2 * slots), False, probe_ref, own_here, own_there, marks, rolled, seen
    )


def propagate(left, right, field, inner, outer):
    n = inner.shape[1] // 2
    count = field.shape[1] // n
    product = mm(left[...], field[...]).astype(BF)
    for w in range(count):
        inner[w * n : (w + 1) * n, :n] = product[:n, w * n : (w + 1) * n]
        inner[w * n : (w + 1) * n, n:] = product[n:, w * n : (w + 1) * n]
    outer[...] = mm(inner[...], right[...])


class Waves:
    def __init__(self, which_set, placed, near, far, field, inner, outer):
        own = owned(which_set)
        self.own, self.near, self.far = own, near, far
        self.slots, _, self.n, _ = placed[1].shape
        n = self.n
        self.placed = placed
        self.field, self.inner, self.outer = field, inner, outer
        flip = jnp.where(own, 0, -1)
        rows = lax.broadcasted_iota(jnp.int32, (n, n), 0) ^ flip
        cols = lax.broadcasted_iota(jnp.int32, (n, n), 1)
        self.marks = [self.pick(0, w) for w in range(self.slots)]
        self.masks = [(rows >= mark[0:1], cols >= mark[1:2]) for mark in self.marks]

    def pick(self, kind, *at):
        return jnp.where(self.own, self.placed[kind][at], self.placed[3 + kind][at])

    def window(self, w, layer, other):
        mine, left = self.masks[w]
        planes = []
        for part in range(2):
            plane = jnp.concatenate([piece[0] for piece in other[part]], axis=0).astype(F32)
            outside = jnp.where(left, plane[:, : self.n], plane[:, self.n :])
            planes.append(jnp.where(mine, self.pick(2, w, layer, part).astype(F32), outside))
        return planes

    def probe(self, w):
        return [self.pick(1, w, part).astype(F32) for part in range(2)]

    def put(self, w, re, im):
        n = self.n
        self.field[:n, w * n : (w + 1) * n] = re.astype(BF)
        self.field[n:, w * n : (w + 1) * n] = im.astype(BF)

    def got(self, w):
        n = self.n
        return self.outer[w * n : (w + 1) * n, :n], self.outer[w * n : (w + 1) * n, n:]

    def forward(self, mats):
        propagate(mats[0], mats[1], self.field, self.inner, self.outer)

    def adjoint(self, mats):
        propagate(mats[1], mats[0], self.field, self.inner, self.outer)

    def enter(self, other, psi):
        for w in range(self.slots):
            t_re, t_im = self.window(w, 0, other)
            p_re, p_im = self.probe(w)
            self.put(w, t_re * p_re - t_im * p_im, t_re * p_im + t_im * p_re)
        self.forward(self.near)
        for w in range(self.slots):
            psi[w] = jnp.stack(self.got(w)).astype(BF)

    def leave(self, other, psi, own_int, int_here, int_there, back):
        for w in range(self.slots):
            t_re, t_im = self.window(w, 1, other)
            p_re, p_im = psi[w, 0].astype(F32), psi[w, 1].astype(F32)
            self.put(w, t_re * p_re - t_im * p_im, t_re * p_im + t_im * p_re)
        self.forward(self.far)
        n = self.n
        top = in_top()
        for w in range(self.slots):
            re, im = self.got(w)
            near, away = int_here[w, : n // 2].astype(F32), int_there[w, : n // 2].astype(F32)
            first, second = jnp.where(top, near, away), jnp.where(top, away, near)
            measured = jnp.where(
                self.own, own_int[w].astype(F32), jnp.concatenate([first, second], axis=0)
            )
            weight = self.marks[w][2:3].astype(F32)
            factor = weight * (re * re + im * im - measured)
            self.put(w, factor * re, factor * im)
        self.adjoint(self.far)
        for w in range(self.slots):
            back[w] = jnp.stack(self.got(w)).astype(BF)

    def reach_first(self, other, back):
        for w in range(self.slots):
            t_re, t_im = self.window(w, 1, other)
            y_re, y_im = back[w, 0].astype(F32), back[w, 1].astype(F32)
            self.put(w, t_re * y_re + t_im * y_im, t_re * y_im - t_im * y_re)
        self.adjoint(self.near)
        for w in range(self.slots):
            back[w] = jnp.stack(self.got(w)).astype(BF)

    def gradient(self, entering, back, base, out):
        n = self.n
        for part in range(2):
            sums = [0.0, 0.0] if base is None else [base[part, 0, :, :n], base[part, 0, :, n:]]
            for w in range(self.slots):
                mine, left = self.masks[w]
                a_re, a_im = entering(w)
                y_re, y_im = back[w, 0].astype(F32), back[w, 1].astype(F32)
                value = a_re * y_re + a_im * y_im if part == 0 else a_re * y_im - a_im * y_re
                value = jnp.where(mine, value, 0.0)
                sums[0] = sums[0] + jnp.where(left, value, 0.0)
                sums[1] = sums[1] + jnp.where(left, 0.0, value)
            out[part, 0, :, :n] = sums[0]
            out[part, 0, :, n:] = sums[1]


def facing_kernel(
    here_re, here_im, there_re0, there_re1, there_im0, there_im1, own_int, int_here, int_there, nl, nr, fl, fr, m0, r0, s0, m1, r1, s1,
    out, field, inner, outer, psi, back,
):
    waves = Waves(0, (m0, r0, s0, m1, r1, s1), (nl, nr), (fl, fr), field, inner, outer)
    top = in_top()
    ints = (own_int, int_here, int_there)
    here = [[here_re.at[0]], [here_im.at[0]]]
    there = [[there_re0.at[0], there_re1.at[0]], [there_im0.at[0], there_im1.at[0]]]

    @pl.when(top)
    def _():
        waves.enter(here, psi)
        waves.leave(there, psi, *ints, back)
        waves.reach_first(there, back)
        waves.gradient(waves.probe, back, None, out)

    @pl.when(jnp.logical_not(top))
    def _():
        waves.enter(there, psi)
        waves.leave(here, psi, *ints, back)
        waves.gradient(lambda w: psi[w].astype(F32), back, None, out)


def entering_kernel(here_re, here_im, nl, nr, m0, r0, s0, m1, r1, s1, psi, field, inner, outer):
    @pl.when(in_top())
    def _():
        waves = Waves(1, (m0, r0, s0, m1, r1, s1), (nl, nr), None, field, inner, outer)
        waves.enter([[here_re.at[0]], [here_im.at[0]]], psi)


def opposite_kernel(
    here_re, here_im, there_re, there_im, own_int, int_here, int_there, nl, nr, fl, fr, m0, r0, s0, m1, r1, s1,
    entered, base, out, field, inner, outer, psi, back,
):
    waves = Waves(1, (m0, r0, s0, m1, r1, s1), (nl, nr), (fl, fr), field, inner, outer)
    ints = (own_int, int_here, int_there)
    here, there = [[here_re.at[0]], [here_im.at[0]]], [[there_re.at[0]], [there_im.at[0]]]
    top = in_top()

    @pl.when(top)
    def _():
        waves.leave(there, entered, *ints, back)
        waves.reach_first(there, back)
        waves.gradient(waves.probe, back, base, out)

    @pl.when(jnp.logical_not(top))
    def _():
        waves.enter(there, psi)
        waves.leave(here, psi, *ints, back)
        waves.gradient(lambda w: psi[w].astype(F32), back, base, out)


def kernel_call(kernel, name, out_shape, in_specs, scratch_shapes=()):
    many = isinstance(out_shape, tuple)
    return pl.pallas_call(
        kernel,
        out_shape=out_shape,
        in_specs=in_specs,
        out_specs=(VM,) * len(out_shape) if many else VM,
        scratch_shapes=scratch_shapes,
        compiler_params=pltpu.CompilerParams(vmem_limit_bytes=16 * MIB),
        cost_estimate=TINY,
        name=name,
    )


def on_device(obj, probe, phases, intensities, pos_row, pos_col, counts):
    n = probe.shape[1]
    slots = pos_row.shape[0]
    tiles = lax.axis_size("tile")
    half = intensities.shape[1] // lax.axis_size("sec")
    after = lax.optimization_barrier

    def swap(value):
        return lax.ppermute(value, "sec", [(0, 1), (1, 0)])

    def send(value, pairs):
        return lax.ppermute(value, "tile", [(a, b) for a, b in pairs if 0 <= b < tiles])

    onward = [(i, i + 1) for i in range(tiles)]
    paired = [(i, i ^ 1) for i in range(tiles)]
    across = [(i, i + 1 if i % 2 else i - 1) for i in range(tiles)]
    relayed = [(i, i - 2 if i % 2 else i + 2) for i in range(tiles)]

    facing_re = send(obj[0:1], paired)
    own_there = swap(obj)
    positions = (pos_row, pos_col, counts)
    cut = (1, *obj.shape[1:])
    message, second = kernel_call(
        message_kernel,
        "message",
        (
            jax.ShapeDtypeStruct((slots, half + CODE_ROWS, n), BF),
            jax.ShapeDtypeStruct(cut, BF),
        ),
        [SM] * 3 + [VM] * 2,
    )(*positions, intensities, obj)
    facing_im = send(second, paired)
    int_here = send(message, onward)
    opposite_re = send(facing_re, relayed)
    direct, _ = after((second, facing_re))
    opposite_im = send(direct, across)
    phases, _ = after((phases, facing_re))

    double = jax.ShapeDtypeStruct((2 * n, 2 * n), BF)
    wave_shapes = (
        jax.ShapeDtypeStruct((slots, 8, n), jnp.int32),
        jax.ShapeDtypeStruct((slots, 2, n, n), BF),
        jax.ShapeDtypeStruct((slots, 2, 2, n, n), BF),
    )
    nl, nr, fl, fr, *own_waves = kernel_call(
        own_kernel, "own", (double,) * 4 + wave_shapes, [SM] * 3 + [VM] * 4
    )(*positions, phases[None], probe, obj, own_there)
    int_here, nl = after((int_here, nl))
    int_there = swap(int_here)
    past_waves = kernel_call(past_kernel, "past", wave_shapes, [VM] * 4)(
        int_here, probe, obj, own_there
    )
    placed = (*own_waves, *past_waves)

    work = [
        pltpu.VMEM((2 * n, slots * n), BF),
        pltpu.VMEM((slots * n, 2 * n), BF),
        pltpu.VMEM((slots * n, 2 * n), F32),
    ]
    def pieces(value):
        middle = value.shape[2] // 2
        return swap(value[:, :, :middle]), swap(value[:, :, middle:])

    pair = pltpu.VMEM((slots, 2, n, n), BF)
    own_ints, opposite_re = after((intensities, opposite_re))
    ints = (own_ints, int_here, int_there)
    grad_shape = jax.ShapeDtypeStruct(obj.shape, F32)
    partial = kernel_call(
        facing_kernel, "facing", grad_shape, [VM] * 19, work + [pair, pair]
    )(facing_re, facing_im, *pieces(facing_re), *pieces(facing_im), *ints, nl, nr, fl, fr, *placed)
    opposite_re, opposite_im, partial = after((opposite_re, opposite_im, partial))
    opposite = (opposite_re, opposite_im)
    opposite_there = (swap(opposite_re), swap(opposite_im))
    entered = kernel_call(
        entering_kernel, "entering", jax.ShapeDtypeStruct((slots, 2, n, n), BF), [VM] * 10, work
    )(*opposite, nl, nr, *placed)
    return kernel_call(
        opposite_kernel, "opposite", grad_shape, [VM] * 19, work + [pair, pair]
    )(*opposite, *opposite_there, *ints, nl, nr, fl, fr, *placed, entered, partial)


def solution(mesh):
    placed = (
        P(None, "sec", "tile", None),
        P(),
        P(),
        P("tile", None, None),
        P("tile"),
        P("tile"),
        P("tile"),
    )
    return jax.shard_map(
        on_device,
        mesh=mesh,
        in_specs=placed,
        out_specs=P(None, "sec", "tile", None),
        check_vma=False,
    )
```

time: 55.7 us -> 36.3 us (0.65)
  waiting for transfers between devices: 17.9 us -> 3.1 us
  local copies, waits for them, and re-layouts: 6.69 us -> 2.23 us
    ppermute x4 -> x5, waiting for transfers between devices: 17.9 us -> 2.72 us  [send(): lax.ppermute(value, 'tile', [(a, b) for a, b in pairs if 0 <= b < tiles])]
    unnamed x20 -> x12, local copies, waits for them, and re-layouts: 5.13 us -> 1.16 us
    ppermute x4 -> x5, starting transfers between devices: 16.1 us -> 14.2 us  [send(): lax.ppermute(value, 'tile', [(a, b) for a, b in pairs if 0 <= b < tiles])]
    ppermute x4 -> x8, starting transfers between devices: 0.1 us -> 1.78 us  [swap(): return lax.ppermute(value, 'sec', [(0, 1), (1, 0)])]
    dynamic_slice x1 -> x0, local copies, waits for them, and re-layouts: 1.56 us -> none  [on_device(): lax.dynamic_slice_in_dim(intensities, sec * half, half, 1)]
    slice x0 -> x3, local copies, waits for them, and re-layouts: none -> 1.07 us  [the longest x1 1.04 us: on_device(): facing_re = send(obj[0:1], paired)]
    pallas_call x3 -> x6, Pallas kernels: 13.4 us -> 13.6 us  [the longest x1 3.83 us: on_device(): kernel_call(opposite_kernel, 'opposite', grad_shape, [VM] * 19, work + [p...]
  transfers between devices with their start and end apart: 8 -> 13, of which waited for: 3 -> 3; matrix products, arithmetic and copies ran while one was open for 3% -> 3% of each run, Pallas kernels for 13% -> 27%
where the time goes in v2:
time: 36.3 us; the launch traced here: 35.8 us
  starting transfers between devices  16 us (44%)
  Pallas kernels  13.6 us (37%)
  waiting for transfers between devices  3.1 us (9%)
  local copies, waits for them, and re-layouts  2.23 us (6%)
  between operations  0.89 us (2%)
    ppermute x5, starting transfers between devices, send(): lax.ppermute(value, 'tile', [(a, b) for a, b in pairs if 0 <= b < tiles])  14.2 us
    pallas_call x1, Pallas kernels, on_device(): kernel_call(opposite_kernel, 'opposite', grad_shape, [VM] * 19, work + [p...  3.83 us
    pallas_call x1, Pallas kernels, on_device(): kernel_call(facing_kernel, 'facing', grad_shape, [VM] * 19, work + [pair,...  3.73 us
    pallas_call x1, Pallas kernels, on_device(): kernel_call(own_kernel, 'own', (double,) * 4 + wave_shapes, [SM] * 3 + [V...  3.2 us
    ppermute x5, waiting for transfers between devices, send(): lax.ppermute(value, 'tile', [(a, b) for a, b in pairs if 0 <= b < tiles])  2.72 us
    ppermute x8, starting transfers between devices, swap(): return lax.ppermute(value, 'sec', [(0, 1), (1, 0)])  1.78 us
    pallas_call x1, Pallas kernels, on_device(): kernel_call(past_kernel, 'past', wave_shapes, [VM] * 4)  1.29 us
    unnamed x12, local copies, waits for them, and re-layouts  1.16 us
  transfers between devices with their start and end apart: 13, of which 3 were waited for; matrix products, arithmetic and copies ran while one was open for 3% of the time, Pallas kernels for 27%

profile of v2, /device:TPU:24, one launch (start us, length us, event | category | flops | bytes accessed | tf_op | source)
XLA Modules:
  0.0 35.8 jit_solution(12256860431471450180)
XLA Ops:
  0.0 0.0 copy-start
  0.0 0.0 collective-permute-start.9
  0.0 1.0 %slice.15 = bf16[1,1,256,512]{3,2,1,0:T(8,128)(2,1)S(1)} slice(bf16[2,1,256,512]{3,2,1,0:T(8,128)(2,1)} %own_here.3), slice={[0:1], [0:1], [0:256], [0:512]} | slice | bytes 524288 | tf_op jit(solution)/shard_map/slice | solution.py:338
  1.0 0.0 copy-start.3
  1.1 0.0 copy-start.4
  1.1 1.6 %collective-permute-start = (bf16[1,1,256,512]{3,2,1,0:T(8,128)(2,1)S(1)}, bf16[1,1,256,512]{3,2,1,0:T(8,128)(2,1)S(1)}, u32[]{:S(2)}, u32[]{:S(2)}) collective-permute-start(bf16[1,1,256,512]{3,2,1,0:T(8,128)(2,1)S(1)} %slice.15), channel_id=1, source_target_pairs={{0,1},{1,0},{2,3},{3,2},{4,5},{5,4},{6,7},{7,6},{8,9},{9,8},{10,11... | collective-permute-start | bytes 786440 | tf_op jit(solution)/shard_map/ppermute | solution.py:331
  3.3 0.0 copy-done
  3.3 0.0 copy-done.3
  3.3 0.0 copy-done.4
  3.3 0.0 copy-start.1
  3.3 0.9 %copy-done.1 = bf16[2,256,256]{2,1,0:T(8,128)(2,1)S(1)} copy-done((bf16[2,256,256]{2,1,0:T(8,128)(2,1)S(1)}, bf16[2,256,256]{2,1,0:T(8,128)(2,1)}, u32[]{:S(2)}) %copy-start.1) | copy-done | bytes 262168
  4.3 0.6 %message.1 = (bf16[2,144,256]{2,1,0:T(8,128)(2,1)S(1)}, bf16[1,1,256,512]{3,2,1,0:T(8,128)(2,1)S(1)}) custom-call(s32[2]{0:T(128)S(1)} %copy-done.3, s32[2]{0:T(128)S(1)} %copy-done.4, s32[1]{0:T(128)S(6)} %copy.8.count_ref, bf16[2,256,256]{2,1,0:T(8,128)(2,1)S(1)} %copy-done.1, bf16[2,1,256,512]{3,2,1,0:T(8,128)(2,1)S(1)} %copy-done), custom_call_target="tpu_custom_call" | custom-call | flops 1000 | bytes 1000 | tf_op jit(solution)/shard_map/message/pallas_call | solution.py:342
  4.8 0.6 %collective-permute-start.3 = (bf16[1,1,256,512]{3,2,1,0:T(8,128)(2,1)S(1)}, bf16[1,1,256,512]{3,2,1,0:T(8,128)(2,1)S(1)}, u32[]{:S(2)}, u32[]{:S(2)}) collective-permute-start(bf16[1,1,256,512]{3,2,1,0:T(8,128)(2,1)S(1)} %get-tuple-element.28), channel_id=1, source_target_pairs={{0,1},{1,0},{2,3},{3,2},{4,5},{5,4},{6,7},{7,6},{8,9},{9,8},{10,11... | collective-permute-start | bytes 786440 | tf_op jit(solution)/shard_map/ppermute | solution.py:331
  5.4 0.0 copy-start.2
  5.4 3.5 %collective-permute-start.8 = (bf16[2,144,256]{2,1,0:T(8,128)(2,1)S(1)}, bf16[2,144,256]{2,1,0:T(8,128)(2,1)S(1)}, u32[]{:S(2)}, u32[]{:S(2)}) collective-permute-start(bf16[2,144,256]{2,1,0:T(8,128)(2,1)S(1)} %get-tuple-element.30), channel_id=1, source_target_pairs={{0,1},{1,2},{2,3},{3,4},{4,5},{5,6},{6,7},{7,8},{8,9},{9,10},{10,1... | collective-permute-start | bytes 442376 | tf_op jit(solution)/shard_map/ppermute | solution.py:331
  9.0 1.3 %collective-permute-done.here_re = bf16[1,1,256,512]{3,2,1,0:T(8,128)(2,1)S(1)} collective-permute-done((bf16[1,1,256,512]{3,2,1,0:T(8,128)(2,1)S(1)}, bf16[1,1,256,512]{3,2,1,0:T(8,128)(2,1)S(1)}, u32[]{:S(2)}, u32[]{:S(2)}) %collective-permute-start) | collective-permute-done | bytes 262176 | tf_op jit(solution)/shard_map/ppermute | solution.py:331
  10.2 3.4 %collective-permute-start.1 = (bf16[1,1,256,512]{3,2,1,0:T(8,128)(2,1)S(1)}, bf16[1,1,256,512]{3,2,1,0:T(8,128)(2,1)S(1)}, u32[]{:S(2)}, u32[]{:S(2)}) collective-permute-start(bf16[1,1,256,512]{3,2,1,0:T(8,128)(2,1)S(1)} %collective-permute-done.here_re), channel_id=1, source_target_pairs={{0,2},{2,4},{3,1},{4,6},{5,3},{6,8},{7,5},{8,10},{9,7},{10,12},{11... | collective-permute-start | bytes 786440 | tf_op jit(solution)/shard_map/ppermute | solution.py:331
  13.7 0.1 collective-permute-start.5
  13.8 0.0 collective-permute-done.9.own_there
  13.8 0.0 copy-start.5
  13.8 0.5 %collective-permute-start.4 = (bf16[1,1,128,512]{3,2,1,0:T(8,128)(2,1)S(1)}, bf16[1,1,128,512]{3,2,1,0:T(8,128)(2,1)S(1)}, u32[]{:S(2)}, u32[]{:S(2)}) collective-permute-start(bf16[1,1,128,512]{3,2,1,0:T(8,128)(2,1)S(1)} %get-tuple-element.50), channel_id=1, source_target_pairs={{0,16},{16,0},{1,17},{17,1},{2,18},{18,2},{3,19},{19,3},{4,20},{20... | collective-permute-start | bytes 393224 | tf_op jit(solution)/shard_map/ppermute | solution.py:328
  14.3 0.0 copy-done.2
  14.3 0.2 copy-done.5
  14.5 3.2 %own.1 = (bf16[512,512]{1,0:T(8,128)(2,1)S(1)}, bf16[512,512]{1,0:T(8,128)(2,1)S(1)}, bf16[512,512]{1,0:T(8,128)(2,1)S(1)}, bf16[512,512]{1,0:T(8,128)(2,1)S(1)}...) custom-call(s32[2]{0:T(128)S(1)} %copy-done.3, ...), custom_call_target="tpu_custom_call" | custom-call | flops 1000 | bytes 1000 | tf_op jit(solution)/shard_map/own/pallas_call | solution.py:364
  17.7 0.0 collective-permute-done.8.received.int_here
  17.7 5.1 %collective-permute-start.2 = (bf16[1,1,256,512]{3,2,1,0:T(8,128)(2,1)S(1)}, bf16[1,1,256,512]{3,2,1,0:T(8,128)(2,1)S(1)}, u32[]{:S(2)}, u32[]{:S(2)}) collective-permute-start(bf16[1,1,256,512]{3,2,1,0:T(8,128)(2,1)S(1)} %get-tuple-element.28), channel_id=1, source_target_pairs={{1,2},{2,1},{3,4},{4,3},{5,6},{6,5},{7,8},{8,7},{9,10},{10,9},{11,... | collective-permute-start | bytes 786440 | tf_op jit(solution)/shard_map/ppermute | solution.py:331
  22.8 0.0 collective-permute-done.3.here_im
  22.8 0.1 collective-permute-start.10
  22.9 0.0 collective-permute-done.5.there_re1
  22.9 0.6 %collective-permute-start.7 = (bf16[1,1,128,512]{3,2,1,0:T(8,128)(2,1)S(1)}, bf16[1,1,128,512]{3,2,1,0:T(8,128)(2,1)S(1)}, u32[]{:S(2)}, u32[]{:S(2)}) collective-permute-start(bf16[1,1,128,512]{3,2,1,0:T(8,128)(2,1)S(1)} %get-tuple-element.47), channel_id=1, source_target_pairs={{0,16},{16,0},{1,17},{17,1},{2,18},{18,2},{3,19},{19,3},{4,20},{20... | collective-permute-start | bytes 393224 | tf_op jit(solution)/shard_map/ppermute | solution.py:328
  23.5 0.0 collective-permute-done.1.here_re
  23.5 0.1 collective-permute-start.6
  23.6 1.3 %past.1 = (s32[2,8,256]{2,1,0:T(8,128)S(1)}, bf16[2,2,256,256]{3,2,1,0:T(8,128)(2,1)S(1)}, bf16[2,2,2,256,256]{4,3,2,1,0:T(8,128)(2,1)S(1)}) custom-call(bf16[2,144,256]{2,1,0:T(8,128)(2,1)S(1)} %collective-permute-done.8.received.int_here, bf16[2,256,256]{2,1,0:T(8,128)(2,1)S(1)} %copy-done.2, bf16[2,1,256,512]{3,2,1,0:T(8,128)(2,1)S(1)} %copy-done, ...), custom_call_target="tpu_custom_call" | custom-call | flops 1000 | bytes 1000 | tf_op jit(solution)/shard_map/past/pallas_call | solution.py:369
  24.9 0.0 collective-permute-done.4.there_re0
  24.9 0.0 collective-permute-done.7.there_im1
  24.9 0.0 collective-permute-done.6.there_im0
  24.9 0.0 collective-permute-done.10.int_there
  24.9 3.7 %facing.1.base = f32[2,1,256,512]{3,2,1,0:T(8,128)S(1)} custom-call(bf16[1,1,256,512]{3,2,1,0:T(8,128)(2,1)S(1)} %collective-permute-done.here_re, bf16[1,1,256,512]{3,2,1,0:T(8,128)(2,1)S(1)} %collective-permute-done.3.here_im, bf16[1,1,128,512]{3,2,1,0:T(8,128)(2,1)S(1)} %collective-permute-done.4.there_re0, ...), custom_call_target="tpu_custom_call" | custom-call | flops 1000 | bytes 1000 | tf_op jit(solution)/shard_map/facing/pallas_call | solution.py:387
  28.7 1.4 %collective-permute-done.2.here_im = bf16[1,1,256,512]{3,2,1,0:T(8,128)(2,1)S(1)} collective-permute-done((bf16[1,1,256,512]{3,2,1,0:T(8,128)(2,1)S(1)}, bf16[1,1,256,512]{3,2,1,0:T(8,128)(2,1)S(1)}, u32[]{:S(2)}, u32[]{:S(2)}) %collective-permute-start.2) | collective-permute-done | bytes 262176 | tf_op jit(solution)/shard_map/ppermute | solution.py:331
  30.1 0.0 collective-permute-start.11
  30.1 0.5 %collective-permute-start.12 = (bf16[1,1,256,512]{3,2,1,0:T(8,128)(2,1)S(1)}, bf16[1,1,256,512]{3,2,1,0:T(8,128)(2,1)S(1)}, u32[]{:S(2)}, u32[]{:S(2)}) collective-permute-start(bf16[1,1,256,512]{3,2,1,0:T(8,128)(2,1)S(1)} %collective-permute-done.2.here_im), channel_id=1, source_target_pairs={{0,16},{16,0},{1,17},{17,1},{2,18},{18,2},{3,19},{19,3},{4,20},{20... | collective-permute-start | bytes 786440 | tf_op jit(solution)/shard_map/ppermute | solution.py:328
  30.6 1.0 %entering.1.entered = bf16[2,2,256,256]{3,2,1,0:T(8,128)(2,1)S(1)} custom-call(bf16[1,1,256,512]{3,2,1,0:T(8,128)(2,1)S(1)} %collective-permute-done.1.here_re, bf16[1,1,256,512]{3,2,1,0:T(8,128)(2,1)S(1)} %collective-permute-done.2.here_im, bf16[512,512]{1,0:T(8,128)(2,1)S(1)} %get-tuple-element.34.nl, bf16[512,512]{1,0:T(8,128)(2,1)S(1)} %get-tuple-element.35.nr, ...), custom_call_target="tpu_custom_call" | custom-call | flops 1000 | bytes 1000 | tf_op jit(solution)/shard_map/entering/pallas_call | solution.py:393
  31.6 0.0 collective-permute-done.11.there_re
  31.6 0.4 %collective-permute-done.12.there_im = bf16[1,1,256,512]{3,2,1,0:T(8,128)(2,1)S(1)} collective-permute-done((bf16[1,1,256,512]{3,2,1,0:T(8,128)(2,1)S(1)}, bf16[1,1,256,512]{3,2,1,0:T(8,128)(2,1)S(1)}, u32[]{:S(2)}, u32[]{:S(2)}) %collective-permute-start.12) | collective-permute-done | bytes 262176 | tf_op jit(solution)/shard_map/ppermute | solution.py:328
  32.0 3.8 %opposite.1 = f32[2,1,256,512]{3,2,1,0:T(8,128)} custom-call(bf16[1,1,256,512]{3,2,1,0:T(8,128)(2,1)S(1)} %collective-permute-done.1.here_re, bf16[1,1,256,512]{3,2,1,0:T(8,128)(2,1)S(1)} %collective-permute-done.2.here_im, bf16[1,1,256,512]{3,2,1,0:T(8,128)(2,1)S(1)} %collective-permute-done.11.there_re, ...), custom_call_target="tpu_custom_call" | custom-call | flops 1000 | bytes 1000 | tf_op jit(solution)/shard_map/opposite/pallas_call | solution.py:396
  (2 shorter events, 0.0 us)
Async XLA Ops:
  0.0 3.3 %copy-start = (bf16[2,1,256,512]{3,2,1,0:T(8,128)(2,1)S(1)}, bf16[2,1,256,512]{3,2,1,0:T(8,128)(2,1)}, u32[]{:S(2)}) copy-start(bf16[2,1,256,512]{3,2,1,0:T(8,128)(2,1)} %own_here.3) | copy-start | bytes 1572868
  0.0 13.8 %collective-permute-start.9 = (bf16[2,1,256,512]{3,2,1,0:T(8,128)(2,1)}, bf16[2,1,256,512]{3,2,1,0:T(8,128)(2,1)S(1)}, u32[]{:S(2)}, u32[]{:S(2)}) collective-permute-start(bf16[2,1,256,512]{3,2,1,0:T(8,128)(2,1)} %own_here.3), channel_id=1, source_target_pairs={{0,16},{16,0},{1,17},{17,1},{2,18},{18,2},{3,19},{19,3},{4,20},{20... | collective-permute-start | bytes 1572872 | tf_op jit(solution)/shard_map/ppermute | solution.py:328
  1.0 2.2 %copy-start.3 = (s32[2]{0:T(128)S(1)}, s32[2]{0:T(128)}, u32[]{:S(2)}) copy-start(s32[2]{0:T(128)} %row_ref.3) | copy-start | bytes 28
  1.1 2.2 %copy-start.4 = (s32[2]{0:T(128)S(1)}, s32[2]{0:T(128)}, u32[]{:S(2)}) copy-start(s32[2]{0:T(128)} %col_ref.3) | copy-start | bytes 28
  1.1 9.2 %collective-permute-start = (bf16[1,1,256,512]{3,2,1,0:T(8,128)(2,1)S(1)}, bf16[1,1,256,512]{3,2,1,0:T(8,128)(2,1)S(1)}, u32[]{:S(2)}, u32[]{:S(2)}) collective-permute-start(bf16[1,1,256,512]{3,2,1,0:T(8,128)(2,1)S(1)} %slice.15), channel_id=1, source_target_pairs={{0,1},{1,0},{2,3},{3,2},{4,5},{5,4},{6,7},{7,6},{8,9},{9,8},{10,11... | collective-permute-start | bytes 786440 | tf_op jit(solution)/shard_map/ppermute | solution.py:331
  3.3 1.0 %copy-start.1 = (bf16[2,256,256]{2,1,0:T(8,128)(2,1)S(1)}, bf16[2,256,256]{2,1,0:T(8,128)(2,1)}, u32[]{:S(2)}) copy-start(bf16[2,256,256]{2,1,0:T(8,128)(2,1)} %own_int.1) | copy-start | bytes 786436
  4.8 18.0 %collective-permute-start.3 = (bf16[1,1,256,512]{3,2,1,0:T(8,128)(2,1)S(1)}, bf16[1,1,256,512]{3,2,1,0:T(8,128)(2,1)S(1)}, u32[]{:S(2)}, u32[]{:S(2)}) collective-permute-start(bf16[1,1,256,512]{3,2,1,0:T(8,128)(2,1)S(1)} %get-tuple-element.28), channel_id=1, source_target_pairs={{0,1},{1,0},{2,3},{3,2},{4,5},{5,4},{6,7},{7,6},{8,9},{9,8},{10,11... | collective-permute-start | bytes 786440 | tf_op jit(solution)/shard_map/ppermute | solution.py:331
  5.4 8.8 %copy-start.2 = (bf16[2,256,256]{2,1,0:T(8,128)(2,1)S(1)}, bf16[2,256,256]{2,1,0:T(8,128)(2,1)}, u32[]{:S(2)}) copy-start(bf16[2,256,256]{2,1,0:T(8,128)(2,1)} %probe_ref.3) | copy-start | bytes 786436
  5.4 12.2 %collective-permute-start.8 = (bf16[2,144,256]{2,1,0:T(8,128)(2,1)S(1)}, bf16[2,144,256]{2,1,0:T(8,128)(2,1)S(1)}, u32[]{:S(2)}, u32[]{:S(2)}) collective-permute-start(bf16[2,144,256]{2,1,0:T(8,128)(2,1)S(1)} %get-tuple-element.30), channel_id=1, source_target_pairs={{0,1},{1,2},{2,3},{3,4},{4,5},{5,6},{6,7},{7,8},{8,9},{9,10},{10,1... | collective-permute-start | bytes 442376 | tf_op jit(solution)/shard_map/ppermute | solution.py:331
  10.2 13.2 %collective-permute-start.1 = (bf16[1,1,256,512]{3,2,1,0:T(8,128)(2,1)S(1)}, bf16[1,1,256,512]{3,2,1,0:T(8,128)(2,1)S(1)}, u32[]{:S(2)}, u32[]{:S(2)}) collective-permute-start(bf16[1,1,256,512]{3,2,1,0:T(8,128)(2,1)S(1)} %collective-permute-done.here_re), channel_id=1, source_target_pairs={{0,2},{2,4},{3,1},{4,6},{5,3},{6,8},{7,5},{8,10},{9,7},{10,12},{11... | collective-permute-start | bytes 786440 | tf_op jit(solution)/shard_map/ppermute | solution.py:331
  13.7 9.2 %collective-permute-start.5 = (bf16[1,1,128,512]{3,2,1,0:T(8,128)(2,1)S(1)}, bf16[1,1,128,512]{3,2,1,0:T(8,128)(2,1)S(1)}, u32[]{:S(2)}, u32[]{:S(2)}) collective-permute-start(bf16[1,1,128,512]{3,2,1,0:T(8,128)(2,1)S(1)} %get-tuple-element.49), channel_id=1, source_target_pairs={{0,16},{16,0},{1,17},{17,1},{2,18},{18,2},{3,19},{19,3},{4,20},{20... | collective-permute-start | bytes 393224 | tf_op jit(solution)/shard_map/ppermute | solution.py:328
  13.8 0.7 %copy-start.5 = (f32[256]{0:T(256)S(1)}, f32[256]{0:T(256)}, u32[]{:S(2)}) copy-start(f32[256]{0:T(256)} %param.9) | copy-start | bytes 3076
  13.8 11.1 %collective-permute-start.4 = (bf16[1,1,128,512]{3,2,1,0:T(8,128)(2,1)S(1)}, bf16[1,1,128,512]{3,2,1,0:T(8,128)(2,1)S(1)}, u32[]{:S(2)}, u32[]{:S(2)}) collective-permute-start(bf16[1,1,128,512]{3,2,1,0:T(8,128)(2,1)S(1)} %get-tuple-element.50), channel_id=1, source_target_pairs={{0,16},{16,0},{1,17},{17,1},{2,18},{18,2},{3,19},{19,3},{4,20},{20... | collective-permute-start | bytes 393224 | tf_op jit(solution)/shard_map/ppermute | solution.py:328
  17.7 12.4 %collective-permute-start.2 = (bf16[1,1,256,512]{3,2,1,0:T(8,128)(2,1)S(1)}, bf16[1,1,256,512]{3,2,1,0:T(8,128)(2,1)S(1)}, u32[]{:S(2)}, u32[]{:S(2)}) collective-permute-start(bf16[1,1,256,512]{3,2,1,0:T(8,128)(2,1)S(1)} %get-tuple-element.28), channel_id=1, source_target_pairs={{1,2},{2,1},{3,4},{4,3},{5,6},{6,5},{7,8},{8,7},{9,10},{10,9},{11,... | collective-permute-start | bytes 786440 | tf_op jit(solution)/shard_map/ppermute | solution.py:331
  22.8 2.1 %collective-permute-start.10 = (bf16[2,144,256]{2,1,0:T(8,128)(2,1)S(1)}, bf16[2,144,256]{2,1,0:T(8,128)(2,1)S(1)}, u32[]{:S(2)}, u32[]{:S(2)}) collective-permute-start(bf16[2,144,256]{2,1,0:T(8,128)(2,1)S(1)} %collective-permute-done.8.received.int_here), channel_id=1, source_target_pairs={{0,16},{16,0},{1,17},{17,1},{2,18},{18,2},{3,19},{19,3},{4,20},{20... | collective-permute-start | bytes 442376 | tf_op jit(solution)/shard_map/ppermute | solution.py:328
  22.9 2.0 %collective-permute-start.7 = (bf16[1,1,128,512]{3,2,1,0:T(8,128)(2,1)S(1)}, bf16[1,1,128,512]{3,2,1,0:T(8,128)(2,1)S(1)}, u32[]{:S(2)}, u32[]{:S(2)}) collective-permute-start(bf16[1,1,128,512]{3,2,1,0:T(8,128)(2,1)S(1)} %get-tuple-element.47), channel_id=1, source_target_pairs={{0,16},{16,0},{1,17},{17,1},{2,18},{18,2},{3,19},{19,3},{4,20},{20... | collective-permute-start | bytes 393224 | tf_op jit(solution)/shard_map/ppermute | solution.py:328
  23.5 1.4 %collective-permute-start.6 = (bf16[1,1,128,512]{3,2,1,0:T(8,128)(2,1)S(1)}, bf16[1,1,128,512]{3,2,1,0:T(8,128)(2,1)S(1)}, u32[]{:S(2)}, u32[]{:S(2)}) collective-permute-start(bf16[1,1,128,512]{3,2,1,0:T(8,128)(2,1)S(1)} %get-tuple-element.48), channel_id=1, source_target_pairs={{0,16},{16,0},{1,17},{17,1},{2,18},{18,2},{3,19},{19,3},{4,20},{20... | collective-permute-start | bytes 393224 | tf_op jit(solution)/shard_map/ppermute | solution.py:328
  30.1 1.5 %collective-permute-start.11 = (bf16[1,1,256,512]{3,2,1,0:T(8,128)(2,1)S(1)}, bf16[1,1,256,512]{3,2,1,0:T(8,128)(2,1)S(1)}, u32[]{:S(2)}, u32[]{:S(2)}) collective-permute-start(bf16[1,1,256,512]{3,2,1,0:T(8,128)(2,1)S(1)} %collective-permute-done.1.here_re), channel_id=1, source_target_pairs={{0,16},{16,0},{1,17},{17,1},{2,18},{18,2},{3,19},{19,3},{4,20},{20... | collective-permute-start | bytes 786440 | tf_op jit(solution)/shard_map/ppermute | solution.py:328
  30.1 1.9 %collective-permute-start.12 = (bf16[1,1,256,512]{3,2,1,0:T(8,128)(2,1)S(1)}, bf16[1,1,256,512]{3,2,1,0:T(8,128)(2,1)S(1)}, u32[]{:S(2)}, u32[]{:S(2)}) collective-permute-start(bf16[1,1,256,512]{3,2,1,0:T(8,128)(2,1)S(1)} %collective-permute-done.2.here_im), channel_id=1, source_target_pairs={{0,16},{16,0},{1,17},{17,1},{2,18},{18,2},{3,19},{19,3},{4,20},{20... | collective-permute-start | bytes 786440 | tf_op jit(solution)/shard_map/ppermute | solution.py:328

commit v3 on v2

v3 whole, which is shorter than its diff:
```python
import math

import jax
import jax.numpy as jnp
import numpy as np
from jax import lax
from jax.experimental import pallas as pl
from jax.experimental.pallas import tpu as pltpu
from jax.sharding import PartitionSpec as P

BF = jnp.bfloat16
F32 = jnp.float32
VM = pl.BlockSpec(memory_space=pltpu.VMEM)
SM = pl.BlockSpec(memory_space=pltpu.SMEM)
MIB = 1024 * 1024
CODE_ROWS = 16
STEP = 32
SENT = 64
TINY = pl.CostEstimate(flops=1000, bytes_accessed=1000, transcendentals=0)


def mm(a, b):
    return jnp.dot(a, b, preferred_element_type=F32)


def in_top():
    return lax.axis_index("sec") == 0


def owned(which_set):
    return lax.axis_index("tile") % 2 == which_set


def message_kernel(row_ref, col_ref, count_ref, ints_ref, strip_ref, out, second):
    second[...] = strip_ref[1:2]
    slots, size, n = out.shape
    half = size - CODE_ROWS
    start = pl.multiple_of(lax.axis_index("sec") * half, half)
    out[:, :half, :] = ints_ref[:, pl.ds(start, half), :]
    at_row = lax.broadcasted_iota(jnp.int32, (CODE_ROWS, n), 0)
    values = [row_ref[w] for w in range(slots)] + [col_ref[w] for w in range(slots)]
    codes = jnp.zeros((CODE_ROWS, n), F32)
    for k, value in enumerate(values + [count_ref[0]]):
        codes = jnp.where(at_row == k, value.astype(F32), codes)
    for w in range(slots):
        out[w, half:, :] = codes.astype(BF)


def place_waves(corners, live, own, probe_ref, own_here, own_there, marks, rolled, seen):
    n = probe_ref.shape[1]
    rows = lax.broadcasted_iota(jnp.int32, (n, n), 0)
    cols = lax.broadcasted_iota(jnp.int32, (n, n), 1)
    at_row = lax.broadcasted_iota(jnp.int32, (8, n), 0)
    top = in_top()
    for w, (r, c) in enumerate(corners):
        weight = jnp.where(w < live, 2, 0)
        signed = r if own else -r
        marks[w] = jnp.where(at_row == 0, signed, jnp.where(at_row == 1, c, weight))
        mine, left = (rows >= r) if own else (rows < r), cols >= c
        for part in range(2):
            plane = pltpu.roll(probe_ref[part].astype(F32), r, 0)
            rolled[w, part] = pltpu.roll(plane, c, 1).astype(BF)

            def choose(ref):
                plane = ref[part, 0].astype(F32)
                both = jnp.where(left, plane[:, :n], plane[:, n:])
                return jnp.where(mine, both, 0.0).astype(BF)

            here, there = choose(own_here), choose(own_there)

            @pl.when(top)
            def _():
                seen[w, 0, part] = here
                seen[w, 1, part] = there

            @pl.when(jnp.logical_not(top))
            def _():
                seen[w, 0, part] = there
                seen[w, 1, part] = here


def own_kernel(
    row_ref, col_ref, count_ref, phase_ref, probe_ref, own_here, own_there,
    near_left, near_right, far_left, far_right, marks, rolled, seen,
):
    n = probe_ref.shape[1]
    slots = rolled.shape[0]
    phase = jnp.broadcast_to(phase_ref[...], (8, n))
    turn = jnp.where(
        lax.broadcasted_iota(jnp.int32, (8, n), 0) == 0, jnp.cos(phase), jnp.sin(phase)
    )

    def exact(a, b):
        return jnp.dot(a, b, precision=lax.Precision.HIGHEST, preferred_element_type=F32)

    product = lax.broadcasted_iota(jnp.int32, (n, n), 0) * lax.broadcasted_iota(
        jnp.int32, (n, n), 1
    )
    angles = lax.rem(product, n).astype(F32) * (2.0 * math.pi / n)
    cosine, sine = jnp.cos(angles), jnp.sin(angles)
    by_cos = exact(turn, cosine)
    by_sin = exact(turn, sine)
    scale = 1.0 / n

    def circulant(row):
        return pltpu.roll(
            jnp.broadcast_to(row * scale, (n, n)), 0, 1, stride=1, stride_axis=0
        ).astype(BF)

    m_re, m_im = circulant(by_cos[0:1] + by_sin[1:2]), circulant(by_cos[1:2] - by_sin[0:1])
    t_re, t_im = circulant(by_cos[0:1] - by_sin[1:2]), circulant(by_cos[1:2] + by_sin[0:1])
    f_re, f_im = (cosine / math.sqrt(n)).astype(BF), (-sine / math.sqrt(n)).astype(BF)

    def fill(table, re, im, low):
        table[:n, :n] = re
        table[n:, n:] = re
        table[:n, n:] = -im if low else im
        table[n:, :n] = im if low else -im

    fill(near_left, m_re, m_im, True)
    fill(near_right, t_re, t_im, False)
    fill(far_left, f_re, f_im, True)
    fill(far_right, f_re, f_im, False)
    corners = [(row_ref[w], col_ref[w]) for w in range(slots)]
    place_waves(
        corners, count_ref[0], True, probe_ref, own_here, own_there, marks, rolled, seen
    )


def past_kernel(received, probe_ref, own_here, own_there, marks, rolled, seen):
    slots, n = rolled.shape[0], rolled.shape[2]
    height = received.shape[1] - CODE_ROWS
    codes = received[0, height:].astype(F32)
    at_row = lax.broadcasted_iota(jnp.int32, codes.shape, 0)

    def decode(k):
        return jnp.max(jnp.where(at_row == k, codes, 0.0)).astype(jnp.int32)

    corners = [(decode(w), decode(slots + w)) for w in range(slots)]
    place_waves(
        corners, decode(2 * slots), False, probe_ref, own_here, own_there, marks, rolled, seen
    )


class Waves:
    def __init__(self, which_set, placed, near, far, work):
        self.placed, self.near, self.far = placed, near, far
        self.field, self.inner, self.outer, self.last = work
        self.slots, _, self.n, _ = placed[1].shape
        self.own = owned(which_set)
        self.flip = jnp.where(self.own, 0, -1)
        self.marks = [self.pick(0, w) for w in range(self.slots)]
        cols = lax.broadcasted_iota(jnp.int32, (STEP, self.n), 1)
        self.left = [cols >= mark[1:2] for mark in self.marks]

    def pick(self, kind, *at):
        return jnp.where(self.own, self.placed[kind][at], self.placed[3 + kind][at])

    def rows(self):
        return [slice(at, at + STEP) for at in range(0, self.n, STEP)]

    def mine(self, w, at):
        index = lax.broadcasted_iota(jnp.int32, (STEP, self.n), 0) + at.start
        return (index ^ self.flip) >= self.marks[w][0:1]

    def window(self, w, layer, other, at):
        n = self.n
        mine, left = self.mine(w, at), self.left[w]
        planes = []
        for part in range(2):
            pieces = other[part]
            size = n // len(pieces)
            piece, first = pieces[at.start // size], at.start % size
            plane = piece[0, first : first + STEP, :].astype(F32)
            outside = jnp.where(left, plane[:, :n], plane[:, n:])
            inside = self.pick(2, w, layer, part, at).astype(F32)
            planes.append(jnp.where(mine, inside, outside))
        return planes

    def probe(self, w, at):
        return [self.pick(1, w, part, at).astype(F32) for part in range(2)]

    def pair(self, ref, w, at):
        return ref[w, 0, at, :].astype(F32), ref[w, 1, at, :].astype(F32)

    def put(self, w, at, re, im):
        n = self.n
        lower = slice(n + at.start, n + at.stop)
        self.field[at, w * n : (w + 1) * n] = re.astype(BF)
        self.field[lower, w * n : (w + 1) * n] = im.astype(BF)

    def got(self, w, at):
        n = self.n
        here = slice(w * n + at.start, w * n + at.stop)
        return self.outer[here, :n], self.outer[here, n:]

    def propagate(self, left, right):
        n = self.n
        for w in range(self.slots):
            product = mm(left[...], self.field[:, w * n : (w + 1) * n]).astype(BF)
            self.inner[w * n : (w + 1) * n, :n] = product[:n]
            self.inner[w * n : (w + 1) * n, n:] = product[n:]
        for w in range(self.slots):
            here = slice(w * n, (w + 1) * n)
            self.outer[here, :] = mm(self.inner[here, :], right[...])

    def enter(self, other, psi):
        for w in range(self.slots):
            for at in self.rows():
                t_re, t_im = self.window(w, 0, other, at)
                p_re, p_im = self.probe(w, at)
                self.put(w, at, t_re * p_re - t_im * p_im, t_re * p_im + t_im * p_re)
        self.propagate(*self.near)
        for w in range(self.slots):
            for at in self.rows():
                re, im = self.got(w, at)
                psi[w, 0, at, :] = re.astype(BF)
                psi[w, 1, at, :] = im.astype(BF)

    def leave(self, other, psi, own_int, int_here, int_there):
        for w in range(self.slots):
            for at in self.rows():
                t_re, t_im = self.window(w, 1, other, at)
                self.last[w, 0, at, :] = t_re.astype(BF)
                self.last[w, 1, at, :] = t_im.astype(BF)
                p_re, p_im = self.pair(psi, w, at)
                self.put(w, at, t_re * p_re - t_im * p_im, t_re * p_im + t_im * p_re)
        self.propagate(*self.far)
        half = self.n // 2
        top = in_top()
        for w in range(self.slots):
            weight = self.marks[w][2:3].astype(F32)
            for at in self.rows():
                re, im = self.got(w, at)
                part = slice(at.start % half, at.start % half + STEP)
                is_here = top == (at.start < half)
                received = jnp.where(
                    is_here, int_here[w, part, :].astype(F32), int_there[w, part, :].astype(F32)
                )
                measured = jnp.where(self.own, own_int[w, at, :].astype(F32), received)
                factor = weight * (re * re + im * im - measured)
                self.put(w, at, factor * re, factor * im)
        self.propagate(self.far[1], self.far[0])

    def reach_first(self):
        for w in range(self.slots):
            for at in self.rows():
                t_re, t_im = self.pair(self.last, w, at)
                y_re, y_im = (part.astype(BF).astype(F32) for part in self.got(w, at))
                self.put(w, at, t_re * y_re + t_im * y_im, t_re * y_im - t_im * y_re)
        self.propagate(self.near[1], self.near[0])

    def gradient(self, entering, base, out, final=None, sems=None):
        n = self.n
        copies = []
        for at in self.rows():
            sums = [0.0] * 4
            if base is not None:
                sums = [base[part, 0, at, c : c + n] for part in range(2) for c in (0, n)]
            for w in range(self.slots):
                mine, left = self.mine(w, at), self.left[w]
                a_re, a_im = entering(w, at)
                y_re, y_im = (part.astype(BF).astype(F32) for part in self.got(w, at))
                values = (a_re * y_re + a_im * y_im, a_re * y_im - a_im * y_re)
                for part, value in enumerate(values):
                    value = jnp.where(mine, value, 0.0)
                    first = jnp.where(left, value, 0.0)
                    sums[2 * part] = sums[2 * part] + first
                    sums[2 * part + 1] = sums[2 * part + 1] + (value - first)
            for part in range(2):
                out[part, 0, at, :n] = sums[2 * part]
                out[part, 0, at, n:] = sums[2 * part + 1]
            if final is not None and at.stop % SENT == 0:
                done = slice(at.stop - SENT, at.stop)
                copy = pltpu.make_async_copy(
                    out.at[:, :, done, :], final.at[:, :, done, :], sems.at[len(copies)]
                )
                copy.start()
                copies.append(copy)
        for copy in copies:
            copy.wait()


def facing_kernel(
    here_re, here_im, there_re, there_im, own_int, int_here, int_there, nl, nr, fl, fr,
    m0, r0, s0, m1, r1, s1, out, field, inner, outer, last, psi,
):
    placed = (m0, r0, s0, m1, r1, s1)
    waves = Waves(0, placed, (nl, nr), (fl, fr), (field, inner, outer, last))
    ints = (own_int, int_here, int_there)
    here, there = [[here_re.at[0]], [here_im.at[0]]], [[there_re.at[0]], [there_im.at[0]]]
    top = in_top()

    @pl.when(top)
    def _():
        waves.enter(here, psi)
        waves.leave(there, psi, *ints)
        waves.reach_first()
        waves.gradient(waves.probe, None, out)

    @pl.when(jnp.logical_not(top))
    def _():
        waves.enter(there, psi)
        waves.leave(here, psi, *ints)
        waves.gradient(lambda w, at: waves.pair(psi, w, at), None, out)


def entering_kernel(
    here_re, here_im, nl, nr, m0, r0, s0, m1, r1, s1, psi, field, inner, outer, last
):
    @pl.when(in_top())
    def _():
        placed = (m0, r0, s0, m1, r1, s1)
        waves = Waves(1, placed, (nl, nr), None, (field, inner, outer, last))
        waves.enter([[here_re.at[0]], [here_im.at[0]]], psi)


def opposite_kernel(
    here_re, here_im, there_re, there_im, own_int, int_here, int_there, nl, nr, fl, fr,
    m0, r0, s0, m1, r1, s1, entered, base, out, field, inner, outer, last, psi, total, sems,
):
    placed = (m0, r0, s0, m1, r1, s1)
    waves = Waves(1, placed, (nl, nr), (fl, fr), (field, inner, outer, last))
    ints = (own_int, int_here, int_there)
    here, there = [[here_re.at[0]], [here_im.at[0]]], [[there_re.at[0]], [there_im.at[0]]]
    top = in_top()

    @pl.when(top)
    def _():
        waves.leave(there, entered, *ints)
        waves.reach_first()
        waves.gradient(waves.probe, base, total, out, sems)

    @pl.when(jnp.logical_not(top))
    def _():
        waves.enter(there, psi)
        waves.leave(here, psi, *ints)
        waves.gradient(lambda w, at: waves.pair(psi, w, at), base, total, out, sems)


def kernel_call(kernel, name, out_shape, in_specs, scratch_shapes=(), out_spec=VM):
    many = isinstance(out_shape, tuple)
    return pl.pallas_call(
        kernel,
        out_shape=out_shape,
        in_specs=in_specs,
        out_specs=(VM,) * len(out_shape) if many else out_spec,
        scratch_shapes=scratch_shapes,
        compiler_params=pltpu.CompilerParams(vmem_limit_bytes=16 * MIB),
        cost_estimate=TINY,
        name=name,
    )


def on_device(obj, probe, phases, intensities, pos_row, pos_col, counts):
    n = probe.shape[1]
    slots = pos_row.shape[0]
    tiles = lax.axis_size("tile")
    half = intensities.shape[1] // lax.axis_size("sec")
    after = lax.optimization_barrier

    def swap(value):
        return lax.ppermute(value, "sec", [(0, 1), (1, 0)])

    def send(value, pairs):
        inside = [(a, b) for a, b in pairs if 0 <= min(a, b) and max(a, b) < tiles]
        return lax.ppermute(value, "tile", inside)

    onward = [(i, i + 1) for i in range(tiles)]
    paired = [(i, i ^ 1) for i in range(tiles)]
    relayed = [(i, i - 2 if i % 2 else i + 2) for i in range(tiles)]

    sideways = [(b, a) for a, b in relayed]
    facing_re = send(obj[0:1], paired)
    crossed = send(obj[1:2], sideways)
    opposite_im = send(crossed, paired)
    own_there = swap(obj)
    positions = (pos_row, pos_col, counts)
    cut = (1, *obj.shape[1:])
    message, second = kernel_call(
        message_kernel,
        "message",
        (
            jax.ShapeDtypeStruct((slots, half + CODE_ROWS, n), BF),
            jax.ShapeDtypeStruct(cut, BF),
        ),
        [SM] * 3 + [VM] * 2,
    )(*positions, intensities, obj)
    facing_im = send(second, paired)
    int_here = send(message, onward)
    opposite_re = send(facing_re, relayed)
    phases, _ = after((phases, facing_re))

    double = jax.ShapeDtypeStruct((2 * n, 2 * n), BF)
    wave_shapes = (
        jax.ShapeDtypeStruct((slots, 8, n), jnp.int32),
        jax.ShapeDtypeStruct((slots, 2, n, n), BF),
        jax.ShapeDtypeStruct((slots, 2, 2, n, n), BF),
    )
    nl, nr, fl, fr, *own_waves = kernel_call(
        own_kernel, "own", (double,) * 4 + wave_shapes, [SM] * 3 + [VM] * 4
    )(*positions, phases[None], probe, obj, own_there)
    facing_im, nl = after((facing_im, nl))
    int_here, _ = after((int_here, facing_im))
    int_there = swap(int_here)
    past_waves = kernel_call(past_kernel, "past", wave_shapes, [VM] * 4)(
        int_here, probe, obj, own_there
    )
    placed = (*own_waves, *past_waves)

    work = [
        pltpu.VMEM((2 * n, slots * n), BF),
        pltpu.VMEM((slots * n, 2 * n), BF),
        pltpu.VMEM((slots * n, 2 * n), F32),
    ]
    def pieces(value):
        middle = value.shape[2] // 2
        return swap(value[:, :, :middle]), swap(value[:, :, middle:])

    pair = pltpu.VMEM((slots, 2, n, n), BF)
    work.append(pair)
    ints = (intensities, int_here, int_there)
    grad_shape = jax.ShapeDtypeStruct(obj.shape, F32)
    partial = kernel_call(
        facing_kernel, "facing", grad_shape, [VM] * 17, work + [pair]
    )(facing_re, facing_im, swap(facing_re), swap(facing_im), *ints, nl, nr, fl, fr, *placed)
    opposite_re_there = swap(opposite_re)
    opposite_im, partial = after((opposite_im, partial))
    opposite = (opposite_re, opposite_im)
    opposite_there = (opposite_re_there, swap(opposite_im))
    entered = kernel_call(
        entering_kernel, "entering", jax.ShapeDtypeStruct((slots, 2, n, n), BF), [VM] * 10, work
    )(*opposite, nl, nr, *placed)
    return kernel_call(
        opposite_kernel,
        "opposite",
        grad_shape,
        [VM] * 19,
        work + [pair, pltpu.VMEM(obj.shape, F32), pltpu.SemaphoreType.DMA((n // SENT,))],
        out_spec=pl.BlockSpec(memory_space=pltpu.HBM),
    )(*opposite, *opposite_there, *ints, nl, nr, fl, fr, *placed, entered, partial)


def solution(mesh):
    placed = (
        P(None, "sec", "tile", None),
        P(),
        P(),
        P("tile", None, None),
        P("tile"),
        P("tile"),
        P("tile"),
    )
    return jax.shard_map(
        on_device,
        mesh=mesh,
        in_specs=placed,
        out_specs=P(None, "sec", "tile", None),
        check_vma=False,
    )
```

time: 36.3 us -> 34.5 us (0.950)
  starting transfers between devices: 16 us -> 14.1 us
  waiting for transfers between devices: 3.1 us -> 4.38 us
  local copies, waits for them, and re-layouts: 2.23 us -> 1.17 us
  Pallas kernels: 13.6 us -> 13.2 us
    ppermute x5 -> x6, waiting for transfers between devices: 2.72 us -> 4.08 us  [send(): return lax.ppermute(value, 'tile', inside)]
    ppermute x8 -> x6, starting transfers between devices: 1.78 us -> 0.45 us  [swap(): return lax.ppermute(value, 'sec', [(0, 1), (1, 0)])]
    unnamed x12, local copies, waits for them, and re-layouts: 1.16 us -> 0.03 us
    ppermute x5 -> x6, starting transfers between devices: 14.2 us -> 13.6 us  [send(): return lax.ppermute(value, 'tile', inside)]
    slice x3 -> x1, local copies, waits for them, and re-layouts: 1.07 us -> 1.14 us  [on_device(): crossed = send(obj[1:2], sideways)]
  transfers between devices with their start and end apart: 13 -> 12, of which waited for: 3 -> 3; matrix products, arithmetic and copies ran while one was open for 3% -> 3% of each run, Pallas kernels for 27% -> 29%
where the time goes in v3:
time: 34.5 us; the launch traced here: 33.9 us
  starting transfers between devices  14.1 us (41%)
  Pallas kernels  13.2 us (38%)
  waiting for transfers between devices  4.38 us (13%)
  local copies, waits for them, and re-layouts  1.17 us (3%)
  between operations  1.04 us (3%)
    ppermute x6, starting transfers between devices, send(): return lax.ppermute(value, 'tile', inside)  13.6 us
    ppermute x6, waiting for transfers between devices, send(): return lax.ppermute(value, 'tile', inside)  4.08 us
    pallas_call x1, Pallas kernels, on_device(): kernel_call(opposite_kernel, 'opposite', grad_shape, [VM] * 19, work + [p...  3.49 us
    pallas_call x1, Pallas kernels, on_device(): kernel_call(facing_kernel, 'facing', grad_shape, [VM] * 17, work + [pair])  3.43 us
    pallas_call x1, Pallas kernels, on_device(): kernel_call(own_kernel, 'own', (double,) * 4 + wave_shapes, [SM] * 3 + [V...  3.21 us
    pallas_call x1, Pallas kernels, on_device(): kernel_call(past_kernel, 'past', wave_shapes, [VM] * 4)  1.29 us
    pallas_call x1, Pallas kernels, on_device(): kernel_call(entering_kernel, 'entering', jax.ShapeDtypeStruct((slots, 2,...  1.21 us
    slice x1, local copies, waits for them, and re-layouts, on_device(): crossed = send(obj[1:2], sideways)  1.14 us
  transfers between devices with their start and end apart: 12, of which 3 were waited for; matrix products, arithmetic and copies ran while one was open for 3% of the time, Pallas kernels for 29%

profile of v3, /device:TPU:24, one launch (start us, length us, event | category | flops | bytes accessed | tf_op | source)
XLA Modules:
  0.0 33.9 jit_solution(14392738353189431069)
XLA Ops:
  0.0 0.0 copy-start
  0.0 0.0 copy-start.1
  0.0 0.0 collective-permute-start.5
  0.0 1.1 %fusion = (bf16[1,1,256,512]{3,2,1,0:T(8,128)(2,1)S(1)}, bf16[1,1,256,512]{3,2,1,0:T(8,128)(2,1)S(1)}) fusion(bf16[2,1,256,512]{3,2,1,0:T(8,128)(2,1)} %own_here.3), kind=kLoop, calls=%fused_computation | loop fusion | bytes 1048576 | tf_op jit(solution)/shard_map/slice | solution.py:375
  1.2 0.0 copy-start.3
  1.2 0.0 copy-start.4
  1.2 1.6 %collective-permute-start = (bf16[1,1,256,512]{3,2,1,0:T(8,128)(2,1)S(1)}, bf16[1,1,256,512]{3,2,1,0:T(8,128)(2,1)S(1)}, u32[]{:S(2)}, u32[]{:S(2)}) collective-permute-start(bf16[1,1,256,512]{3,2,1,0:T(8,128)(2,1)S(1)} %get-tuple-element.42), channel_id=1, source_target_pairs={{0,1},{1,0},{2,3},{3,2},{4,5},{5,4},{6,7},{7,6},{8,9},{9,8},{10,11... | collective-permute-start | bytes 786440 | tf_op jit(solution)/shard_map/ppermute | solution.py:367
  3.4 0.0 copy-done
  3.4 0.0 copy-done.1
  3.4 0.0 copy-done.3
  3.4 0.0 copy-done.4
  3.4 0.0 copy-start.2
  3.4 0.6 %message.1 = (bf16[2,144,256]{2,1,0:T(8,128)(2,1)S(1)}, bf16[1,1,256,512]{3,2,1,0:T(8,128)(2,1)S(1)}) custom-call(s32[2]{0:T(128)S(1)} %copy-done.3, s32[2]{0:T(128)S(1)} %copy-done.4, s32[1]{0:T(128)S(6)} %copy.8.count_ref, bf16[2,256,256]{2,1,0:T(8,128)(2,1)S(1)} %copy-done.1, bf16[2,1,256,512]{3,2,1,0:T(8,128)(2,1)S(1)} %copy-done), custom_call_target="tpu_custom_call" | custom-call | flops 1000 | bytes 1000 | tf_op jit(solution)/shard_map/message/pallas_call | solution.py:380
  4.0 0.6 %collective-permute-start.4 = (bf16[1,1,256,512]{3,2,1,0:T(8,128)(2,1)S(1)}, bf16[1,1,256,512]{3,2,1,0:T(8,128)(2,1)S(1)}, u32[]{:S(2)}, u32[]{:S(2)}) collective-permute-start(bf16[1,1,256,512]{3,2,1,0:T(8,128)(2,1)S(1)} %get-tuple-element.23), channel_id=1, source_target_pairs={{0,1},{1,0},{2,3},{3,2},{4,5},{5,4},{6,7},{7,6},{8,9},{9,8},{10,11... | collective-permute-start | bytes 786440 | tf_op jit(solution)/shard_map/ppermute | solution.py:367
  4.6 3.3 %collective-permute-start.2 = (bf16[1,1,256,512]{3,2,1,0:T(8,128)(2,1)S(1)}, bf16[1,1,256,512]{3,2,1,0:T(8,128)(2,1)S(1)}, u32[]{:S(2)}, u32[]{:S(2)}) collective-permute-start(bf16[1,1,256,512]{3,2,1,0:T(8,128)(2,1)S(1)} %get-tuple-element.41), channel_id=1, source_target_pairs={{2,0},{4,2},{1,3},{6,4},{3,5},{8,6},{5,7},{10,8},{7,9},{12,10},{9,... | collective-permute-start | bytes 786440 | tf_op jit(solution)/shard_map/ppermute | solution.py:367
  7.9 0.0 copy-start.5
  7.9 3.5 %collective-permute-start.8 = (bf16[2,144,256]{2,1,0:T(8,128)(2,1)S(1)}, bf16[2,144,256]{2,1,0:T(8,128)(2,1)S(1)}, u32[]{:S(2)}, u32[]{:S(2)}) collective-permute-start(bf16[2,144,256]{2,1,0:T(8,128)(2,1)S(1)} %get-tuple-element.27), channel_id=1, source_target_pairs={{0,1},{1,2},{2,3},{3,4},{4,5},{5,6},{6,7},{7,8},{8,9},{9,10},{10,1... | collective-permute-start | bytes 442376 | tf_op jit(solution)/shard_map/ppermute | solution.py:367
  11.5 0.0 collective-permute-done.here_re
  11.5 0.1 collective-permute-start.6
  11.6 0.0 collective-permute-done.5.own_there
  11.6 2.2 %collective-permute-start.1 = (bf16[1,1,256,512]{3,2,1,0:T(8,128)(2,1)S(1)}, bf16[1,1,256,512]{3,2,1,0:T(8,128)(2,1)S(1)}, u32[]{:S(2)}, u32[]{:S(2)}) collective-permute-start(bf16[1,1,256,512]{3,2,1,0:T(8,128)(2,1)S(1)} %collective-permute-done.here_re), channel_id=1, source_target_pairs={{0,2},{2,4},{3,1},{4,6},{5,3},{6,8},{7,5},{8,10},{9,7},{10,12},{11... | collective-permute-start | bytes 786440 | tf_op jit(solution)/shard_map/ppermute | solution.py:367
  13.8 0.0 copy-done.2
  13.8 0.0 copy-done.5
  13.8 3.2 %own.1 = (bf16[512,512]{1,0:T(8,128)(2,1)S(1)}, bf16[512,512]{1,0:T(8,128)(2,1)S(1)}, bf16[512,512]{1,0:T(8,128)(2,1)S(1)}, bf16[512,512]{1,0:T(8,128)(2,1)S(1)}...) custom-call(s32[2]{0:T(128)S(1)} %copy-done.3, ...), custom_call_target="tpu_custom_call" | custom-call | flops 1000 | bytes 1000 | tf_op jit(solution)/shard_map/own/pallas_call | solution.py:400
  17.0 0.0 collective-permute-done.4.here_im
  17.0 0.3 collective-permute-start.7
  17.3 0.0 collective-permute-done.2
  17.3 2.4 %collective-permute-start.3 = (bf16[1,1,256,512]{3,2,1,0:T(8,128)(2,1)S(1)}, bf16[1,1,256,512]{3,2,1,0:T(8,128)(2,1)S(1)}, u32[]{:S(2)}, u32[]{:S(2)}) collective-permute-start(bf16[1,1,256,512]{3,2,1,0:T(8,128)(2,1)S(1)} %collective-permute-done.2), channel_id=1, source_target_pairs={{0,1},{1,0},{2,3},{3,2},{4,5},{5,4},{6,7},{7,6},{8,9},{9,8},{10,11... | collective-permute-start | bytes 786440 | tf_op jit(solution)/shard_map/ppermute | solution.py:367
  19.8 1.7 %collective-permute-done.8.received.int_here = bf16[2,144,256]{2,1,0:T(8,128)(2,1)S(1)} collective-permute-done((bf16[2,144,256]{2,1,0:T(8,128)(2,1)S(1)}, bf16[2,144,256]{2,1,0:T(8,128)(2,1)S(1)}, u32[]{:S(2)}, u32[]{:S(2)}) %collective-permute-start.8) | collective-permute-done | bytes 147488 | tf_op jit(solution)/shard_map/ppermute | solution.py:367
  21.5 0.0 collective-permute-start.9
  21.5 1.3 %past.1 = (s32[2,8,256]{2,1,0:T(8,128)S(1)}, bf16[2,2,256,256]{3,2,1,0:T(8,128)(2,1)S(1)}, bf16[2,2,2,256,256]{4,3,2,1,0:T(8,128)(2,1)S(1)}) custom-call(bf16[2,144,256]{2,1,0:T(8,128)(2,1)S(1)} %collective-permute-done.8.received.int_here, bf16[2,256,256]{2,1,0:T(8,128)(2,1)S(1)} %copy-done.2, bf16[2,1,256,512]{3,2,1,0:T(8,128)(2,1)S(1)} %copy-done, ...), custom_call_target="tpu_custom_call" | custom-call | flops 1000 | bytes 1000 | tf_op jit(solution)/shard_map/past/pallas_call | solution.py:406
  22.8 2.4 %collective-permute-done.1.here_re = bf16[1,1,256,512]{3,2,1,0:T(8,128)(2,1)S(1)} collective-permute-done((bf16[1,1,256,512]{3,2,1,0:T(8,128)(2,1)S(1)}, bf16[1,1,256,512]{3,2,1,0:T(8,128)(2,1)S(1)}, u32[]{:S(2)}, u32[]{:S(2)}) %collective-permute-start.1) | collective-permute-done | bytes 262176 | tf_op jit(solution)/shard_map/ppermute | solution.py:367
  25.2 0.0 collective-permute-start.10
  25.2 0.0 collective-permute-done.6.there_re
  25.2 0.0 collective-permute-done.9.int_there
  25.2 0.0 collective-permute-done.7.there_im
  25.2 3.4 %facing.1.base = f32[2,1,256,512]{3,2,1,0:T(8,128)S(1)} custom-call(bf16[1,1,256,512]{3,2,1,0:T(8,128)(2,1)S(1)} %collective-permute-done.here_re, bf16[1,1,256,512]{3,2,1,0:T(8,128)(2,1)S(1)} %collective-permute-done.4.here_im, bf16[1,1,256,512]{3,2,1,0:T(8,128)(2,1)S(1)} %collective-permute-done.6.there_re, ...), custom_call_target="tpu_custom_call" | custom-call | flops 1000 | bytes 1000 | tf_op jit(solution)/shard_map/facing/pallas_call | solution.py:424
  28.6 0.0 collective-permute-done.3.here_im
  28.6 0.1 collective-permute-start.11
  28.7 1.2 %entering.1.entered = bf16[2,2,256,256]{3,2,1,0:T(8,128)(2,1)S(1)} custom-call(bf16[1,1,256,512]{3,2,1,0:T(8,128)(2,1)S(1)} %collective-permute-done.1.here_re, bf16[1,1,256,512]{3,2,1,0:T(8,128)(2,1)S(1)} %collective-permute-done.3.here_im, bf16[512,512]{1,0:T(8,128)(2,1)S(1)} %get-tuple-element.29.nl, bf16[512,512]{1,0:T(8,128)(2,1)S(1)} %get-tuple-element.30.nr, ...), custom_call_target="tpu_custom_call" | custom-call | flops 1000 | bytes 1000 | tf_op jit(solution)/shard_map/entering/pallas_call | solution.py:431
  29.9 0.0 collective-permute-done.10.there_re
  29.9 0.3 collective-permute-done.11.there_im
  30.2 3.5 %opposite.1 = f32[2,1,256,512]{3,2,1,0:T(8,128)} custom-call(bf16[1,1,256,512]{3,2,1,0:T(8,128)(2,1)S(1)} %collective-permute-done.1.here_re, bf16[1,1,256,512]{3,2,1,0:T(8,128)(2,1)S(1)} %collective-permute-done.3.here_im, bf16[1,1,256,512]{3,2,1,0:T(8,128)(2,1)S(1)} %collective-permute-done.10.there_re, ...), custom_call_target="tpu_custom_call" | custom-call | flops 1000 | bytes 1000 | tf_op jit(solution)/shard_map/opposite/pallas_call | solution.py:434
Async XLA Ops:
  0.0 3.4 %copy-start = (bf16[2,1,256,512]{3,2,1,0:T(8,128)(2,1)S(1)}, bf16[2,1,256,512]{3,2,1,0:T(8,128)(2,1)}, u32[]{:S(2)}) copy-start(bf16[2,1,256,512]{3,2,1,0:T(8,128)(2,1)} %own_here.3) | copy-start | bytes 1572868
  0.0 3.4 %copy-start.1 = (bf16[2,256,256]{2,1,0:T(8,128)(2,1)S(1)}, bf16[2,256,256]{2,1,0:T(8,128)(2,1)}, u32[]{:S(2)}) copy-start(bf16[2,256,256]{2,1,0:T(8,128)(2,1)} %own_int.3) | copy-start | bytes 786436
  0.0 11.5 %collective-permute-start.5 = (bf16[2,1,256,512]{3,2,1,0:T(8,128)(2,1)}, bf16[2,1,256,512]{3,2,1,0:T(8,128)(2,1)S(1)}, u32[]{:S(2)}, u32[]{:S(2)}) collective-permute-start(bf16[2,1,256,512]{3,2,1,0:T(8,128)(2,1)} %own_here.3), channel_id=1, source_target_pairs={{0,16},{16,0},{1,17},{17,1},{2,18},{18,2},{3,19},{19,3},{4,20},{20... | collective-permute-start | bytes 1572872 | tf_op jit(solution)/shard_map/ppermute | solution.py:363
  1.2 2.3 %copy-start.3 = (s32[2]{0:T(128)S(1)}, s32[2]{0:T(128)}, u32[]{:S(2)}) copy-start(s32[2]{0:T(128)} %row_ref.3) | copy-start | bytes 28
  1.2 2.3 %copy-start.4 = (s32[2]{0:T(128)S(1)}, s32[2]{0:T(128)}, u32[]{:S(2)}) copy-start(s32[2]{0:T(128)} %col_ref.3) | copy-start | bytes 28
  1.2 10.3 %collective-permute-start = (bf16[1,1,256,512]{3,2,1,0:T(8,128)(2,1)S(1)}, bf16[1,1,256,512]{3,2,1,0:T(8,128)(2,1)S(1)}, u32[]{:S(2)}, u32[]{:S(2)}) collective-permute-start(bf16[1,1,256,512]{3,2,1,0:T(8,128)(2,1)S(1)} %get-tuple-element.42), channel_id=1, source_target_pairs={{0,1},{1,0},{2,3},{3,2},{4,5},{5,4},{6,7},{7,6},{8,9},{9,8},{10,11... | collective-permute-start | bytes 786440 | tf_op jit(solution)/shard_map/ppermute | solution.py:367
  3.4 10.4 %copy-start.2 = (bf16[2,256,256]{2,1,0:T(8,128)(2,1)S(1)}, bf16[2,256,256]{2,1,0:T(8,128)(2,1)}, u32[]{:S(2)}) copy-start(bf16[2,256,256]{2,1,0:T(8,128)(2,1)} %probe_ref.3) | copy-start | bytes 786436
  4.0 13.0 %collective-permute-start.4 = (bf16[1,1,256,512]{3,2,1,0:T(8,128)(2,1)S(1)}, bf16[1,1,256,512]{3,2,1,0:T(8,128)(2,1)S(1)}, u32[]{:S(2)}, u32[]{:S(2)}) collective-permute-start(bf16[1,1,256,512]{3,2,1,0:T(8,128)(2,1)S(1)} %get-tuple-element.23), channel_id=1, source_target_pairs={{0,1},{1,0},{2,3},{3,2},{4,5},{5,4},{6,7},{7,6},{8,9},{9,8},{10,11... | collective-permute-start | bytes 786440 | tf_op jit(solution)/shard_map/ppermute | solution.py:367
  4.6 12.7 %collective-permute-start.2 = (bf16[1,1,256,512]{3,2,1,0:T(8,128)(2,1)S(1)}, bf16[1,1,256,512]{3,2,1,0:T(8,128)(2,1)S(1)}, u32[]{:S(2)}, u32[]{:S(2)}) collective-permute-start(bf16[1,1,256,512]{3,2,1,0:T(8,128)(2,1)S(1)} %get-tuple-element.41), channel_id=1, source_target_pairs={{2,0},{4,2},{1,3},{6,4},{3,5},{8,6},{5,7},{10,8},{7,9},{12,10},{9,... | collective-permute-start | bytes 786440 | tf_op jit(solution)/shard_map/ppermute | solution.py:367
  7.9 5.9 %copy-start.5 = (f32[256]{0:T(256)S(1)}, f32[256]{0:T(256)}, u32[]{:S(2)}) copy-start(f32[256]{0:T(256)} %param.9) | copy-start | bytes 3076
  7.9 13.5 %collective-permute-start.8 = (bf16[2,144,256]{2,1,0:T(8,128)(2,1)S(1)}, bf16[2,144,256]{2,1,0:T(8,128)(2,1)S(1)}, u32[]{:S(2)}, u32[]{:S(2)}) collective-permute-start(bf16[2,144,256]{2,1,0:T(8,128)(2,1)S(1)} %get-tuple-element.27), channel_id=1, source_target_pairs={{0,1},{1,2},{2,3},{3,4},{4,5},{5,6},{6,7},{7,8},{8,9},{9,10},{10,1... | collective-permute-start | bytes 442376 | tf_op jit(solution)/shard_map/ppermute | solution.py:367
  11.5 13.7 %collective-permute-start.6 = (bf16[1,1,256,512]{3,2,1,0:T(8,128)(2,1)S(1)}, bf16[1,1,256,512]{3,2,1,0:T(8,128)(2,1)S(1)}, u32[]{:S(2)}, u32[]{:S(2)}) collective-permute-start(bf16[1,1,256,512]{3,2,1,0:T(8,128)(2,1)S(1)} %collective-permute-done.here_re), channel_id=1, source_target_pairs={{0,16},{16,0},{1,17},{17,1},{2,18},{18,2},{3,19},{19,3},{4,20},{20... | collective-permute-start | bytes 786440 | tf_op jit(solution)/shard_map/ppermute | solution.py:363
  11.6 13.6 %collective-permute-start.1 = (bf16[1,1,256,512]{3,2,1,0:T(8,128)(2,1)S(1)}, bf16[1,1,256,512]{3,2,1,0:T(8,128)(2,1)S(1)}, u32[]{:S(2)}, u32[]{:S(2)}) collective-permute-start(bf16[1,1,256,512]{3,2,1,0:T(8,128)(2,1)S(1)} %collective-permute-done.here_re), channel_id=1, source_target_pairs={{0,2},{2,4},{3,1},{4,6},{5,3},{6,8},{7,5},{8,10},{9,7},{10,12},{11... | collective-permute-start | bytes 786440 | tf_op jit(solution)/shard_map/ppermute | solution.py:367
  17.0 8.1 %collective-permute-start.7 = (bf16[1,1,256,512]{3,2,1,0:T(8,128)(2,1)S(1)}, bf16[1,1,256,512]{3,2,1,0:T(8,128)(2,1)S(1)}, u32[]{:S(2)}, u32[]{:S(2)}) collective-permute-start(bf16[1,1,256,512]{3,2,1,0:T(8,128)(2,1)S(1)} %collective-permute-done.4.here_im), channel_id=1, source_target_pairs={{0,16},{16,0},{1,17},{17,1},{2,18},{18,2},{3,19},{19,3},{4,20},{20... | collective-permute-start | bytes 786440 | tf_op jit(solution)/shard_map/ppermute | solution.py:363
  17.3 11.3 %collective-permute-start.3 = (bf16[1,1,256,512]{3,2,1,0:T(8,128)(2,1)S(1)}, bf16[1,1,256,512]{3,2,1,0:T(8,128)(2,1)S(1)}, u32[]{:S(2)}, u32[]{:S(2)}) collective-permute-start(bf16[1,1,256,512]{3,2,1,0:T(8,128)(2,1)S(1)} %collective-permute-done.2), channel_id=1, source_target_pairs={{0,1},{1,0},{2,3},{3,2},{4,5},{5,4},{6,7},{7,6},{8,9},{9,8},{10,11... | collective-permute-start | bytes 786440 | tf_op jit(solution)/shard_map/ppermute | solution.py:367
  21.5 3.7 %collective-permute-start.9 = (bf16[2,144,256]{2,1,0:T(8,128)(2,1)S(1)}, bf16[2,144,256]{2,1,0:T(8,128)(2,1)S(1)}, u32[]{:S(2)}, u32[]{:S(2)}) collective-permute-start(bf16[2,144,256]{2,1,0:T(8,128)(2,1)S(1)} %collective-permute-done.8.received.int_here), channel_id=1, source_target_pairs={{0,16},{16,0},{1,17},{17,1},{2,18},{18,2},{3,19},{19,3},{4,20},{20... | collective-permute-start | bytes 442376 | tf_op jit(solution)/shard_map/ppermute | solution.py:363
  25.2 4.8 %collective-permute-start.10 = (bf16[1,1,256,512]{3,2,1,0:T(8,128)(2,1)S(1)}, bf16[1,1,256,512]{3,2,1,0:T(8,128)(2,1)S(1)}, u32[]{:S(2)}, u32[]{:S(2)}) collective-permute-start(bf16[1,1,256,512]{3,2,1,0:T(8,128)(2,1)S(1)} %collective-permute-done.1.here_re), channel_id=1, source_target_pairs={{0,16},{16,0},{1,17},{17,1},{2,18},{18,2},{3,19},{19,3},{4,20},{20... | collective-permute-start | bytes 786440 | tf_op jit(solution)/shard_map/ppermute | solution.py:363
  28.6 1.6 %collective-permute-start.11 = (bf16[1,1,256,512]{3,2,1,0:T(8,128)(2,1)S(1)}, bf16[1,1,256,512]{3,2,1,0:T(8,128)(2,1)S(1)}, u32[]{:S(2)}, u32[]{:S(2)}) collective-permute-start(bf16[1,1,256,512]{3,2,1,0:T(8,128)(2,1)S(1)} %collective-permute-done.3.here_im), channel_id=1, source_target_pairs={{0,16},{16,0},{1,17},{17,1},{2,18},{18,2},{3,19},{19,3},{4,20},{20... | collective-permute-start | bytes 786440 | tf_op jit(solution)/shard_map/ppermute | solution.py:363

commit v4 on v3

--- a/solution.py
+++ b/solution.py
@@ -14,6 +14,7 @@
 SM = pl.BlockSpec(memory_space=pltpu.SMEM)
 MIB = 1024 * 1024
 CODE_ROWS = 16
+PIECES = 2
 STEP = 32
 SENT = 64
 TINY = pl.CostEstimate(flops=1000, bytes_accessed=1000, transcendentals=0)
@@ -281,14 +282,17 @@
             copy.wait()
 
 
-def facing_kernel(
-    here_re, here_im, there_re, there_im, own_int, int_here, int_there, nl, nr, fl, fr,
-    m0, r0, s0, m1, r1, s1, out, field, inner, outer, last, psi,
-):
+def facing_kernel(here_re, here_im, there_re, *refs):
+    there_im, refs = refs[:PIECES], refs[PIECES:]
+    (
+        own_int, int_here, int_there, nl, nr, fl, fr, m0, r0, s0, m1, r1, s1,
+        out, field, inner, outer, last, psi,
+    ) = refs
     placed = (m0, r0, s0, m1, r1, s1)
     waves = Waves(0, placed, (nl, nr), (fl, fr), (field, inner, outer, last))
     ints = (own_int, int_here, int_there)
-    here, there = [[here_re.at[0]], [here_im.at[0]]], [[there_re.at[0]], [there_im.at[0]]]
+    here = [[here_re.at[0]], [here_im.at[0]]]
+    there = [[there_re.at[0]], [piece.at[0] for piece in there_im]]
     top = in_top()
 
     @pl.when(top)
@@ -414,16 +418,16 @@
         pltpu.VMEM((slots * n, 2 * n), F32),
     ]
     def pieces(value):
-        middle = value.shape[2] // 2
-        return swap(value[:, :, :middle]), swap(value[:, :, middle:])
+        step = value.shape[2] // PIECES
+        return [swap(value[:, :, at : at + step]) for at in range(0, value.shape[2], step)]
 
     pair = pltpu.VMEM((slots, 2, n, n), BF)
     work.append(pair)
     ints = (intensities, int_here, int_there)
     grad_shape = jax.ShapeDtypeStruct(obj.shape, F32)
     partial = kernel_call(
-        facing_kernel, "facing", grad_shape, [VM] * 17, work + [pair]
-    )(facing_re, facing_im, swap(facing_re), swap(facing_im), *ints, nl, nr, fl, fr, *placed)
+        facing_kernel, "facing", grad_shape, [VM] * (16 + PIECES), work + [pair]
+    )(facing_re, facing_im, swap(facing_re), *pieces(facing_im), *ints, nl, nr, fl, fr, *placed)
     opposite_re_there = swap(opposite_re)
     opposite_im, partial = after((opposite_im, partial))
     opposite = (opposite_re, opposite_im)

time: 34.5 us -> 33.7 us (0.977)
  the two profiles are of different devices: /device:TPU:24 before, /device:TPU:0 now
where the time goes in v4:
time: 33.7 us; the launch traced here: 33.5 us
  starting transfers between devices  14.8 us (44%)
  Pallas kernels  13.2 us (39%)
  waiting for transfers between devices  3.37 us (10%)
  local copies, waits for them, and re-layouts  1.11 us (3%)
  between operations  1.03 us (3%)
    ppermute x6, starting transfers between devices, send(): return lax.ppermute(value, 'tile', inside)  13.1 us
    pallas_call x1, Pallas kernels, on_device(): kernel_call(opposite_kernel, 'opposite', grad_shape, [VM] * 19, work + [p...  3.48 us
    pallas_call x1, Pallas kernels, on_device(): kernel_call(facing_kernel, 'facing', grad_shape, [VM] * (16 + PIECES), wo...  3.46 us
    pallas_call x1, Pallas kernels, on_device(): kernel_call(own_kernel, 'own', (double,) * 4 + wave_shapes, [SM] * 3 + [V...  3.21 us
    ppermute x6, waiting for transfers between devices, send(): return lax.ppermute(value, 'tile', inside)  3.06 us
    ppermute x7, starting transfers between devices, swap(): return lax.ppermute(value, 'sec', [(0, 1), (1, 0)])  1.66 us
    pallas_call x1, Pallas kernels, on_device(): kernel_call(past_kernel, 'past', wave_shapes, [VM] * 4)  1.29 us
    pallas_call x1, Pallas kernels, on_device(): kernel_call(entering_kernel, 'entering', jax.ShapeDtypeStruct((slots, 2,...  1.21 us
  transfers between devices with their start and end apart: 13, of which 3 were waited for; matrix products, arithmetic and copies ran while one was open for 3% of the time, Pallas kernels for 29%

profile of v4, /device:TPU:0, one launch (start us, length us, event | category | flops | bytes accessed | tf_op | source)
XLA Modules:
  0.0 33.5 jit_solution(7611777952412599180)
XLA Ops:
  0.0 0.0 copy-start
  0.0 0.0 copy-start.1
  0.0 0.5 %collective-permute-start.5 = (bf16[2,1,256,512]{3,2,1,0:T(8,128)(2,1)}, bf16[2,1,256,512]{3,2,1,0:T(8,128)(2,1)S(1)}, u32[]{:S(2)}, u32[]{:S(2)}) collective-permute-start(bf16[2,1,256,512]{3,2,1,0:T(8,128)(2,1)} %own_here.3), channel_id=1, source_target_pairs={{0,16},{16,0},{1,17},{17,1},{2,18},{18,2},{3,19},{19,3},{4,20},{20... | collective-permute-start | bytes 1572872 | tf_op jit(solution)/shard_map/ppermute | solution.py:367
  0.5 1.1 %fusion = (bf16[1,1,256,512]{3,2,1,0:T(8,128)(2,1)S(1)}, bf16[1,1,256,512]{3,2,1,0:T(8,128)(2,1)S(1)}) fusion(bf16[2,1,256,512]{3,2,1,0:T(8,128)(2,1)} %own_here.3), kind=kLoop, calls=%fused_computation | loop fusion | bytes 1048576 | tf_op jit(solution)/shard_map/slice | solution.py:379
  1.5 2.6 %collective-permute-start = (bf16[1,1,256,512]{3,2,1,0:T(8,128)(2,1)S(1)}, bf16[1,1,256,512]{3,2,1,0:T(8,128)(2,1)S(1)}, u32[]{:S(2)}, u32[]{:S(2)}) collective-permute-start(bf16[1,1,256,512]{3,2,1,0:T(8,128)(2,1)S(1)} %get-tuple-element.42), channel_id=1, source_target_pairs={{0,1},{1,0},{2,3},{3,2},{4,5},{5,4},{6,7},{7,6},{8,9},{9,8},{10,11... | collective-permute-start | bytes 786440 | tf_op jit(solution)/shard_map/ppermute | solution.py:371
  4.2 0.0 copy-start.3
  4.2 0.0 copy-start.4
  4.2 1.4 %collective-permute-start.2 = (bf16[1,1,256,512]{3,2,1,0:T(8,128)(2,1)S(1)}, bf16[1,1,256,512]{3,2,1,0:T(8,128)(2,1)S(1)}, u32[]{:S(2)}, u32[]{:S(2)}) collective-permute-start(bf16[1,1,256,512]{3,2,1,0:T(8,128)(2,1)S(1)} %get-tuple-element.41), channel_id=1, source_target_pairs={{2,0},{4,2},{1,3},{6,4},{3,5},{8,6},{5,7},{10,8},{7,9},{12,10},{9,... | collective-permute-start | bytes 786440 | tf_op jit(solution)/shard_map/ppermute | solution.py:371
  6.2 0.0 copy-done
  6.2 0.0 copy-done.1
  6.2 0.0 copy-done.3
  6.3 0.0 copy-done.4
  6.3 0.0 copy-start.2
  6.3 0.6 %message.1 = (bf16[2,144,256]{2,1,0:T(8,128)(2,1)S(1)}, bf16[1,1,256,512]{3,2,1,0:T(8,128)(2,1)S(1)}) custom-call(s32[2]{0:T(128)S(1)} %copy-done.3, s32[2]{0:T(128)S(1)} %copy-done.4, s32[1]{0:T(128)S(6)} %copy.8.count_ref, bf16[2,256,256]{2,1,0:T(8,128)(2,1)S(1)} %copy-done.1, bf16[2,1,256,512]{3,2,1,0:T(8,128)(2,1)S(1)} %copy-done), custom_call_target="tpu_custom_call" | custom-call | flops 1000 | bytes 1000 | tf_op jit(solution)/shard_map/message/pallas_call | solution.py:384
  6.9 2.7 %collective-permute-start.4 = (bf16[1,1,256,512]{3,2,1,0:T(8,128)(2,1)S(1)}, bf16[1,1,256,512]{3,2,1,0:T(8,128)(2,1)S(1)}, u32[]{:S(2)}, u32[]{:S(2)}) collective-permute-start(bf16[1,1,256,512]{3,2,1,0:T(8,128)(2,1)S(1)} %get-tuple-element.23), channel_id=1, source_target_pairs={{0,1},{1,0},{2,3},{3,2},{4,5},{5,4},{6,7},{7,6},{8,9},{9,8},{10,11... | collective-permute-start | bytes 786440 | tf_op jit(solution)/shard_map/ppermute | solution.py:371
  9.6 0.0 copy-start.5
  9.6 1.9 %collective-permute-start.9 = (bf16[2,144,256]{2,1,0:T(8,128)(2,1)S(1)}, bf16[2,144,256]{2,1,0:T(8,128)(2,1)S(1)}, u32[]{:S(2)}, u32[]{:S(2)}) collective-permute-start(bf16[2,144,256]{2,1,0:T(8,128)(2,1)S(1)} %get-tuple-element.27), channel_id=1, source_target_pairs={{0,1},{1,2},{2,3},{3,4},{4,5},{5,6},{6,7},{7,8},{8,9},{9,10},{10,1... | collective-permute-start | bytes 442376 | tf_op jit(solution)/shard_map/ppermute | solution.py:371
  11.6 0.0 collective-permute-done.here_re
  11.6 0.1 collective-permute-start.6
  11.6 2.9 %collective-permute-done.2 = bf16[1,1,256,512]{3,2,1,0:T(8,128)(2,1)S(1)} collective-permute-done((bf16[1,1,256,512]{3,2,1,0:T(8,128)(2,1)S(1)}, bf16[1,1,256,512]{3,2,1,0:T(8,128)(2,1)S(1)}, u32[]{:S(2)}, u32[]{:S(2)}) %collective-permute-start.2) | collective-permute-done | bytes 262176 | tf_op jit(solution)/shard_map/ppermute | solution.py:371
  14.5 4.3 %collective-permute-start.1 = (bf16[1,1,256,512]{3,2,1,0:T(8,128)(2,1)S(1)}, bf16[1,1,256,512]{3,2,1,0:T(8,128)(2,1)S(1)}, u32[]{:S(2)}, u32[]{:S(2)}) collective-permute-start(bf16[1,1,256,512]{3,2,1,0:T(8,128)(2,1)S(1)} %collective-permute-done.here_re), channel_id=1, source_target_pairs={{0,2},{2,4},{3,1},{4,6},{5,3},{6,8},{7,5},{8,10},{9,7},{10,12},{11... | collective-permute-start | bytes 786440 | tf_op jit(solution)/shard_map/ppermute | solution.py:371
  18.9 0.0 collective-permute-done.5.own_there
  18.9 0.1 collective-permute-start.3
  19.0 0.0 copy-done.2
  19.0 0.0 copy-done.5
  19.0 3.2 %own.1 = (bf16[512,512]{1,0:T(8,128)(2,1)S(1)}, bf16[512,512]{1,0:T(8,128)(2,1)S(1)}, bf16[512,512]{1,0:T(8,128)(2,1)S(1)}, bf16[512,512]{1,0:T(8,128)(2,1)S(1)}...) custom-call(s32[2]{0:T(128)S(1)} %copy-done.3, ...), custom_call_target="tpu_custom_call" | custom-call | flops 1000 | bytes 1000 | tf_op jit(solution)/shard_map/own/pallas_call | solution.py:404
  22.2 0.0 collective-permute-done.4.here_im
  22.2 0.0 collective-permute-done.9.received.refs_3_.int_here
  22.2 0.1 collective-permute-start.10
  22.3 0.6 %collective-permute-start.8 = (bf16[1,1,128,512]{3,2,1,0:T(8,128)(2,1)S(1)}, bf16[1,1,128,512]{3,2,1,0:T(8,128)(2,1)S(1)}, u32[]{:S(2)}, u32[]{:S(2)}) collective-permute-start(bf16[1,1,128,512]{3,2,1,0:T(8,128)(2,1)S(1)} %get-tuple-element.43), channel_id=1, source_target_pairs={{0,16},{16,0},{1,17},{17,1},{2,18},{18,2},{3,19},{19,3},{4,20},{20... | collective-permute-start | bytes 393224 | tf_op jit(solution)/shard_map/ppermute | solution.py:367
  22.9 0.0 collective-permute-done.6.there_re
  22.9 0.1 collective-permute-start.7
  23.0 1.3 %past.1 = (s32[2,8,256]{2,1,0:T(8,128)S(1)}, bf16[2,2,256,256]{3,2,1,0:T(8,128)(2,1)S(1)}, bf16[2,2,2,256,256]{4,3,2,1,0:T(8,128)(2,1)S(1)}) custom-call(bf16[2,144,256]{2,1,0:T(8,128)(2,1)S(1)} %collective-permute-done.9.received.refs_3_.int_here, bf16[2,256,256]{2,1,0:T(8,128)(2,1)S(1)} %copy-done.2, bf16[2,1,256,512]{3,2,1,0:T(8,128)(2,1)S(1)} %copy-done, ...), custom_call_target="tpu_custom_call" | custom-call | flops 1000 | bytes 1000 | tf_op jit(solution)/shard_map/past/pallas_call | solution.py:410
  24.3 0.1 collective-permute-done.1.here_re
  24.4 0.4 %collective-permute-start.11 = (bf16[1,1,256,512]{3,2,1,0:T(8,128)(2,1)S(1)}, bf16[1,1,256,512]{3,2,1,0:T(8,128)(2,1)S(1)}, u32[]{:S(2)}, u32[]{:S(2)}) collective-permute-start(bf16[1,1,256,512]{3,2,1,0:T(8,128)(2,1)S(1)} %collective-permute-done.1.here_re), channel_id=1, source_target_pairs={{0,16},{16,0},{1,17},{17,1},{2,18},{18,2},{3,19},{19,3},{4,20},{20... | collective-permute-start | bytes 786440 | tf_op jit(solution)/shard_map/ppermute | solution.py:367
  24.8 0.0 collective-permute-done.8.refs_1_
  24.8 0.0 collective-permute-done.7.refs_0_
  24.8 0.0 collective-permute-done.10.refs_4_.int_there
  24.8 3.5 %facing.1.base = f32[2,1,256,512]{3,2,1,0:T(8,128)S(1)} custom-call(bf16[1,1,256,512]{3,2,1,0:T(8,128)(2,1)S(1)} %collective-permute-done.here_re, bf16[1,1,256,512]{3,2,1,0:T(8,128)(2,1)S(1)} %collective-permute-done.4.here_im, bf16[1,1,256,512]{3,2,1,0:T(8,128)(2,1)S(1)} %collective-permute-done.6.there_re, ...), custom_call_target="tpu_custom_call" | custom-call | flops 1000 | bytes 1000 | tf_op jit(solution)/shard_map/facing/pallas_call | solution.py:428
  28.3 0.0 collective-permute-done.3.here_im
  28.3 0.1 collective-permute-start.12
  28.4 1.2 %entering.1.entered = bf16[2,2,256,256]{3,2,1,0:T(8,128)(2,1)S(1)} custom-call(bf16[1,1,256,512]{3,2,1,0:T(8,128)(2,1)S(1)} %collective-permute-done.1.here_re, bf16[1,1,256,512]{3,2,1,0:T(8,128)(2,1)S(1)} %collective-permute-done.3.here_im, bf16[512,512]{1,0:T(8,128)(2,1)S(1)} %get-tuple-element.29.refs_5_.nl, ...), custom_call_target="tpu_custom_call" | custom-call | flops 1000 | bytes 1000 | tf_op jit(solution)/shard_map/entering/pallas_call | solution.py:435
  29.6 0.0 collective-permute-done.11.there_re
  29.6 0.3 collective-permute-done.12.there_im
  29.9 3.5 %opposite.1 = f32[2,1,256,512]{3,2,1,0:T(8,128)} custom-call(bf16[1,1,256,512]{3,2,1,0:T(8,128)(2,1)S(1)} %collective-permute-done.1.here_re, bf16[1,1,256,512]{3,2,1,0:T(8,128)(2,1)S(1)} %collective-permute-done.3.here_im, bf16[1,1,256,512]{3,2,1,0:T(8,128)(2,1)S(1)} %collective-permute-done.11.there_re, ...), custom_call_target="tpu_custom_call" | custom-call | flops 1000 | bytes 1000 | tf_op jit(solution)/shard_map/opposite/pallas_call | solution.py:438
  (1 shorter events, 0.0 us)
Async XLA Ops:
  0.0 6.2 %copy-start = (bf16[2,1,256,512]{3,2,1,0:T(8,128)(2,1)S(1)}, bf16[2,1,256,512]{3,2,1,0:T(8,128)(2,1)}, u32[]{:S(2)}) copy-start(bf16[2,1,256,512]{3,2,1,0:T(8,128)(2,1)} %own_here.3) | copy-start | bytes 1572868
  0.0 6.2 %copy-start.1 = (bf16[2,256,256]{2,1,0:T(8,128)(2,1)S(1)}, bf16[2,256,256]{2,1,0:T(8,128)(2,1)}, u32[]{:S(2)}) copy-start(bf16[2,256,256]{2,1,0:T(8,128)(2,1)} %own_int.1) | copy-start | bytes 786436
  0.0 18.9 %collective-permute-start.5 = (bf16[2,1,256,512]{3,2,1,0:T(8,128)(2,1)}, bf16[2,1,256,512]{3,2,1,0:T(8,128)(2,1)S(1)}, u32[]{:S(2)}, u32[]{:S(2)}) collective-permute-start(bf16[2,1,256,512]{3,2,1,0:T(8,128)(2,1)} %own_here.3), channel_id=1, source_target_pairs={{0,16},{16,0},{1,17},{17,1},{2,18},{18,2},{3,19},{19,3},{4,20},{20... | collective-permute-start | bytes 1572872 | tf_op jit(solution)/shard_map/ppermute | solution.py:367
  1.5 10.0 %collective-permute-start = (bf16[1,1,256,512]{3,2,1,0:T(8,128)(2,1)S(1)}, bf16[1,1,256,512]{3,2,1,0:T(8,128)(2,1)S(1)}, u32[]{:S(2)}, u32[]{:S(2)}) collective-permute-start(bf16[1,1,256,512]{3,2,1,0:T(8,128)(2,1)S(1)} %get-tuple-element.42), channel_id=1, source_target_pairs={{0,1},{1,0},{2,3},{3,2},{4,5},{5,4},{6,7},{7,6},{8,9},{9,8},{10,11... | collective-permute-start | bytes 786440 | tf_op jit(solution)/shard_map/ppermute | solution.py:371
  4.2 2.1 %copy-start.3 = (s32[2]{0:T(128)S(1)}, s32[2]{0:T(128)}, u32[]{:S(2)}) copy-start(s32[2]{0:T(128)} %row_ref.3) | copy-start | bytes 28
  4.2 2.1 %copy-start.4 = (s32[2]{0:T(128)S(1)}, s32[2]{0:T(128)}, u32[]{:S(2)}) copy-start(s32[2]{0:T(128)} %col_ref.3) | copy-start | bytes 28
  4.2 10.4 %collective-permute-start.2 = (bf16[1,1,256,512]{3,2,1,0:T(8,128)(2,1)S(1)}, bf16[1,1,256,512]{3,2,1,0:T(8,128)(2,1)S(1)}, u32[]{:S(2)}, u32[]{:S(2)}) collective-permute-start(bf16[1,1,256,512]{3,2,1,0:T(8,128)(2,1)S(1)} %get-tuple-element.41), channel_id=1, source_target_pairs={{2,0},{4,2},{1,3},{6,4},{3,5},{8,6},{5,7},{10,8},{7,9},{12,10},{9,... | collective-permute-start | bytes 786440 | tf_op jit(solution)/shard_map/ppermute | solution.py:371
  6.3 12.7 %copy-start.2 = (bf16[2,256,256]{2,1,0:T(8,128)(2,1)S(1)}, bf16[2,256,256]{2,1,0:T(8,128)(2,1)}, u32[]{:S(2)}) copy-start(bf16[2,256,256]{2,1,0:T(8,128)(2,1)} %probe_ref.3) | copy-start | bytes 786436
  6.9 15.4 %collective-permute-start.4 = (bf16[1,1,256,512]{3,2,1,0:T(8,128)(2,1)S(1)}, bf16[1,1,256,512]{3,2,1,0:T(8,128)(2,1)S(1)}, u32[]{:S(2)}, u32[]{:S(2)}) collective-permute-start(bf16[1,1,256,512]{3,2,1,0:T(8,128)(2,1)S(1)} %get-tuple-element.23), channel_id=1, source_target_pairs={{0,1},{1,0},{2,3},{3,2},{4,5},{5,4},{6,7},{7,6},{8,9},{9,8},{10,11... | collective-permute-start | bytes 786440 | tf_op jit(solution)/shard_map/ppermute | solution.py:371
  9.6 9.4 %copy-start.5 = (f32[256]{0:T(256)S(1)}, f32[256]{0:T(256)}, u32[]{:S(2)}) copy-start(f32[256]{0:T(256)} %param.9) | copy-start | bytes 3076
  9.6 12.6 %collective-permute-start.9 = (bf16[2,144,256]{2,1,0:T(8,128)(2,1)S(1)}, bf16[2,144,256]{2,1,0:T(8,128)(2,1)S(1)}, u32[]{:S(2)}, u32[]{:S(2)}) collective-permute-start(bf16[2,144,256]{2,1,0:T(8,128)(2,1)S(1)} %get-tuple-element.27), channel_id=1, source_target_pairs={{0,1},{1,2},{2,3},{3,4},{4,5},{5,6},{6,7},{7,8},{8,9},{9,10},{10,1... | collective-permute-start | bytes 442376 | tf_op jit(solution)/shard_map/ppermute | solution.py:371
  11.6 11.3 %collective-permute-start.6 = (bf16[1,1,256,512]{3,2,1,0:T(8,128)(2,1)S(1)}, bf16[1,1,256,512]{3,2,1,0:T(8,128)(2,1)S(1)}, u32[]{:S(2)}, u32[]{:S(2)}) collective-permute-start(bf16[1,1,256,512]{3,2,1,0:T(8,128)(2,1)S(1)} %collective-permute-done.here_re), channel_id=1, source_target_pairs={{0,16},{16,0},{1,17},{17,1},{2,18},{18,2},{3,19},{19,3},{4,20},{20... | collective-permute-start | bytes 786440 | tf_op jit(solution)/shard_map/ppermute | solution.py:367
  14.5 9.9 %collective-permute-start.1 = (bf16[1,1,256,512]{3,2,1,0:T(8,128)(2,1)S(1)}, bf16[1,1,256,512]{3,2,1,0:T(8,128)(2,1)S(1)}, u32[]{:S(2)}, u32[]{:S(2)}) collective-permute-start(bf16[1,1,256,512]{3,2,1,0:T(8,128)(2,1)S(1)} %collective-permute-done.here_re), channel_id=1, source_target_pairs={{0,2},{2,4},{3,1},{4,6},{5,3},{6,8},{7,5},{8,10},{9,7},{10,12},{11... | collective-permute-start | bytes 786440 | tf_op jit(solution)/shard_map/ppermute | solution.py:371
  18.9 9.4 %collective-permute-start.3 = (bf16[1,1,256,512]{3,2,1,0:T(8,128)(2,1)S(1)}, bf16[1,1,256,512]{3,2,1,0:T(8,128)(2,1)S(1)}, u32[]{:S(2)}, u32[]{:S(2)}) collective-permute-start(bf16[1,1,256,512]{3,2,1,0:T(8,128)(2,1)S(1)} %collective-permute-done.2), channel_id=1, source_target_pairs={{0,1},{1,0},{2,3},{3,2},{4,5},{5,4},{6,7},{7,6},{8,9},{9,8},{10,11... | collective-permute-start | bytes 786440 | tf_op jit(solution)/shard_map/ppermute | solution.py:371
  22.2 2.6 %collective-permute-start.10 = (bf16[2,144,256]{2,1,0:T(8,128)(2,1)S(1)}, bf16[2,144,256]{2,1,0:T(8,128)(2,1)S(1)}, u32[]{:S(2)}, u32[]{:S(2)}) collective-permute-start(bf16[2,144,256]{2,1,0:T(8,128)(2,1)S(1)} %collective-permute-done.9.received.refs_3_.int_here), channel_id=1, source_target_pairs={{0,16},{16,0},{1,17},{17,1},{2,18},{18,2},{3,19},{19,3},{4,20},{20... | collective-permute-start | bytes 442376 | tf_op jit(solution)/shard_map/ppermute | solution.py:367
  22.3 2.4 %collective-permute-start.8 = (bf16[1,1,128,512]{3,2,1,0:T(8,128)(2,1)S(1)}, bf16[1,1,128,512]{3,2,1,0:T(8,128)(2,1)S(1)}, u32[]{:S(2)}, u32[]{:S(2)}) collective-permute-start(bf16[1,1,128,512]{3,2,1,0:T(8,128)(2,1)S(1)} %get-tuple-element.43), channel_id=1, source_target_pairs={{0,16},{16,0},{1,17},{17,1},{2,18},{18,2},{3,19},{19,3},{4,20},{20... | collective-permute-start | bytes 393224 | tf_op jit(solution)/shard_map/ppermute | solution.py:367
  22.9 1.9 %collective-permute-start.7 = (bf16[1,1,128,512]{3,2,1,0:T(8,128)(2,1)S(1)}, bf16[1,1,128,512]{3,2,1,0:T(8,128)(2,1)S(1)}, u32[]{:S(2)}, u32[]{:S(2)}) collective-permute-start(bf16[1,1,128,512]{3,2,1,0:T(8,128)(2,1)S(1)} %get-tuple-element.44), channel_id=1, source_target_pairs={{0,16},{16,0},{1,17},{17,1},{2,18},{18,2},{3,19},{19,3},{4,20},{20... | collective-permute-start | bytes 393224 | tf_op jit(solution)/shard_map/ppermute | solution.py:367
  24.4 5.1 %collective-permute-start.11 = (bf16[1,1,256,512]{3,2,1,0:T(8,128)(2,1)S(1)}, bf16[1,1,256,512]{3,2,1,0:T(8,128)(2,1)S(1)}, u32[]{:S(2)}, u32[]{:S(2)}) collective-permute-start(bf16[1,1,256,512]{3,2,1,0:T(8,128)(2,1)S(1)} %collective-permute-done.1.here_re), channel_id=1, source_target_pairs={{0,16},{16,0},{1,17},{17,1},{2,18},{18,2},{3,19},{19,3},{4,20},{20... | collective-permute-start | bytes 786440 | tf_op jit(solution)/shard_map/ppermute | solution.py:367
  28.3 1.6 %collective-permute-start.12 = (bf16[1,1,256,512]{3,2,1,0:T(8,128)(2,1)S(1)}, bf16[1,1,256,512]{3,2,1,0:T(8,128)(2,1)S(1)}, u32[]{:S(2)}, u32[]{:S(2)}) collective-permute-start(bf16[1,1,256,512]{3,2,1,0:T(8,128)(2,1)S(1)} %collective-permute-done.3.here_im), channel_id=1, source_target_pairs={{0,16},{16,0},{1,17},{17,1},{2,18},{18,2},{3,19},{19,3},{4,20},{20... | collective-permute-start | bytes 786440 | tf_op jit(solution)/shard_map/ppermute | solution.py:367

commit v5 on v4

--- a/solution.py
+++ b/solution.py
@@ -195,13 +195,24 @@
         here = slice(w * n + at.start, w * n + at.stop)
         return self.outer[here, :n], self.outer[here, n:]
 
-    def propagate(self, left, right):
+    def right_rows(self, at):
+        n = self.n
+        here = [slice(w * n + at.start, w * n + at.stop) for w in range(self.slots)]
+        product = mm(
+            jnp.concatenate([self.inner[rows, :] for rows in here], axis=0), self.pending[...]
+        )
+        size = at.stop - at.start
+        for w, rows in enumerate(here):
+            self.outer[rows, :] = product[w * size : (w + 1) * size]
+
+    def propagate(self, left, right, defer=False):
         n = self.n
         for w in range(self.slots):
             product = mm(left[...], self.field[:, w * n : (w + 1) * n]).astype(BF)
             self.inner[w * n : (w + 1) * n, :n] = product[:n]
             self.inner[w * n : (w + 1) * n, n:] = product[n:]
-        for w in range(self.slots):
+        self.pending = right if defer else None
+        for w in range(0 if defer else self.slots):
             here = slice(w * n, (w + 1) * n)
             self.outer[here, :] = mm(self.inner[here, :], right[...])
 
@@ -218,7 +229,7 @@
                 psi[w, 0, at, :] = re.astype(BF)
                 psi[w, 1, at, :] = im.astype(BF)
 
-    def leave(self, other, psi, own_int, int_here, int_there):
+    def leave(self, other, psi, own_int, int_here, int_there, defer=False):
         for w in range(self.slots):
             for at in self.rows():
                 t_re, t_im = self.window(w, 1, other, at)
@@ -241,20 +252,22 @@
                 measured = jnp.where(self.own, own_int[w, at, :].astype(F32), received)
                 factor = weight * (re * re + im * im - measured)
                 self.put(w, at, factor * re, factor * im)
-        self.propagate(self.far[1], self.far[0])
-
-    def reach_first(self):
+        self.propagate(self.far[1], self.far[0], defer)
+
+    def reach_first(self, defer=False):
         for w in range(self.slots):
             for at in self.rows():
                 t_re, t_im = self.pair(self.last, w, at)
                 y_re, y_im = (part.astype(BF).astype(F32) for part in self.got(w, at))
                 self.put(w, at, t_re * y_re + t_im * y_im, t_re * y_im - t_im * y_re)
-        self.propagate(self.near[1], self.near[0])
+        self.propagate(self.near[1], self.near[0], defer)
 
     def gradient(self, entering, base, out, final=None, sems=None):
         n = self.n
         copies = []
         for at in self.rows():
+            if self.pending is not None and at.start % SENT == 0:
+                self.right_rows(slice(at.start, at.start + SENT))
             sums = [0.0] * 4
             if base is not None:
                 sums = [base[part, 0, at, c : c + n] for part in range(2) for c in (0, n)]
@@ -332,13 +345,13 @@
     @pl.when(top)
     def _():
         waves.leave(there, entered, *ints)
-        waves.reach_first()
+        waves.reach_first(defer=True)
         waves.gradient(waves.probe, base, total, out, sems)
 
     @pl.when(jnp.logical_not(top))
     def _():
         waves.enter(there, psi)
-        waves.leave(here, psi, *ints)
+        waves.leave(here, psi, *ints, defer=True)
         waves.gradient(lambda w, at: waves.pair(psi, w, at), base, total, out, sems)
 
 

time: 33.7 us -> 33.6 us (level)
  no operation moved by 1% of the time
where the time goes in v5:
time: 33.6 us; the launch traced here: 33.4 us
  starting transfers between devices  14.8 us (44%)
  Pallas kernels  13.1 us (39%)
  waiting for transfers between devices  3.37 us (10%)
  local copies, waits for them, and re-layouts  1.11 us (3%)
  between operations  1.03 us (3%)
    ppermute x6, starting transfers between devices, send(): return lax.ppermute(value, 'tile', inside)  13.1 us
    pallas_call x1, Pallas kernels, on_device(): kernel_call(facing_kernel, 'facing', grad_shape, [VM] * (16 + PIECES), wo...  3.46 us
    pallas_call x1, Pallas kernels, on_device(): kernel_call(opposite_kernel, 'opposite', grad_shape, [VM] * 19, work + [p...  3.32 us
    pallas_call x1, Pallas kernels, on_device(): kernel_call(own_kernel, 'own', (double,) * 4 + wave_shapes, [SM] * 3 + [V...  3.21 us
    ppermute x6, waiting for transfers between devices, send(): return lax.ppermute(value, 'tile', inside)  3.06 us
    ppermute x7, starting transfers between devices, swap(): return lax.ppermute(value, 'sec', [(0, 1), (1, 0)])  1.66 us
    pallas_call x1, Pallas kernels, on_device(): kernel_call(past_kernel, 'past', wave_shapes, [VM] * 4)  1.29 us
    pallas_call x1, Pallas kernels, on_device(): kernel_call(entering_kernel, 'entering', jax.ShapeDtypeStruct((slots, 2,...  1.21 us
  transfers between devices with their start and end apart: 13, of which 3 were waited for; matrix products, arithmetic and copies ran while one was open for 3% of the time, Pallas kernels for 29%

profile of v5, /device:TPU:0, one launch (start us, length us, event | category | flops | bytes accessed | tf_op | source)
XLA Modules:
  0.0 33.4 jit_solution(13142721825836649417)
XLA Ops:
  0.0 0.0 copy-start
  0.0 0.0 copy-start.1
  0.0 0.5 %collective-permute-start.5 = (bf16[2,1,256,512]{3,2,1,0:T(8,128)(2,1)}, bf16[2,1,256,512]{3,2,1,0:T(8,128)(2,1)S(1)}, u32[]{:S(2)}, u32[]{:S(2)}) collective-permute-start(bf16[2,1,256,512]{3,2,1,0:T(8,128)(2,1)} %own_here.3), channel_id=1, source_target_pairs={{0,16},{16,0},{1,17},{17,1},{2,18},{18,2},{3,19},{19,3},{4,20},{20... | collective-permute-start | bytes 1572872 | tf_op jit(solution)/shard_map/ppermute | solution.py:380
  0.5 1.1 %fusion = (bf16[1,1,256,512]{3,2,1,0:T(8,128)(2,1)S(1)}, bf16[1,1,256,512]{3,2,1,0:T(8,128)(2,1)S(1)}) fusion(bf16[2,1,256,512]{3,2,1,0:T(8,128)(2,1)} %own_here.3), kind=kLoop, calls=%fused_computation | loop fusion | bytes 1048576 | tf_op jit(solution)/shard_map/slice | solution.py:392
  1.5 2.6 %collective-permute-start = (bf16[1,1,256,512]{3,2,1,0:T(8,128)(2,1)S(1)}, bf16[1,1,256,512]{3,2,1,0:T(8,128)(2,1)S(1)}, u32[]{:S(2)}, u32[]{:S(2)}) collective-permute-start(bf16[1,1,256,512]{3,2,1,0:T(8,128)(2,1)S(1)} %get-tuple-element.42), channel_id=1, source_target_pairs={{0,1},{1,0},{2,3},{3,2},{4,5},{5,4},{6,7},{7,6},{8,9},{9,8},{10,11... | collective-permute-start | bytes 786440 | tf_op jit(solution)/shard_map/ppermute | solution.py:384
  4.2 0.0 copy-start.3
  4.2 0.0 copy-start.4
  4.2 1.4 %collective-permute-start.2 = (bf16[1,1,256,512]{3,2,1,0:T(8,128)(2,1)S(1)}, bf16[1,1,256,512]{3,2,1,0:T(8,128)(2,1)S(1)}, u32[]{:S(2)}, u32[]{:S(2)}) collective-permute-start(bf16[1,1,256,512]{3,2,1,0:T(8,128)(2,1)S(1)} %get-tuple-element.41), channel_id=1, source_target_pairs={{2,0},{4,2},{1,3},{6,4},{3,5},{8,6},{5,7},{10,8},{7,9},{12,10},{9,... | collective-permute-start | bytes 786440 | tf_op jit(solution)/shard_map/ppermute | solution.py:384
  6.2 0.0 copy-done
  6.2 0.0 copy-done.1
  6.2 0.0 copy-done.3
  6.3 0.0 copy-done.4
  6.3 0.0 copy-start.2
  6.3 0.6 %message.1 = (bf16[2,144,256]{2,1,0:T(8,128)(2,1)S(1)}, bf16[1,1,256,512]{3,2,1,0:T(8,128)(2,1)S(1)}) custom-call(s32[2]{0:T(128)S(1)} %copy-done.3, s32[2]{0:T(128)S(1)} %copy-done.4, s32[1]{0:T(128)S(6)} %copy.8.count_ref, bf16[2,256,256]{2,1,0:T(8,128)(2,1)S(1)} %copy-done.1, bf16[2,1,256,512]{3,2,1,0:T(8,128)(2,1)S(1)} %copy-done), custom_call_target="tpu_custom_call" | custom-call | flops 1000 | bytes 1000 | tf_op jit(solution)/shard_map/message/pallas_call | solution.py:397
  6.9 2.7 %collective-permute-start.4 = (bf16[1,1,256,512]{3,2,1,0:T(8,128)(2,1)S(1)}, bf16[1,1,256,512]{3,2,1,0:T(8,128)(2,1)S(1)}, u32[]{:S(2)}, u32[]{:S(2)}) collective-permute-start(bf16[1,1,256,512]{3,2,1,0:T(8,128)(2,1)S(1)} %get-tuple-element.23), channel_id=1, source_target_pairs={{0,1},{1,0},{2,3},{3,2},{4,5},{5,4},{6,7},{7,6},{8,9},{9,8},{10,11... | collective-permute-start | bytes 786440 | tf_op jit(solution)/shard_map/ppermute | solution.py:384
  9.6 0.0 copy-start.5
  9.6 1.9 %collective-permute-start.9 = (bf16[2,144,256]{2,1,0:T(8,128)(2,1)S(1)}, bf16[2,144,256]{2,1,0:T(8,128)(2,1)S(1)}, u32[]{:S(2)}, u32[]{:S(2)}) collective-permute-start(bf16[2,144,256]{2,1,0:T(8,128)(2,1)S(1)} %get-tuple-element.27), channel_id=1, source_target_pairs={{0,1},{1,2},{2,3},{3,4},{4,5},{5,6},{6,7},{7,8},{8,9},{9,10},{10,1... | collective-permute-start | bytes 442376 | tf_op jit(solution)/shard_map/ppermute | solution.py:384
  11.6 0.0 collective-permute-done.here_re
  11.6 0.1 collective-permute-start.6
  11.6 2.9 %collective-permute-done.2 = bf16[1,1,256,512]{3,2,1,0:T(8,128)(2,1)S(1)} collective-permute-done((bf16[1,1,256,512]{3,2,1,0:T(8,128)(2,1)S(1)}, bf16[1,1,256,512]{3,2,1,0:T(8,128)(2,1)S(1)}, u32[]{:S(2)}, u32[]{:S(2)}) %collective-permute-start.2) | collective-permute-done | bytes 262176 | tf_op jit(solution)/shard_map/ppermute | solution.py:384
  14.5 4.3 %collective-permute-start.1 = (bf16[1,1,256,512]{3,2,1,0:T(8,128)(2,1)S(1)}, bf16[1,1,256,512]{3,2,1,0:T(8,128)(2,1)S(1)}, u32[]{:S(2)}, u32[]{:S(2)}) collective-permute-start(bf16[1,1,256,512]{3,2,1,0:T(8,128)(2,1)S(1)} %collective-permute-done.here_re), channel_id=1, source_target_pairs={{0,2},{2,4},{3,1},{4,6},{5,3},{6,8},{7,5},{8,10},{9,7},{10,12},{11... | collective-permute-start | bytes 786440 | tf_op jit(solution)/shard_map/ppermute | solution.py:384
  18.9 0.0 collective-permute-done.5.own_there
  18.9 0.1 collective-permute-start.3
  19.0 0.0 copy-done.2
  19.0 0.0 copy-done.5
  19.0 3.2 %own.1 = (bf16[512,512]{1,0:T(8,128)(2,1)S(1)}, bf16[512,512]{1,0:T(8,128)(2,1)S(1)}, bf16[512,512]{1,0:T(8,128)(2,1)S(1)}, bf16[512,512]{1,0:T(8,128)(2,1)S(1)}...) custom-call(s32[2]{0:T(128)S(1)} %copy-done.3, ...), custom_call_target="tpu_custom_call" | custom-call | flops 1000 | bytes 1000 | tf_op jit(solution)/shard_map/own/pallas_call | solution.py:417
  22.2 0.0 collective-permute-done.4.here_im
  22.2 0.0 collective-permute-done.9.received.refs_3_.int_here
  22.2 0.1 collective-permute-start.10
  22.3 0.6 %collective-permute-start.8 = (bf16[1,1,128,512]{3,2,1,0:T(8,128)(2,1)S(1)}, bf16[1,1,128,512]{3,2,1,0:T(8,128)(2,1)S(1)}, u32[]{:S(2)}, u32[]{:S(2)}) collective-permute-start(bf16[1,1,128,512]{3,2,1,0:T(8,128)(2,1)S(1)} %get-tuple-element.43), channel_id=1, source_target_pairs={{0,16},{16,0},{1,17},{17,1},{2,18},{18,2},{3,19},{19,3},{4,20},{20... | collective-permute-start | bytes 393224 | tf_op jit(solution)/shard_map/ppermute | solution.py:380
  22.9 0.0 collective-permute-done.6.there_re
  22.9 0.1 collective-permute-start.7
  23.0 1.3 %past.1 = (s32[2,8,256]{2,1,0:T(8,128)S(1)}, bf16[2,2,256,256]{3,2,1,0:T(8,128)(2,1)S(1)}, bf16[2,2,2,256,256]{4,3,2,1,0:T(8,128)(2,1)S(1)}) custom-call(bf16[2,144,256]{2,1,0:T(8,128)(2,1)S(1)} %collective-permute-done.9.received.refs_3_.int_here, bf16[2,256,256]{2,1,0:T(8,128)(2,1)S(1)} %copy-done.2, bf16[2,1,256,512]{3,2,1,0:T(8,128)(2,1)S(1)} %copy-done, ...), custom_call_target="tpu_custom_call" | custom-call | flops 1000 | bytes 1000 | tf_op jit(solution)/shard_map/past/pallas_call | solution.py:423
  24.3 0.1 collective-permute-done.1.here_re
  24.4 0.4 %collective-permute-start.11 = (bf16[1,1,256,512]{3,2,1,0:T(8,128)(2,1)S(1)}, bf16[1,1,256,512]{3,2,1,0:T(8,128)(2,1)S(1)}, u32[]{:S(2)}, u32[]{:S(2)}) collective-permute-start(bf16[1,1,256,512]{3,2,1,0:T(8,128)(2,1)S(1)} %collective-permute-done.1.here_re), channel_id=1, source_target_pairs={{0,16},{16,0},{1,17},{17,1},{2,18},{18,2},{3,19},{19,3},{4,20},{20... | collective-permute-start | bytes 786440 | tf_op jit(solution)/shard_map/ppermute | solution.py:380
  24.8 0.0 collective-permute-done.8.refs_1_
  24.8 0.0 collective-permute-done.7.refs_0_
  24.8 0.0 collective-permute-done.10.refs_4_.int_there
  24.8 3.5 %facing.1.base = f32[2,1,256,512]{3,2,1,0:T(8,128)S(1)} custom-call(bf16[1,1,256,512]{3,2,1,0:T(8,128)(2,1)S(1)} %collective-permute-done.here_re, bf16[1,1,256,512]{3,2,1,0:T(8,128)(2,1)S(1)} %collective-permute-done.4.here_im, bf16[1,1,256,512]{3,2,1,0:T(8,128)(2,1)S(1)} %collective-permute-done.6.there_re, ...), custom_call_target="tpu_custom_call" | custom-call | flops 1000 | bytes 1000 | tf_op jit(solution)/shard_map/facing/pallas_call | solution.py:441
  28.3 0.0 collective-permute-done.3.here_im
  28.3 0.1 collective-permute-start.12
  28.4 1.2 %entering.1.entered = bf16[2,2,256,256]{3,2,1,0:T(8,128)(2,1)S(1)} custom-call(bf16[1,1,256,512]{3,2,1,0:T(8,128)(2,1)S(1)} %collective-permute-done.1.here_re, bf16[1,1,256,512]{3,2,1,0:T(8,128)(2,1)S(1)} %collective-permute-done.3.here_im, bf16[512,512]{1,0:T(8,128)(2,1)S(1)} %get-tuple-element.29.refs_5_.nl, ...), custom_call_target="tpu_custom_call" | custom-call | flops 1000 | bytes 1000 | tf_op jit(solution)/shard_map/entering/pallas_call | solution.py:448
  29.6 0.0 collective-permute-done.11.there_re
  29.6 0.3 collective-permute-done.12.there_im
  29.9 3.3 %opposite.1 = f32[2,1,256,512]{3,2,1,0:T(8,128)} custom-call(bf16[1,1,256,512]{3,2,1,0:T(8,128)(2,1)S(1)} %collective-permute-done.1.here_re, bf16[1,1,256,512]{3,2,1,0:T(8,128)(2,1)S(1)} %collective-permute-done.3.here_im, bf16[1,1,256,512]{3,2,1,0:T(8,128)(2,1)S(1)} %collective-permute-done.11.there_re, ...), custom_call_target="tpu_custom_call" | custom-call | flops 1000 | bytes 1000 | tf_op jit(solution)/shard_map/opposite/pallas_call | solution.py:451
  (1 shorter events, 0.0 us)
Async XLA Ops:
  0.0 6.2 %copy-start = (bf16[2,1,256,512]{3,2,1,0:T(8,128)(2,1)S(1)}, bf16[2,1,256,512]{3,2,1,0:T(8,128)(2,1)}, u32[]{:S(2)}) copy-start(bf16[2,1,256,512]{3,2,1,0:T(8,128)(2,1)} %own_here.3) | copy-start | bytes 1572868
  0.0 6.2 %copy-start.1 = (bf16[2,256,256]{2,1,0:T(8,128)(2,1)S(1)}, bf16[2,256,256]{2,1,0:T(8,128)(2,1)}, u32[]{:S(2)}) copy-start(bf16[2,256,256]{2,1,0:T(8,128)(2,1)} %own_int.1) | copy-start | bytes 786436
  0.0 18.9 %collective-permute-start.5 = (bf16[2,1,256,512]{3,2,1,0:T(8,128)(2,1)}, bf16[2,1,256,512]{3,2,1,0:T(8,128)(2,1)S(1)}, u32[]{:S(2)}, u32[]{:S(2)}) collective-permute-start(bf16[2,1,256,512]{3,2,1,0:T(8,128)(2,1)} %own_here.3), channel_id=1, source_target_pairs={{0,16},{16,0},{1,17},{17,1},{2,18},{18,2},{3,19},{19,3},{4,20},{20... | collective-permute-start | bytes 1572872 | tf_op jit(solution)/shard_map/ppermute | solution.py:380
  1.5 10.0 %collective-permute-start = (bf16[1,1,256,512]{3,2,1,0:T(8,128)(2,1)S(1)}, bf16[1,1,256,512]{3,2,1,0:T(8,128)(2,1)S(1)}, u32[]{:S(2)}, u32[]{:S(2)}) collective-permute-start(bf16[1,1,256,512]{3,2,1,0:T(8,128)(2,1)S(1)} %get-tuple-element.42), channel_id=1, source_target_pairs={{0,1},{1,0},{2,3},{3,2},{4,5},{5,4},{6,7},{7,6},{8,9},{9,8},{10,11... | collective-permute-start | bytes 786440 | tf_op jit(solution)/shard_map/ppermute | solution.py:384
  4.2 2.1 %copy-start.3 = (s32[2]{0:T(128)S(1)}, s32[2]{0:T(128)}, u32[]{:S(2)}) copy-start(s32[2]{0:T(128)} %row_ref.3) | copy-start | bytes 28
  4.2 2.1 %copy-start.4 = (s32[2]{0:T(128)S(1)}, s32[2]{0:T(128)}, u32[]{:S(2)}) copy-start(s32[2]{0:T(128)} %col_ref.3) | copy-start | bytes 28
  4.2 10.4 %collective-permute-start.2 = (bf16[1,1,256,512]{3,2,1,0:T(8,128)(2,1)S(1)}, bf16[1,1,256,512]{3,2,1,0:T(8,128)(2,1)S(1)}, u32[]{:S(2)}, u32[]{:S(2)}) collective-permute-start(bf16[1,1,256,512]{3,2,1,0:T(8,128)(2,1)S(1)} %get-tuple-element.41), channel_id=1, source_target_pairs={{2,0},{4,2},{1,3},{6,4},{3,5},{8,6},{5,7},{10,8},{7,9},{12,10},{9,... | collective-permute-start | bytes 786440 | tf_op jit(solution)/shard_map/ppermute | solution.py:384
  6.3 12.7 %copy-start.2 = (bf16[2,256,256]{2,1,0:T(8,128)(2,1)S(1)}, bf16[2,256,256]{2,1,0:T(8,128)(2,1)}, u32[]{:S(2)}) copy-start(bf16[2,256,256]{2,1,0:T(8,128)(2,1)} %probe_ref.3) | copy-start | bytes 786436
  6.9 15.4 %collective-permute-start.4 = (bf16[1,1,256,512]{3,2,1,0:T(8,128)(2,1)S(1)}, bf16[1,1,256,512]{3,2,1,0:T(8,128)(2,1)S(1)}, u32[]{:S(2)}, u32[]{:S(2)}) collective-permute-start(bf16[1,1,256,512]{3,2,1,0:T(8,128)(2,1)S(1)} %get-tuple-element.23), channel_id=1, source_target_pairs={{0,1},{1,0},{2,3},{3,2},{4,5},{5,4},{6,7},{7,6},{8,9},{9,8},{10,11... | collective-permute-start | bytes 786440 | tf_op jit(solution)/shard_map/ppermute | solution.py:384
  9.6 9.4 %copy-start.5 = (f32[256]{0:T(256)S(1)}, f32[256]{0:T(256)}, u32[]{:S(2)}) copy-start(f32[256]{0:T(256)} %param.9) | copy-start | bytes 3076
  9.6 12.6 %collective-permute-start.9 = (bf16[2,144,256]{2,1,0:T(8,128)(2,1)S(1)}, bf16[2,144,256]{2,1,0:T(8,128)(2,1)S(1)}, u32[]{:S(2)}, u32[]{:S(2)}) collective-permute-start(bf16[2,144,256]{2,1,0:T(8,128)(2,1)S(1)} %get-tuple-element.27), channel_id=1, source_target_pairs={{0,1},{1,2},{2,3},{3,4},{4,5},{5,6},{6,7},{7,8},{8,9},{9,10},{10,1... | collective-permute-start | bytes 442376 | tf_op jit(solution)/shard_map/ppermute | solution.py:384
  11.6 11.3 %collective-permute-start.6 = (bf16[1,1,256,512]{3,2,1,0:T(8,128)(2,1)S(1)}, bf16[1,1,256,512]{3,2,1,0:T(8,128)(2,1)S(1)}, u32[]{:S(2)}, u32[]{:S(2)}) collective-permute-start(bf16[1,1,256,512]{3,2,1,0:T(8,128)(2,1)S(1)} %collective-permute-done.here_re), channel_id=1, source_target_pairs={{0,16},{16,0},{1,17},{17,1},{2,18},{18,2},{3,19},{19,3},{4,20},{20... | collective-permute-start | bytes 786440 | tf_op jit(solution)/shard_map/ppermute | solution.py:380
  14.5 9.9 %collective-permute-start.1 = (bf16[1,1,256,512]{3,2,1,0:T(8,128)(2,1)S(1)}, bf16[1,1,256,512]{3,2,1,0:T(8,128)(2,1)S(1)}, u32[]{:S(2)}, u32[]{:S(2)}) collective-permute-start(bf16[1,1,256,512]{3,2,1,0:T(8,128)(2,1)S(1)} %collective-permute-done.here_re), channel_id=1, source_target_pairs={{0,2},{2,4},{3,1},{4,6},{5,3},{6,8},{7,5},{8,10},{9,7},{10,12},{11... | collective-permute-start | bytes 786440 | tf_op jit(solution)/shard_map/ppermute | solution.py:384
  18.9 9.4 %collective-permute-start.3 = (bf16[1,1,256,512]{3,2,1,0:T(8,128)(2,1)S(1)}, bf16[1,1,256,512]{3,2,1,0:T(8,128)(2,1)S(1)}, u32[]{:S(2)}, u32[]{:S(2)}) collective-permute-start(bf16[1,1,256,512]{3,2,1,0:T(8,128)(2,1)S(1)} %collective-permute-done.2), channel_id=1, source_target_pairs={{0,1},{1,0},{2,3},{3,2},{4,5},{5,4},{6,7},{7,6},{8,9},{9,8},{10,11... | collective-permute-start | bytes 786440 | tf_op jit(solution)/shard_map/ppermute | solution.py:384
  22.2 2.6 %collective-permute-start.10 = (bf16[2,144,256]{2,1,0:T(8,128)(2,1)S(1)}, bf16[2,144,256]{2,1,0:T(8,128)(2,1)S(1)}, u32[]{:S(2)}, u32[]{:S(2)}) collective-permute-start(bf16[2,144,256]{2,1,0:T(8,128)(2,1)S(1)} %collective-permute-done.9.received.refs_3_.int_here), channel_id=1, source_target_pairs={{0,16},{16,0},{1,17},{17,1},{2,18},{18,2},{3,19},{19,3},{4,20},{20... | collective-permute-start | bytes 442376 | tf_op jit(solution)/shard_map/ppermute | solution.py:380
  22.3 2.4 %collective-permute-start.8 = (bf16[1,1,128,512]{3,2,1,0:T(8,128)(2,1)S(1)}, bf16[1,1,128,512]{3,2,1,0:T(8,128)(2,1)S(1)}, u32[]{:S(2)}, u32[]{:S(2)}) collective-permute-start(bf16[1,1,128,512]{3,2,1,0:T(8,128)(2,1)S(1)} %get-tuple-element.43), channel_id=1, source_target_pairs={{0,16},{16,0},{1,17},{17,1},{2,18},{18,2},{3,19},{19,3},{4,20},{20... | collective-permute-start | bytes 393224 | tf_op jit(solution)/shard_map/ppermute | solution.py:380
  22.9 1.9 %collective-permute-start.7 = (bf16[1,1,128,512]{3,2,1,0:T(8,128)(2,1)S(1)}, bf16[1,1,128,512]{3,2,1,0:T(8,128)(2,1)S(1)}, u32[]{:S(2)}, u32[]{:S(2)}) collective-permute-start(bf16[1,1,128,512]{3,2,1,0:T(8,128)(2,1)S(1)} %get-tuple-element.44), channel_id=1, source_target_pairs={{0,16},{16,0},{1,17},{17,1},{2,18},{18,2},{3,19},{19,3},{4,20},{20... | collective-permute-start | bytes 393224 | tf_op jit(solution)/shard_map/ppermute | solution.py:380
  24.4 5.1 %collective-permute-start.11 = (bf16[1,1,256,512]{3,2,1,0:T(8,128)(2,1)S(1)}, bf16[1,1,256,512]{3,2,1,0:T(8,128)(2,1)S(1)}, u32[]{:S(2)}, u32[]{:S(2)}) collective-permute-start(bf16[1,1,256,512]{3,2,1,0:T(8,128)(2,1)S(1)} %collective-permute-done.1.here_re), channel_id=1, source_target_pairs={{0,16},{16,0},{1,17},{17,1},{2,18},{18,2},{3,19},{19,3},{4,20},{20... | collective-permute-start | bytes 786440 | tf_op jit(solution)/shard_map/ppermute | solution.py:380
  28.3 1.6 %collective-permute-start.12 = (bf16[1,1,256,512]{3,2,1,0:T(8,128)(2,1)S(1)}, bf16[1,1,256,512]{3,2,1,0:T(8,128)(2,1)S(1)}, u32[]{:S(2)}, u32[]{:S(2)}) collective-permute-start(bf16[1,1,256,512]{3,2,1,0:T(8,128)(2,1)S(1)} %collective-permute-done.3.here_im), channel_id=1, source_target_pairs={{0,16},{16,0},{1,17},{17,1},{2,18},{18,2},{3,19},{19,3},{4,20},{20... | collective-permute-start | bytes 786440 | tf_op jit(solution)/shard_map/ppermute | solution.py:380
